TPU v7x, 32 devices: a whole 2x2x4 slice. The times are simulated.
32 devices in a mesh: img: 4 (over y, core), txt: 8 (over z, x).
Axes of the slice: x: 2, y: 2, z: 4, core: 2. Of those that a mesh axis runs over, the one named last changes fastest.
Arguments:
- picture_feature_vectors: bfloat16 [4096, 256], P(('img', 'txt')), may hold values from -400 to 400
- wording_feature_vectors: bfloat16 [4096, 256], P('txt'), may hold values from -400 to 400
- logit_softness: float32 [1], replicated, may hold values from 0.0025 to 0.1
- attention_request_vectors: bfloat16 [64, 35, 768], P(('img', 'txt')), may hold values from -64 to 64
- attention_lookup_vectors: bfloat16 [64, 257, 768], P(('img', 'txt')), may hold values from -32 to 32
- attention_content_vectors: bfloat16 [64, 257, 768], P(('img', 'txt')), may hold values from -6 to 6
- picture_distractor_partition: int32 [64, 4], P('img'), may hold values from 0 to 7, all different within a row; in each aligned block of 2 rows (0 to 1, 2 to 3, ...) at most 2 rows name the same one
- picture_distractor_slot: int32 [64, 4], P('img'), may hold values from 0 to 1
- wording_distractor_partition: int32 [64, 4], P('img'), may hold values from 0 to 7, all different within a row; in each aligned block of 2 rows (0 to 1, 2 to 3, ...) at most 2 rows name the same one
- wording_distractor_slot: int32 [64, 4], P('img'), may hold values from 0 to 1
- picture_couple_adjoint: bfloat16 [64, 4, 35, 768], P(('img', 'txt')), may hold values from -6 to 6
- wording_couple_adjoint: bfloat16 [64, 4, 35, 768], P(('img', 'txt')), may hold values from -6 to 6
Outputs:
- image_loss: float32 [4096], P(('img', 'txt'))
- text_loss: float32 [4096], P('txt')
- img_pair_out: bfloat16 [64, 4, 35, 768], P(('img', 'txt'))
- txt_pair_out: bfloat16 [64, 4, 35, 768], P(('img', 'txt'))
- query_grad: bfloat16 [64, 35, 768], P(('img', 'txt'))
- key_grad: bfloat16 [64, 257, 768], P(('img', 'txt'))
- value_grad: bfloat16 [64, 257, 768], P(('img', 'txt'))
Inputs may be any that keep to these rules, and one draw needn't show every extreme that they name: `picture_distractor_partition`: each row names 4 different shards. Among the rows of one device (aligned blocks of 2 rows) no shard is named more than 2 times, and in some such block a shard is named exactly 2 times. `wording_distractor_partition`: each row names 4 different shards. Among the rows of one device (aligned blocks of 2 rows) no shard is named more than 2 times, and in some such block a shard is named exactly 2 times.
All inputs are finite; a program needn't handle non-finite values.
Results may differ from a plain program's by a relative error of at most 0.0059.
Values may be sent and summed in bfloat16 or wider, within the bound.
No kernel may reach another device: no remote copies, remote signals or barrier semaphores. Data moves between devices by JAX's collectives and lax.ppermute only.
A program may use at most 256 MiB of HBM per device.

v0:
```python
import math

import jax
import jax.numpy as jnp
from jax import lax
from jax.sharding import PartitionSpec as P

HEADS = 12
NEGS = 4


EPSILON = 1e-06


def combined_all(part, axis, combine):
    gathered = jax.tree.map(lambda a: lax.all_gather(a, axis), part)

    def take(source):
        return jax.tree.map(lambda a: lax.dynamic_index_in_dim(a, source, 0, False), gathered)

    return lax.fori_loop(
        1, lax.axis_size(axis), lambda source, state: combine(state, take(source)), take(0)
    )


def normalize_rows(projection):
    widened = projection.astype(jnp.float32)
    factor = lax.rsqrt(jnp.sum(widened * widened, axis=-1, keepdims=True) + EPSILON)
    return (widened * factor).astype(jnp.bfloat16)


def join_totals(first, second):
    first_max, first_sum, first_diag = first
    second_max, second_sum, second_diag = second
    highest = jnp.maximum(first_max, second_max)
    summed = first_sum * jnp.exp(first_max - highest) + second_sum * jnp.exp(second_max - highest)
    return (highest, summed, first_diag + second_diag)


def block_totals(logits, on_diag, axis_now):
    highest = jnp.max(logits, axis=axis_now)
    summed = jnp.sum(jnp.exp(logits - jnp.expand_dims(highest, axis_now)), axis=axis_now)
    return (highest, summed, jnp.sum(on_diag, axis=axis_now))


def attend_forward(query_part, key_part, value_part, factor):
    logits = (
        jnp.einsum("bqhd,bphd->bhqp", query_part, key_part, preferred_element_type=jnp.float32)
        * factor
    )
    shifted = jnp.exp(logits - jnp.max(logits, axis=-1, keepdims=True))
    weights = shifted / jnp.sum(shifted, axis=-1, keepdims=True)
    rounded = weights.astype(jnp.bfloat16)
    output = jnp.einsum("bhqp,bphd->bqhd", rounded, value_part, preferred_element_type=jnp.float32)
    return (weights, rounded, output)


def attend_backward(query_part, key_part, value_part, weights, rounded, upstream, factor):
    value_term = jnp.einsum(
        "bhqp,bqhd->bphd", rounded, upstream, preferred_element_type=jnp.float32
    )
    weight_term = jnp.einsum(
        "bqhd,bphd->bhqp", upstream, value_part, preferred_element_type=jnp.float32
    )
    inner_sum = jnp.sum(weights * weight_term, axis=-1, keepdims=True)
    logit_term = (weights * (weight_term - inner_sum) * factor).astype(jnp.bfloat16)
    query_term = jnp.einsum(
        "bhqp,bphd->bqhd", logit_term, key_part, preferred_element_type=jnp.float32
    )
    key_term = jnp.einsum(
        "bhqp,bqhd->bphd", logit_term, query_part, preferred_element_type=jnp.float32
    )
    return (query_term, key_term, value_term)


def owner_ranks(owners):
    length = owners.shape[-1]
    same_owner = owners[..., :, None] == owners[..., None, :]
    earlier = jnp.arange(length)[:, None] > jnp.arange(length)[None, :]
    return jnp.sum(jnp.where(same_owner & earlier, 1, 0), axis=-1).astype(jnp.int32)


def on_device(
    picture_feature_vectors,
    wording_feature_vectors,
    logit_softness,
    attention_request_vectors,
    attention_lookup_vectors,
    attention_content_vectors,
    picture_distractor_partition,
    picture_distractor_slot,
    wording_distractor_partition,
    wording_distractor_slot,
    picture_couple_adjoint,
    wording_couple_adjoint,
):
    txt_count = lax.axis_size("txt")
    txt_place = lax.axis_index("txt")
    img_place = lax.axis_index("img")
    reordering_undo = 1.0 / logit_softness[0]
    unit_images = normalize_rows(picture_feature_vectors)
    unit_texts = normalize_rows(wording_feature_vectors)
    row_count = unit_images.shape[0]
    text_count = unit_texts.shape[0]
    contract = (((1,), (1,)), ((), ()))
    row_ids = (img_place * txt_count + txt_place) * row_count + jnp.arange(row_count)
    empty_rows = (
        jnp.full((row_count,), -jnp.inf, jnp.float32),
        jnp.zeros((row_count,), jnp.float32),
        jnp.zeros((row_count,), jnp.float32),
    )
    shard_rows = lax.all_gather(unit_texts, "txt", axis=0, tiled=True)
    row_state = empty_rows
    count_now = shard_rows.shape[0]
    logits = (
        lax.dot_general(unit_images, shard_rows, contract, preferred_element_type=jnp.float32)
        * reordering_undo
    )
    on_diag = jnp.where(row_ids[:, None] == jnp.arange(count_now)[None, :], logits, 0.0)
    row_state = join_totals(row_state, block_totals(logits, on_diag, 1))
    column_max, column_sum, column_diag = block_totals(logits, on_diag, 0)
    col_max = column_max
    col_sum = column_sum
    col_diag = column_diag
    row_totals, col_max, col_sum, col_diag = (row_state, col_max, col_sum, col_diag)
    col_max, col_sum, col_diag = combined_all(
        (col_max, col_sum, col_diag), ("img", "txt"), join_totals
    )
    first_text = txt_place * text_count
    col_max = lax.dynamic_slice_in_dim(col_max, first_text, text_count, 0)
    col_sum = lax.dynamic_slice_in_dim(col_sum, first_text, text_count, 0)
    col_diag = lax.dynamic_slice_in_dim(col_diag, first_text, text_count, 0)
    image_loss = row_totals[0] + jnp.log(row_totals[1]) - row_totals[2]
    text_loss = col_max + jnp.log(col_sum) - col_diag
    local_images = attention_request_vectors.shape[0]
    caption = attention_request_vectors.shape[1]
    width = attention_request_vectors.shape[2]
    patches = attention_lookup_vectors.shape[1]
    head_dim = width // HEADS
    factor = 1.0 / math.sqrt(head_dim)
    flat_size = caption * width
    entries = local_images * NEGS
    slot_limit = max(2, (entries + txt_count - 1) // txt_count)
    slot_total = txt_count * slot_limit
    slot_ids = jnp.arange(slot_limit)
    image_ids = jnp.arange(local_images)
    owner_ids = jnp.arange(txt_count)
    img_owner_blocks = picture_distractor_partition.reshape(txt_count, entries)
    img_slot_blocks = picture_distractor_slot.reshape(txt_count, entries)
    img_rank_blocks = owner_ranks(img_owner_blocks)
    txt_owner_blocks = wording_distractor_partition.reshape(txt_count, entries)
    txt_slot_blocks = wording_distractor_slot.reshape(txt_count, entries)
    txt_rank_blocks = owner_ranks(txt_owner_blocks)
    named_me = img_owner_blocks == txt_place
    chosen = (
        named_me[:, None, :, None]
        & (img_rank_blocks[:, None, :, None] == slot_ids[None, :, None, None])
        & (img_slot_blocks[:, None, :, None] == image_ids[None, None, None, :])
    )
    serve = jnp.sum(chosen.astype(jnp.int32), axis=2).astype(jnp.bfloat16)
    query_flat = attention_request_vectors.reshape(local_images, flat_size)
    send_image = jnp.einsum(
        "rmf,fx->rmx", serve, query_flat, preferred_element_type=jnp.float32
    ).astype(jnp.bfloat16)
    my_txt_owner = lax.dynamic_index_in_dim(txt_owner_blocks, txt_place, 0, keepdims=False)
    my_txt_rank = lax.dynamic_index_in_dim(txt_rank_blocks, txt_place, 0, keepdims=False)
    pick = (
        (my_txt_owner[None, None, :] == owner_ids[:, None, None])
        & (my_txt_rank[None, None, :] == slot_ids[None, :, None])
    ).astype(jnp.bfloat16)
    entry_queries = jnp.repeat(query_flat, NEGS, axis=0)
    send_query = jnp.einsum(
        "rme,ex->rmx", pick, entry_queries, preferred_element_type=jnp.float32
    ).astype(jnp.bfloat16)
    send_cot = jnp.einsum(
        "rme,ex->rmx",
        pick,
        wording_couple_adjoint.reshape(entries, flat_size),
        preferred_element_type=jnp.float32,
    ).astype(jnp.bfloat16)
    got_image, got_query, got_cot = (
        lax.all_to_all(send_image, "txt", split_axis=0, concat_axis=0, tiled=True),
        lax.all_to_all(send_query, "txt", split_axis=0, concat_axis=0, tiled=True),
        lax.all_to_all(send_cot, "txt", split_axis=0, concat_axis=0, tiled=True),
    )
    my_img_owner = lax.dynamic_index_in_dim(img_owner_blocks, txt_place, 0, keepdims=False)
    my_img_rank = lax.dynamic_index_in_dim(img_rank_blocks, txt_place, 0, keepdims=False)
    choose = (
        (
            (my_img_owner[:, None, None] == owner_ids[None, :, None])
            & (my_img_rank[:, None, None] == slot_ids[None, None, :])
        )
        .astype(jnp.bfloat16)
        .reshape(entries, slot_total)
    )
    image_queries = jnp.einsum(
        "ey,yx->ex",
        choose,
        got_image.reshape(slot_total, flat_size),
        preferred_element_type=jnp.float32,
    ).astype(jnp.bfloat16)
    query_heads = image_queries.reshape(local_images, NEGS * caption, HEADS, head_dim)
    key_heads = attention_lookup_vectors.reshape(local_images, patches, HEADS, head_dim)
    value_heads = attention_content_vectors.reshape(local_images, patches, HEADS, head_dim)
    weights, rounded, output = attend_forward(query_heads, key_heads, value_heads, factor)
    img_pair_out = output.astype(jnp.bfloat16).reshape(local_images, NEGS, caption, width)
    upstream = picture_couple_adjoint.reshape(local_images, NEGS * caption, HEADS, head_dim)
    image_qterm, key_total, value_total = attend_backward(
        query_heads, key_heads, value_heads, weights, rounded, upstream, factor
    )
    back_image = (
        jnp.einsum(
            "ey,ex->yx",
            choose,
            image_qterm.astype(jnp.bfloat16).reshape(entries, flat_size),
            preferred_element_type=jnp.float32,
        )
        .astype(jnp.bfloat16)
        .reshape(txt_count, slot_limit, flat_size)
    )
    named_here = txt_owner_blocks == txt_place
    matched = named_here[:, None, :] & (txt_rank_blocks[:, None, :] == slot_ids[None, :, None])
    slot_image = jnp.sum(jnp.where(matched, txt_slot_blocks[:, None, :], 0), axis=2)
    block_size = math.gcd(slot_total, 8)
    block_count = slot_total // block_size
    slot_queries = got_query.reshape(block_count, block_size, caption, HEADS, head_dim)
    slot_cots = got_cot.reshape(block_count, block_size, caption, HEADS, head_dim)
    slot_images = slot_image.reshape(block_count, block_size)

    def slot_pass(totals, inputs):
        key_sum, value_sum = totals
        block_queries, block_images, block_cots = inputs
        block_keys = key_heads[block_images]
        block_values = value_heads[block_images]
        block_weights, block_rounded, block_out = attend_forward(
            block_queries, block_keys, block_values, factor
        )
        query_part, key_part, value_part = attend_backward(
            block_queries,
            block_keys,
            block_values,
            block_weights,
            block_rounded,
            block_cots,
            factor,
        )
        chooser = (block_images[:, None] == image_ids[None, :]).astype(jnp.float32)
        key_sum = key_sum + jnp.einsum(
            "sf,sphd->fphd", chooser, key_part, precision=lax.Precision.HIGHEST
        )
        value_sum = value_sum + jnp.einsum(
            "sf,sphd->fphd", chooser, value_part, precision=lax.Precision.HIGHEST
        )
        return (
            (key_sum, value_sum),
            (block_out.astype(jnp.bfloat16), query_part.astype(jnp.bfloat16)),
        )

    (key_total, value_total), (slot_out, slot_grads) = lax.scan(
        slot_pass, (key_total, value_total), (slot_queries, slot_images, slot_cots)
    )
    slot_out = slot_out.reshape(txt_count, slot_limit, flat_size)
    slot_grads = slot_grads.reshape(txt_count, slot_limit, flat_size)
    got_out, got_grads, got_back = (
        lax.all_to_all(slot_out, "txt", split_axis=0, concat_axis=0, tiled=True),
        lax.all_to_all(slot_grads, "txt", split_axis=0, concat_axis=0, tiled=True),
        lax.all_to_all(back_image, "txt", split_axis=0, concat_axis=0, tiled=True),
    )
    txt_pair_out = (
        jnp.einsum("rme,rmx->ex", pick, got_out, preferred_element_type=jnp.float32)
        .astype(jnp.bfloat16)
        .reshape(local_images, NEGS, caption, width)
    )
    pick_rows = jnp.sum(pick.reshape(txt_count, slot_limit, local_images, NEGS), axis=3)
    query_sum = jnp.einsum(
        "rmf,rmx->fx", pick_rows, got_grads, preferred_element_type=jnp.float32
    ) + jnp.einsum("rmf,rmx->fx", serve, got_back, preferred_element_type=jnp.float32)
    query_grad = query_sum.astype(jnp.bfloat16).reshape(local_images, caption, width)
    key_grad = key_total.reshape(local_images, patches, width).astype(jnp.bfloat16)
    value_grad = value_total.reshape(local_images, patches, width).astype(jnp.bfloat16)
    return (image_loss, text_loss, img_pair_out, txt_pair_out, query_grad, key_grad, value_grad)


def solution(mesh):
    placed = (
        P(("img", "txt"), None),
        P("txt", None),
        P(),
        P(("img", "txt"), None, None),
        P(("img", "txt"), None, None),
        P(("img", "txt"), None, None),
        P("img", None),
        P("img", None),
        P("img", None),
        P("img", None),
        P(("img", "txt"), None, None, None),
        P(("img", "txt"), None, None, None),
    )
    return jax.shard_map(
        on_device,
        mesh=mesh,
        in_specs=placed,
        out_specs=(
            P(("img", "txt")),
            P("txt"),
            P(("img", "txt"), None, None, None),
            P(("img", "txt"), None, None, None),
            P(("img", "txt"), None, None),
            P(("img", "txt"), None, None),
            P(("img", "txt"), None, None),
        ),
        check_vma=False,
    )
```

profile of v0, /device:TPU:0, one launch (start us, length us, event | category | flops | bytes accessed | tf_op | source)
XLA Modules:
  0.0 800.7 jit_solution(16060746940004648343)
XLA Ops:
  13.3 7.4 all-to-all-start
  24.9 25.8 %all-to-all-done = bf16[8,2,26880]{2,1,0:T(2,128)(2,1)S(1)} async-done(((bf16[8,2,26880]{2,1,0:T(2,128)(2,1)}), bf16[8,2,26880]{2,1,0:T(2,128)(2,1)S(1)}, u32[]{:S(2)}, u32[]{:S(2)}) %all-to-all-start) | async-done | bytes 860192 | tf_op jit(solution)/shard_map/all_to_all | solution.py:182
  50.7 4.2 all-to-all-start.2
  69.5 4.3 copy.162
  73.8 4.4 fusion.151
  84.7 7.6 all-to-all-done.2
  92.3 4.7 all-to-all-start.1
  97.0 5.2 fusion.150
  102.2 4.4 reshape.328
  109.9 26.1 %fusion.104 = bf16[2,140,12,64]{1,3,2,0:T(8,128)(2,1)} fusion(bf16[2,257,12,64]{1,3,2,0:T(8,128)(2,1)S(1)} %bitcast.157, f32[2,12,140,257]{3,2,1,0:T(8,128)} %fusion.151, f32[2,12,140,257]{3,2,1,0:T(8,128)} %get-tuple-element.396, f32[2,12,140]{2,1,0:T(8,128)S(1)} %get-tuple-element.395), kind=kOutput, calls=%fused_computation.103 | convolution fusion | flops 116793856 | bytes 8141184 | tf_op jit(solution)/shard_map/bhqp,bphd->bqhd/dot_general | solution.py:67
  136.1 28.4 %fusion.96 = f32[2,257,12,64]{1,3,2,0:T(8,128)} fusion(bf16[2,140,12,64]{1,3,2,0:T(8,128)(2,1)} %copy.144, f32[2,12,140,257]{3,2,1,0:T(8,128)} %fusion.151, f32[2,12,140,257]{3,2,1,0:T(8,128)} %get-tuple-element.396, f32[2,12,140]{2,1,0:T(8,128)S(1)} %get-tuple-element.395), kind=kOutput, calls=%fused_computation.97 | convolution fusion | flops 116578816 | bytes 8930688 | tf_op jit(solution)/shard_map/bhqp,bqhd->bphd/dot_general | solution.py:70
  164.5 4.8 convolution_bitcast_fusion.6
  169.3 4.5 reshape.326
  177.4 4.9 copy.160
  191.7 6.0 all-to-all-start.5
  197.7 320.9 %while.37 = (s32[]{:T(128)}, f32[2,257,12,64]{1,0,3,2:T(2,128)}, f32[2,257,12,64]{1,0,3,2:T(2,128)}, bf16[2,8,35,12,64]{4,2,3,1,0:T(8,128)(2,1)}, bf16[2,8,35,12...) while((s32[]{:T(128)}, f32[2,257,12,64]{1,0,3,2:T(2,128)}, ...), condition=%wide.region_21.22_spmd.clone, body=%wide.region_17.21_spmd.clone.sunk | while | flops 759201344 | bytes 184476112 | solution.py:259
  218.2 6.1 gather_fusion.1
  224.2 12.1 %copy.214 = bf16[8,257,12,64]{1,3,2,0:T(8,128)(2,1)} copy(bf16[8,257,12,64]{3,2,1,0:T(8,128)(2,1)} %gather_fusion.1) | data formatting | bytes 6316032 | tf_op jit(solution)/shard_map/while/body/eval_jaxpr/gather | solution.py:233
  236.3 3.8 fusion.216
  240.1 3.8 fusion.217
  243.9 4.5 gather_fusion
  248.4 12.2 %copy.213 = bf16[8,257,12,64]{1,3,2,0:T(8,128)(2,1)} copy(bf16[8,257,12,64]{3,2,1,0:T(8,128)(2,1)} %gather_fusion) | data formatting | bytes 6316032 | tf_op jit(solution)/shard_map/while/body/eval_jaxpr/gather | solution.py:234
  260.6 7.1 fusion.221
  271.3 30.9 %fusion.222 = bf16[2,8,35,12,64]{4,2,3,1,0:T(8,128)(2,1)} fusion(bf16[2,8,35,12,64]{4,2,3,1,0:T(8,128)(2,1)} %get-tuple-element.564, s32[]{:T(128)S(6)} %copy.234, bf16[8,257,12,64]{1,3,2,0:T(8,128)(2,1)} %copy.214, f32[8,12,35,257]{3,2,1,0:T(8,128)} %fusion.215, f32[8,12,35,257]{3,2,1,0:T(8,128)} %get-tuple-element.517, ...), kind=kOutput, calls=%fused_computation.34.clone.1 | convolution fusion | flops 116793856 | bytes 29425668 | tf_op jit(solution)/shard_map/while/body/eval_jaxpr/bhqp,bphd->bqhd/dot_general | solution.py:67
  302.3 31.5 %convolution_bitcast_fusion.9 = f32[8,257,12,64]{1,3,2,0:T(8,128)} fusion(f32[8,12,35,257]{3,2,1,0:T(8,128)} %fusion.215, bf16[2,8,35,12,64]{4,2,3,1,0:T(8,128)(2,1)} %get-tuple-element.577, s32[]{:T(128)S(6)} %copy.234, f32[8,12,35,257]{3,2,1,0:T(8,128)} %get-tuple-element.517, f32[8,12,35]{2,1,0:T(8,128)S(1)} %get-tuple-element.518), kind=kOutput, calls=%fused_computation.20.clone.1 | convolution fusion | flops 116578816 | bytes 31023108 | tf_op jit(solution)/shard_map/while/body/eval_jaxpr/bhqp,bqhd->bphd/dot_general | solution.py:70
  333.8 15.8 %fusion.219 = f32[2,257,12,64]{1,0,3,2:T(2,128)} fusion(f32[2,257,12,64]{1,0,3,2:T(2,128)} %get-tuple-element.561, f32[8,257,12,64]{1,3,2,0:T(8,128)} %convolution_bitcast_fusion.9, s32[8]{0:T(128)S(1)} %fusion.218), kind=kOutput, calls=%fused_computation.29.clone.1 | convolution fusion | flops 38290960 | bytes 9474080 | tf_op jit(solution)/shard_map/while/body/eval_jaxpr/sf,sphd->fphd/dot_general | solution.py:248
  349.6 3.9 convolution_bitcast_fusion.10
  353.6 9.6 %fusion.220 = f32[2,257,12,64]{1,0,3,2:T(2,128)S(1)} fusion(f32[2,257,12,64]{1,0,3,2:T(2,128)S(1)} %copy-done.1, f32[8,257,12,64]{1,3,2,0:T(8,128)S(1)} %convolution_bitcast_fusion.10, s32[8]{0:T(128)S(1)} %fusion.218), kind=kOutput, calls=%fused_computation.30.clone.1 | convolution fusion | flops 38290960 | bytes 9474080 | tf_op jit(solution)/shard_map/while/body/eval_jaxpr/sf,sphd->fphd/dot_general | solution.py:251
  364.6 6.1 gather_fusion.1
  370.8 12.1 %copy.214 = bf16[8,257,12,64]{1,3,2,0:T(8,128)(2,1)} copy(bf16[8,257,12,64]{3,2,1,0:T(8,128)(2,1)} %gather_fusion.1) | data formatting | bytes 6316032 | tf_op jit(solution)/shard_map/while/body/eval_jaxpr/gather | solution.py:233
  382.9 3.8 fusion.216
  386.7 3.8 fusion.217
  390.5 4.5 gather_fusion
  395.0 12.2 %copy.213 = bf16[8,257,12,64]{1,3,2,0:T(8,128)(2,1)} copy(bf16[8,257,12,64]{3,2,1,0:T(8,128)(2,1)} %gather_fusion) | data formatting | bytes 6316032 | tf_op jit(solution)/shard_map/while/body/eval_jaxpr/gather | solution.py:234
  407.2 7.0 fusion.221
  417.9 30.9 %fusion.222 = bf16[2,8,35,12,64]{4,2,3,1,0:T(8,128)(2,1)} fusion(bf16[2,8,35,12,64]{4,2,3,1,0:T(8,128)(2,1)} %get-tuple-element.564, s32[]{:T(128)S(6)} %copy.234, bf16[8,257,12,64]{1,3,2,0:T(8,128)(2,1)} %copy.214, f32[8,12,35,257]{3,2,1,0:T(8,128)} %fusion.215, f32[8,12,35,257]{3,2,1,0:T(8,128)} %get-tuple-element.517, ...), kind=kOutput, calls=%fused_computation.34.clone.1 | convolution fusion | flops 116793856 | bytes 29425668 | tf_op jit(solution)/shard_map/while/body/eval_jaxpr/bhqp,bphd->bqhd/dot_general | solution.py:67
  448.9 31.5 %convolution_bitcast_fusion.9 = f32[8,257,12,64]{1,3,2,0:T(8,128)} fusion(f32[8,12,35,257]{3,2,1,0:T(8,128)} %fusion.215, bf16[2,8,35,12,64]{4,2,3,1,0:T(8,128)(2,1)} %get-tuple-element.577, s32[]{:T(128)S(6)} %copy.234, f32[8,12,35,257]{3,2,1,0:T(8,128)} %get-tuple-element.517, f32[8,12,35]{2,1,0:T(8,128)S(1)} %get-tuple-element.518), kind=kOutput, calls=%fused_computation.20.clone.1 | convolution fusion | flops 116578816 | bytes 31023108 | tf_op jit(solution)/shard_map/while/body/eval_jaxpr/bhqp,bqhd->bphd/dot_general | solution.py:70
  480.4 15.8 %fusion.219 = f32[2,257,12,64]{1,0,3,2:T(2,128)} fusion(f32[2,257,12,64]{1,0,3,2:T(2,128)} %get-tuple-element.561, f32[8,257,12,64]{1,3,2,0:T(8,128)} %convolution_bitcast_fusion.9, s32[8]{0:T(128)S(1)} %fusion.218), kind=kOutput, calls=%fused_computation.29.clone.1 | convolution fusion | flops 38290960 | bytes 9474080 | tf_op jit(solution)/shard_map/while/body/eval_jaxpr/sf,sphd->fphd/dot_general | solution.py:248
  496.2 3.9 convolution_bitcast_fusion.10
  500.2 9.6 %fusion.220 = f32[2,257,12,64]{1,0,3,2:T(2,128)S(1)} fusion(f32[2,257,12,64]{1,0,3,2:T(2,128)S(1)} %copy-done.1, f32[8,257,12,64]{1,3,2,0:T(8,128)S(1)} %convolution_bitcast_fusion.10, s32[8]{0:T(128)S(1)} %fusion.218), kind=kOutput, calls=%fused_computation.30.clone.1 | convolution fusion | flops 38290960 | bytes 9474080 | tf_op jit(solution)/shard_map/while/body/eval_jaxpr/sf,sphd->fphd/dot_general | solution.py:251
  522.6 6.5 all-to-all-start.3
  534.4 15.3 %all-to-all-done.3 = bf16[8,2,26880]{2,1,0:T(2,128)(2,1)} async-done(((bf16[8,2,26880]{2,1,0:T(2,128)(2,1)}), bf16[8,2,26880]{2,1,0:T(2,128)(2,1)}, u32[]{:S(2)}, u32[]{:S(2)}) %all-to-all-start.3) | async-done | bytes 860192 | tf_op jit(solution)/shard_map/all_to_all | solution.py:265
  549.7 4.2 all-to-all-start.4
  555.1 3.9 fusion.107
  583.7 69.2 %all-gather.2 = f32[131072]{0:T(1024)S(1)} all-gather(f32[4096]{0:T(1024)S(1)} %get-tuple-element.342), channel_id=4, replica_groups=mesh['img'=4,'txt'=8] {'img','txt'}, dimensions={0}, use_global_device_ids=true | all-gather | bytes 540672 | tf_op jit(solution)/shard_map/all_gather | solution.py:16
  653.1 66.5 %all-gather = f32[131072]{0:T(1024)S(1)} all-gather(f32[4096]{0:T(1024)S(1)} %get-tuple-element.346), channel_id=2, replica_groups=mesh['img'=4,'txt'=8] {'img','txt'}, dimensions={0}, use_global_device_ids=true | all-gather | bytes 540672 | tf_op jit(solution)/shard_map/all_gather | solution.py:16
  719.7 68.7 %all-gather.1 = f32[131072]{0:T(1024)S(1)} all-gather(f32[4096]{0:T(1024)S(1)} %get-tuple-element.344), channel_id=3, replica_groups=mesh['img'=4,'txt'=8] {'img','txt'}, dimensions={0}, use_global_device_ids=true | all-gather | bytes 540672 | tf_op jit(solution)/shard_map/all_gather | solution.py:16
  788.5 4.0 while.36
  (300 shorter events, 96.0 us)
Async XLA Ops:
  7.2 13.5 %copy-start.13 = (bf16[512,256]{1,0:T(8,128)(2,1)S(1)}, bf16[512,256]{1,0:T(8,128)(2,1)}, u32[]{:S(2)}) copy-start(bf16[512,256]{1,0:T(8,128)(2,1)} %param.17) | copy-start | bytes 786436
  7.2 14.6 %copy-start.15 = (bf16[2,4,35,768]{3,1,2,0:T(4,128)(2,1)S(1)}, bf16[2,4,35,768]{3,1,2,0:T(4,128)(2,1)}, u32[]{:S(2)}) copy-start(bf16[2,4,35,768]{3,1,2,0:T(4,128)(2,1)} %param.27) | copy-start | bytes 1290244
  10.4 11.4 %copy-start.21 = (s32[8,2,2]{0,2,1:T(2,128)}, s32[8,2,2]{0,2,1:T(2,128)S(1)}, u32[]{:S(2)}) copy-start(s32[8,2,2]{0,2,1:T(2,128)S(1)} %convert_reduce_fusion) | copy-start | bytes 388
  13.3 41.7 %copy-start.27 = (s32[16,4]{0,1:T(4,128)S(1)}, s32[16,4]{0,1:T(4,128)}, u32[]{:S(2)}) copy-start(s32[16,4]{0,1:T(4,128)} %param.25) | copy-start | bytes 772
  13.3 42.2 %copy-start.16 = (bf16[2,35,768]{2,0,1:T(2,128)(2,1)S(1)}, bf16[2,35,768]{2,0,1:T(2,128)(2,1)}, u32[]{:S(2)}) copy-start(bf16[2,35,768]{2,0,1:T(2,128)(2,1)} %param.19) | copy-start | bytes 322564
  13.3 37.4 %all-to-all-start = ((bf16[8,2,26880]{2,1,0:T(2,128)(2,1)}), bf16[8,2,26880]{2,1,0:T(2,128)(2,1)S(1)}, u32[]{:S(2)}, u32[]{:S(2)}) async-start(bf16[8,2,26880]{2,1,0:T(2,128)(2,1)} %copy.140), calls=%async_computation | async-start | bytes 1720320 | tf_op jit(solution)/shard_map/all_to_all | solution.py:182
  20.7 559.3 %all-gather.5.cloned.1.call-start = ((), (), s32[]{:S(2)}) async-start(), calls=%async_computation.6 | async-start | bytes 2359296 | tf_op jit(solution)/shard_map/all_gather | solution.py:112
  22.1 35.8 %copy-start.14 = (bf16[2,257,768]{2,0,1:T(2,128)(2,1)S(1)}, bf16[2,257,768]{2,0,1:T(2,128)(2,1)}, u32[]{:S(2)}) copy-start(bf16[2,257,768]{2,0,1:T(2,128)(2,1)} %param.20) | copy-start | bytes 2368516
  22.7 37.3 %copy-start.25 = (pred[2,8]{1,0:T(4,128)(4,1)}, pred[2,8]{1,0:T(4,128)(4,1)S(1)}, u32[]{:S(2)}) copy-start(pred[2,8]{1,0:T(4,128)(4,1)S(1)} %iota_compare_fusion.12) | copy-start | bytes 52
  22.8 35.0 %copy-start.23 = (pred[8,8]{0,1:T(8,128)(4,1)}, pred[8,8]{0,1:T(8,128)(4,1)S(1)}, u32[]{:S(2)}) copy-start(pred[8,8]{0,1:T(8,128)(4,1)S(1)} %iota_compare_fusion.8) | copy-start | bytes 196
  50.7 9.3 %copy-start.9 = (bf16[8,2,26880]{2,1,0:T(2,128)(2,1)}, bf16[8,2,26880]{2,1,0:T(2,128)(2,1)S(1)}, u32[]{:S(2)}) copy-start(bf16[8,2,26880]{2,1,0:T(2,128)(2,1)S(1)} %all-to-all-done) | copy-start | bytes 2580484
  50.7 41.6 %all-to-all-start.2 = ((bf16[8,2,26880]{2,1,0:T(2,128)(2,1)}), bf16[8,2,26880]{2,1,0:T(2,128)(2,1)}, u32[]{:S(2)}, u32[]{:S(2)}) async-start(bf16[8,2,26880]{2,1,0:T(2,128)(2,1)} %copy.158), calls=%async_computation.2 | async-start | bytes 1720320 | tf_op jit(solution)/shard_map/all_to_all | solution.py:184
  62.4 11.4 %copy-start.6 = (bf16[2,257,768]{1,2,0:T(8,128)(2,1)}, bf16[2,257,768]{1,2,0:T(8,128)(2,1)S(1)}, u32[]{:S(2)}) copy-start(bf16[2,257,768]{1,2,0:T(8,128)(2,1)S(1)} %copy.145) | copy-start | bytes 2368516
  73.8 4.4 copy-start.10
  78.3 18.7 %copy-start.8 = (bf16[2,257,768]{1,2,0:T(8,128)(2,1)S(1)}, bf16[2,257,768]{1,2,0:T(8,128)(2,1)}, u32[]{:S(2)}) copy-start(bf16[2,257,768]{1,2,0:T(8,128)(2,1)} %copy.143) | copy-start | bytes 2368516
  92.3 77.0 %all-to-all-start.1 = ((bf16[8,2,26880]{2,1,0:T(2,128)(2,1)}), bf16[8,2,26880]{2,1,0:T(2,128)(2,1)}, u32[]{:S(2)}, u32[]{:S(2)}) async-start(bf16[8,2,26880]{2,1,0:T(2,128)(2,1)} %copy.155), calls=%async_computation.1 | async-start | bytes 1720320 | tf_op jit(solution)/shard_map/all_to_all | solution.py:183
  102.2 62.4 %copy-start.19 = (f32[2,12,140]{2,1,0:T(8,128)}, f32[2,12,140]{2,1,0:T(8,128)S(1)}, u32[]{:S(2)}) copy-start(f32[2,12,140]{2,1,0:T(8,128)S(1)} %get-tuple-element.395) | copy-start | bytes 40324
  136.1 28.4 %copy-start.11 = (bf16[2,140,12,64]{1,3,2,0:T(8,128)(2,1)S(1)}, bf16[2,140,12,64]{1,3,2,0:T(8,128)(2,1)}, u32[]{:S(2)}) copy-start(bf16[2,140,12,64]{1,3,2,0:T(8,128)(2,1)} %reshape.376) | copy-start | bytes 1290244
  173.8 8.5 %copy-start.12 = (f32[2,257,12,64]{1,3,2,0:T(8,128)S(1)}, f32[2,257,12,64]{1,3,2,0:T(8,128)}, u32[]{:S(2)}) copy-start(f32[2,257,12,64]{1,3,2,0:T(8,128)} %fusion.96) | copy-start | bytes 4737028
  191.7 330.9 %all-to-all-start.5 = ((bf16[8,2,26880]{2,1,0:T(2,128)(2,1)}), bf16[8,2,26880]{2,1,0:T(2,128)(2,1)}, u32[]{:S(2)}, u32[]{:S(2)}) async-start(bf16[8,2,26880]{2,1,0:T(2,128)(2,1)} %reshape.333), calls=%async_computation.5 | async-start | bytes 1720320 | tf_op jit(solution)/shard_map/all_to_all | solution.py:267
  260.6 7.1 copy-start
  260.6 7.1 copy-start.4
  333.8 15.8 %copy-start.5 = (bf16[2,8,35,12,64]{4,2,3,1,0:T(8,128)(2,1)S(1)}, bf16[2,8,35,12,64]{4,2,3,1,0:T(8,128)(2,1)}, u32[]{:S(2)}) copy-start(bf16[2,8,35,12,64]{4,2,3,1,0:T(8,128)(2,1)} %get-tuple-element.579) | copy-start | bytes 2580484 | tf_op jit(solution)/shard_map/while
  349.6 3.9 copy-start.1
  363.2 1.4 copy-start.2
  407.2 7.1 copy-start
  407.2 7.1 copy-start.4
  480.4 15.8 %copy-start.5 = (bf16[2,8,35,12,64]{4,2,3,1,0:T(8,128)(2,1)S(1)}, bf16[2,8,35,12,64]{4,2,3,1,0:T(8,128)(2,1)}, u32[]{:S(2)}) copy-start(bf16[2,8,35,12,64]{4,2,3,1,0:T(8,128)(2,1)} %get-tuple-element.579) | copy-start | bytes 2580484 | tf_op jit(solution)/shard_map/while
  496.2 3.9 copy-start.1
  509.8 1.4 copy-start.2
  518.6 11.3 %copy-start.31 = (s32[8]{0:T(128)S(1)}, s32[8]{0:T(128)}, u32[]{:S(2)}) copy-start(s32[8]{0:T(128)} %get-tuple-element.390) | copy-start | bytes 100
  518.6 11.4 %copy-start.30 = (s32[8]{0:T(128)S(1)}, s32[8]{0:T(128)}, u32[]{:S(2)}) copy-start(s32[8]{0:T(128)} %get-tuple-element.400) | copy-start | bytes 100
  518.6 11.7 %copy-start.17 = (bf16[128,256]{1,0:T(8,128)(2,1)S(1)}, bf16[128,256]{1,0:T(8,128)(2,1)}, u32[]{:S(2)}) copy-start(bf16[128,256]{1,0:T(8,128)(2,1)} %param.16) | copy-start | bytes 196612
  522.6 27.1 %all-to-all-start.3 = ((bf16[8,2,26880]{2,1,0:T(2,128)(2,1)}), bf16[8,2,26880]{2,1,0:T(2,128)(2,1)}, u32[]{:S(2)}, u32[]{:S(2)}) async-start(bf16[8,2,26880]{2,1,0:T(2,128)(2,1)} %reshape.329), calls=%async_computation.3 | async-start | bytes 1720320 | tf_op jit(solution)/shard_map/all_to_all | solution.py:265
  529.2 25.9 %copy-start.7 = (bf16[2,257,768]{1,2,0:T(8,128)(2,1)S(1)}, bf16[2,257,768]{1,2,0:T(8,128)(2,1)}, u32[]{:S(2)}) copy-start(bf16[2,257,768]{1,2,0:T(8,128)(2,1)} %copy-done.6) | copy-start | bytes 2368516
  529.2 25.9 %copy-start.20 = (f32[2,12,140]{2,1,0:T(8,128)S(1)}, f32[2,12,140]{2,1,0:T(8,128)}, u32[]{:S(2)}) copy-start(f32[2,12,140]{2,1,0:T(8,128)} %copy-done.19) | copy-start | bytes 40324
  549.7 28.1 %all-to-all-start.4 = ((bf16[8,2,26880]{2,1,0:T(2,128)(2,1)}), bf16[8,2,26880]{2,1,0:T(2,128)(2,1)}, u32[]{:S(2)}, u32[]{:S(2)}) async-start(bf16[8,2,26880]{2,1,0:T(2,128)(2,1)} %reshape.331), calls=%async_computation.4 | async-start | bytes 1720320 | tf_op jit(solution)/shard_map/all_to_all | solution.py:266
  559.0 10.7 %copy-start.3 = (f32[2,257,12,64]{1,0,3,2:T(2,128)S(1)}, f32[2,257,12,64]{1,0,3,2:T(2,128)}, u32[]{:S(2)}) copy-start(f32[2,257,12,64]{1,0,3,2:T(2,128)} %get-tuple-element.251) | copy-start | bytes 4737028
  564.3 9.3 %copy-start.24 = (pred[8,8]{0,1:T(8,128)(4,1)S(1)}, pred[8,8]{0,1:T(8,128)(4,1)}, u32[]{:S(2)}) copy-start(pred[8,8]{0,1:T(8,128)(4,1)} %copy-done.23) | copy-start | bytes 196
  564.3 9.3 %copy-start.26 = (pred[2,8]{1,0:T(4,128)(4,1)S(1)}, pred[2,8]{1,0:T(4,128)(4,1)}, u32[]{:S(2)}) copy-start(pred[2,8]{1,0:T(4,128)(4,1)} %copy-done.25) | copy-start | bytes 52
  569.7 6.6 copy-start.22
  570.6 9.3 %copy-start.18 = (bf16[128,256]{1,0:T(8,128)(2,1)S(1)}, bf16[128,256]{1,0:T(8,128)(2,1)}, u32[]{:S(2)}) copy-start(bf16[128,256]{1,0:T(8,128)(2,1)} %param.16) | copy-start | bytes 196612
  570.7 9.3 %copy-start.29 = (f32[128]{0:T(128)S(1)}, f32[128]{0:T(128)}, u32[]{:S(2)}) copy-start(f32[128]{0:T(128)} %add_rsqrt_fusion.1) | copy-start | bytes 1540
  573.6 8.8 %copy-start.28 = (s32[128]{0:T(128)S(1)}, s32[128]{0:T(128)}, u32[]{:S(2)}) copy-start(s32[128]{0:T(128)} %iota_add_fusion) | copy-start | bytes 1540
Sparse Core Ops, SparseCore 0:
  23.6 68.6 all-gather.4
where the time goes:
time: 811 us; the launch traced here: 801 us
  matrix products  298 us (37%)
  blocking collectives  204 us (25%)
  local copies, waits for them, and re-layouts  154 us (19%)
  waiting for transfers between devices  48.7 us (6%)
  starting transfers between devices  33.1 us (4%)
  loops' own time  29.3 us (4%)
  other arithmetic  17.8 us (2%)
  between operations  15.5 us (2%)
    all_gather x3, blocking collectives, combined_all(): gathered = jax.tree.map(lambda a: lax.all_gather(a, axis), part)  204 us
    dot_general x3, matrix products, attend_backward(): jnp.einsum('bhqp,bqhd->bphd', logit_term, query_part, preferred_element_t...  91.5 us
    dot_general x3, matrix products, attend_backward(): jnp.einsum('bhqp,bphd->bqhd', logit_term, key_part, preferred_element_typ...  88 us
    unnamed x71, local copies, waits for them, and re-layouts  39.7 us
    gather x4, local copies, waits for them, and re-layouts, slot_pass(): block_keys = key_heads[block_images]  36.4 us
    gather x4, local copies, waits for them, and re-layouts, slot_pass(): block_values = value_heads[block_images]  33.3 us
    dot_general x2, matrix products, slot_pass(): jnp.einsum('sf,sphd->fphd', chooser, key_part, precision=lax.Precision.HI...  31.7 us
    another operation x1, loops' own time, on_device(): lax.scan(slot_pass, (key_total, value_total), (slot_queries, slot_images,...  27.9 us
  transfers between devices with their start and end apart: 7, of which 3 were waited for; matrix products, arithmetic and copies ran while one was open for 57% of the time, Pallas kernels for 0%

commit v1 on v0

v1 whole, which is shorter than its diff:
```python
import functools
import math

import jax
import jax.numpy as jnp
from jax import lax
from jax.experimental import pallas as pl
from jax.experimental.pallas import tpu as pltpu
from jax.sharding import PartitionSpec as P

HEADS = 12
NEGS = 4
EPSILON = 1e-06
LANES = 128
VMEM = pl.BlockSpec(memory_space=pltpu.VMEM)
SMEM = pl.BlockSpec(memory_space=pltpu.SMEM)
F32 = jnp.float32
BF16 = jnp.bfloat16
NT = (((1,), (1,)), ((), ()))
NN = (((1,), (0,)), ((), ()))


def kernel_call(body, out_shape, n_smem, n_vmem, scratch=(), flops=0, nbytes=0):
    return pl.pallas_call(
        body,
        out_shape=out_shape,
        in_specs=[SMEM] * n_smem + [VMEM] * n_vmem,
        out_specs=jax.tree.map(lambda _: VMEM, out_shape),
        scratch_shapes=list(scratch),
        compiler_params=pltpu.CompilerParams(vmem_limit_bytes=40 * 1024 * 1024),
        cost_estimate=pl.CostEstimate(flops=flops, bytes_accessed=nbytes, transcendentals=0),
    )


def dot(a, b, dims):
    return lax.dot_general(a, b, dims, preferred_element_type=F32)


def send_body(owners, place, cots, sent):
    rows = cots.shape[0]
    sent[...] = jnp.zeros_like(sent)
    for row in range(rows):
        for entry in range(NEGS):
            sent[owners[place[0] * rows + row, entry], row] = cots[row, entry]


def contrast_body(place, softness, images, texts, row_stats, col_stats, unit_images, unit_texts):
    for source, unit in ((images, unit_images), (texts, unit_texts)):
        wide = source[...].astype(F32)
        factor = lax.rsqrt(jnp.sum(wide * wide, axis=-1, keepdims=True) + EPSILON)
        unit[...] = (wide * factor).astype(BF16)
    undo = 1.0 / softness[0]
    n_images, n_texts = images.shape[0], texts.shape[0]
    first_image, first_text = place[1] * n_images, place[0] * n_texts

    def stats(long, long_first, short, short_first):
        logits = dot(long, short, NT) * undo
        highest = jnp.max(logits, axis=0, keepdims=True)
        total = jnp.sum(jnp.exp(logits - highest), axis=0, keepdims=True)
        on_diag = (lax.broadcasted_iota(jnp.int32, logits.shape, 0) + long_first) == (
            lax.broadcasted_iota(jnp.int32, logits.shape, 1) + short_first
        )
        diag = jnp.sum(jnp.where(on_diag, logits, 0.0), axis=0, keepdims=True)
        return highest + jnp.log(total), diag

    for block in range(n_images // LANES):
        first = block * LANES
        lse, diag = stats(
            unit_texts[...], first_text, unit_images[first : first + LANES, :], first_image + first
        )
        row_stats[block, 0:1, :] = lse
        row_stats[block, 1:2, :] = diag
    for block in range(n_texts // LANES):
        first = block * LANES
        lse, diag = stats(
            unit_images[...], first_image, unit_texts[first : first + LANES, :], first_text + first
        )
        col_stats[0:1, first : first + LANES] = lse
        col_stats[1:2, first : first + LANES] = diag


def attend(image, q_at, g_at, queries, cots, keys, values, key_sum, value_sum, key_last, value_last, emit):
    rows = queries.shape[1]
    stack = rows * NEGS
    patches = keys.shape[1] - 1
    half = LANES // 2

    def tile_step(tile, _):
        lanes = pl.ds(pl.multiple_of(tile * LANES, LANES), LANES)
        low = lax.broadcasted_iota(jnp.int32, (stack, LANES), 1) < half
        q = jnp.concatenate([queries[at, :, lanes] for at in q_at], axis=0)
        g = jnp.concatenate([cots[at, :, lanes] for at in g_at], axis=0)
        q2 = jnp.concatenate([jnp.where(low, q, 0.0), jnp.where(low, 0.0, q)], axis=0)
        g2 = jnp.concatenate([jnp.where(low, g, 0.0), jnp.where(low, 0.0, g)], axis=0)
        key, value = keys[image, 0:patches, lanes], values[image, 0:patches, lanes]
        key_end = keys[image, patches : patches + 1, lanes].astype(F32)
        value_end = values[image, patches : patches + 1, lanes].astype(F32)
        logits = dot(q2.astype(BF16), key, NT)
        logit_end = jnp.sum(q2 * key_end, axis=-1, keepdims=True)
        highest = jnp.maximum(jnp.max(logits, axis=-1, keepdims=True), logit_end)
        shifted = jnp.exp(logits - highest)
        shifted_end = jnp.exp(logit_end - highest)
        inverse = 1.0 / (jnp.sum(shifted, axis=-1, keepdims=True) + shifted_end)
        weights = shifted * inverse
        weight_end = shifted_end * inverse
        rounded = weights.astype(BF16)
        rounded_end = weight_end.astype(BF16).astype(F32)
        output = dot(rounded, value, NN) + rounded_end * value_end
        term = dot(g2.astype(BF16), value, NT)
        term_end = jnp.sum(g2 * value_end, axis=-1, keepdims=True)
        inner = jnp.sum(weights * term, axis=-1, keepdims=True) + weight_end * term_end
        logit_term = (weights * (term - inner)).astype(BF16)
        logit_term_end = (weight_end * (term_end - inner)).astype(BF16).astype(F32)
        q_term = (dot(logit_term, key, NN) + logit_term_end * key_end) * 0.125
        emit(
            lanes,
            jnp.where(low, output[:stack], output[stack:]),
            jnp.where(low, q_term[:stack], q_term[stack:]),
        )
        q_turned = jnp.transpose(q).astype(BF16)
        g_turned = jnp.transpose(g).astype(BF16)
        for head in range(2):
            at = pl.ds(pl.multiple_of(tile * LANES, LANES) + head * half, half)
            part = slice(head * half, head * half + half)
            line = slice(head * stack, head * stack + stack)
            key_sum[image, at, :] += dot(q_turned[part], logit_term[line], NN)
            value_sum[image, at, :] += dot(g_turned[part], rounded[line], NN)
        key_last[image, :, lanes] += jnp.sum(logit_term_end * q2, axis=0, keepdims=True)
        value_last[image, :, lanes] += jnp.sum(rounded_end * g2, axis=0, keepdims=True)
        return 0

    lax.fori_loop(0, keys.shape[2] // LANES, tile_step, 0)


def widen(source, wide, at, scale=1.0):
    caption = source.shape[0]
    wide[at, caption:, :] = jnp.zeros((wide.shape[1] - caption, wide.shape[2]), F32)
    wide[at, 0:caption, :] = source.astype(F32) * scale


def image_body(n_parts, owners, slots, place, *refs):
    parts, refs = refs[:n_parts], refs[n_parts:]
    cots, keys, values, out, key_sum, value_sum, key_last, value_last, q_sum, queries, wide = refs
    images, captions = keys.shape[0], parts[0].shape[0]
    caption = parts[0].shape[1]
    for part in range(n_parts):
        for row in range(captions):
            widen(parts[part][row], queries, part * captions + row, 0.125)
    for image in range(images):
        for entry in range(NEGS):
            widen(cots[image, entry], wide, image * NEGS + entry)
    for total in (key_sum, value_sum, key_last, value_last, q_sum):
        total[...] = jnp.zeros_like(total)

    def image_step(image, _):
        line = place[0] * images + image
        at = [
            jnp.bitwise_xor(owners[line, e], place[0]) * captions + slots[line, e] for e in range(NEGS)
        ]
        rows = queries.shape[1]

        def emit(lanes, output, q_term):
            for e in range(NEGS):
                out[image, e, :, lanes] = output[e * rows : e * rows + caption].astype(BF16)
                q_sum[at[e], :, lanes] += (
                    q_term[e * rows : (e + 1) * rows].astype(BF16).astype(F32)
                )

        attend(
            image, at, [image * NEGS + e for e in range(NEGS)], queries, wide, keys, values,
            key_sum, value_sum, key_last, value_last, emit,
        )
        return 0

    lax.fori_loop(0, images, image_step, 0)


def text_body(n_parts, owners, slots, place, *refs):
    parts, refs = refs[:n_parts], refs[n_parts:]
    (cots, keys, values, key_in, value_in, key_last_in, value_last_in, q_in,
     out, q_out, key_grad, value_grad,
     queries, wide, outs, key_sum, value_sum, key_last, value_last, q_sum, lists, counts) = refs
    images, captions = keys.shape[0], parts[0].shape[0]
    caption = parts[0].shape[1]
    rows = queries.shape[1]
    patches = keys.shape[1] - 1
    everyone = n_parts * captions
    for part in range(n_parts):
        for row in range(captions):
            widen(parts[part][row], queries, part * captions + row, 0.125)
            widen(cots[part, row], wide, part * captions + row)
    for ref in (queries, wide):
        ref[everyone] = jnp.zeros(ref.shape[1:], F32)
    key_sum[...] = key_in[...]
    value_sum[...] = value_in[...]
    key_last[...] = key_last_in[...]
    value_last[...] = value_last_in[...]
    q_sum[0:everyone] = q_in[...]
    outs[...] = jnp.zeros_like(outs)
    for image in range(images):
        counts[image] = 0

        def clear(i, _, image=image):
            lists[image, i] = everyone
            return 0

        lax.fori_loop(0, lists.shape[1], clear, 0)

    def find(j, _):
        for entry in range(NEGS):

            @pl.when(owners[j, entry] == place[0])
            def _():
                image = slots[j, entry]
                lists[image, counts[image]] = j
                counts[image] = counts[image] + 1

        return 0

    lax.fori_loop(0, everyone, find, 0)

    def image_step(image, _):
        def chunk_step(chunk, _):
            j = [lists[image, chunk * NEGS + e] for e in range(NEGS)]
            q_at = [
                jnp.where(
                    j[e] < everyone,
                    jnp.bitwise_xor(j[e] // captions, place[0]) * captions + j[e] % captions,
                    everyone,
                )
                for e in range(NEGS)
            ]

            def emit(lanes, output, q_term):
                for e in range(NEGS):
                    outs[j[e], :, lanes] = output[e * rows : (e + 1) * rows]
                    q_sum[q_at[e], :, lanes] += (
                        q_term[e * rows : (e + 1) * rows].astype(BF16).astype(F32)
                    )

            attend(
                image, q_at, j, queries, wide, keys, values,
                key_sum, value_sum, key_last, value_last, emit,
            )
            return 0

        lax.fori_loop(0, (counts[image] + NEGS - 1) // NEGS, chunk_step, 0)
        return 0

    lax.fori_loop(0, images, image_step, 0)

    def finish(part, _):
        source = jnp.bitwise_xor(part, place[0])
        for row in range(captions):
            out[part, row] = outs[part * captions + row, 0:caption, :].astype(BF16)
            q_out[part, row] = q_sum[source * captions + row, 0:caption, :].astype(BF16)
        return 0

    lax.fori_loop(0, n_parts, finish, 0)
    for total, last, grad in ((key_sum, key_last, key_grad), (value_sum, value_last, value_grad)):
        for image in range(images):
            for tile in range(keys.shape[2] // LANES):
                lanes = slice(tile * LANES, (tile + 1) * LANES)
                grad[image, 0:patches, lanes] = jnp.transpose(total[image, lanes, :]).astype(BF16)
            grad[image, patches : patches + 1, :] = last[image].astype(BF16)


def join_body(owners, place, got_out, got_q, pair_out, q_grad):
    rows = pair_out.shape[0]
    for row in range(rows):
        for entry in range(NEGS):
            pair_out[row, entry] = got_out[owners[place[0] * rows + row, entry], row]
        total = got_q[0, row].astype(F32)
        for source in range(1, got_q.shape[0]):
            total = total + got_q[source, row].astype(F32)
        q_grad[row] = total.astype(BF16)


def gathered(block, axis):
    size = lax.axis_size(axis)
    half = size // 2

    def swap(part, mask):
        return lax.ppermute(part, axis, [(s, s ^ mask) for s in range(size)])

    other = swap(block, half)
    near = [block] + [swap(block, mask) for mask in range(1, half)]
    far = [other] + [swap(other, mask) for mask in range(1, half)]
    return near + far


def joined(lse, axis):
    highest = jnp.max(lse, axis=axis, keepdims=True)
    return jnp.squeeze(highest, axis) + jnp.log(jnp.sum(jnp.exp(lse - highest), axis=axis))


def on_device(
    pictures,
    wordings,
    softness,
    queries,
    keys,
    values,
    img_owner,
    img_slot,
    txt_owner,
    txt_slot,
    img_cots,
    txt_cots,
):
    shape = jax.ShapeDtypeStruct
    n_txt = lax.axis_size("txt")
    place = jnp.stack([lax.axis_index("txt"), lax.axis_index("img")]).astype(jnp.int32)
    local, caption, width = queries.shape
    patches = keys.shape[1] - 1
    rows = (caption + 7) // 8 * 8
    everyone = n_txt * local
    slot_shape = (n_txt, local, caption, width)

    parts = gathered(queries, "txt")
    all_pictures = lax.all_gather(pictures, "txt", axis=0, tiled=True)
    sent = kernel_call(send_body, shape(slot_shape, BF16), 2, 1)(txt_owner, place, txt_cots)
    got_cots = lax.all_to_all(sent, "txt", 0, 0, tiled=True)

    pair_flops = 10 * caption * (patches + 1) * width
    sums = (
        shape((local, width, patches), F32),
        shape((local, width, patches), F32),
        shape((local, 1, width), F32),
        shape((local, 1, width), F32),
        shape((everyone, rows, width), F32),
    )
    img_pair_out, *partial = kernel_call(
        functools.partial(image_body, n_txt),
        (shape((local, NEGS, caption, width), BF16),) + sums,
        3,
        n_txt + 3,
        [pltpu.VMEM((everyone, rows, width), F32), pltpu.VMEM((local * NEGS, rows, width), F32)],
        flops=4 * local * NEGS * pair_flops,
        nbytes=10_000_000,
    )(img_owner, img_slot, place, *parts, img_cots, keys, values)

    row_stats, col_stats = kernel_call(
        contrast_body,
        (
            shape((all_pictures.shape[0] // LANES, 2, LANES), F32),
            shape((2, wordings.shape[0]), F32),
        ),
        2,
        2,
        [pltpu.VMEM(all_pictures.shape, BF16), pltpu.VMEM(wordings.shape, BF16)],
        flops=4 * all_pictures.shape[0] * wordings.shape[0] * 256,
        nbytes=1_000_000,
    )(place, softness, all_pictures, wordings)

    out, q_out, key_grad, value_grad = kernel_call(
        functools.partial(text_body, n_txt),
        (
            shape(slot_shape, BF16),
            shape(slot_shape, BF16),
            shape(keys.shape, BF16),
            shape(values.shape, BF16),
        ),
        3,
        n_txt + 8,
        [
            pltpu.VMEM((everyone + 1, rows, width), F32),
            pltpu.VMEM((everyone + 1, rows, width), F32),
            pltpu.VMEM((everyone + 1, rows, width), F32),
            *[pltpu.VMEM(s.shape, F32) for s in sums[:4]],
            pltpu.VMEM((everyone + 1, rows, width), F32),
            pltpu.SMEM((local, everyone + NEGS), jnp.int32),
            pltpu.SMEM((local,), jnp.int32),
        ],
        flops=4 * local * NEGS * pair_flops,
        nbytes=10_000_000,
    )(txt_owner, txt_slot, place, *parts, got_cots, keys, values, *partial)

    got_out = lax.all_to_all(out, "txt", 0, 0, tiled=True)
    got_q = lax.all_to_all(q_out, "txt", 0, 0, tiled=True)
    row_parts = row_stats.reshape(n_txt, -1, 2, LANES)
    got_rows = lax.all_to_all(row_parts, "txt", 0, 0, tiled=True)
    got_cols = lax.all_gather(col_stats, "img", axis=0)
    image_loss = (joined(got_rows[:, :, 0], 0) - jnp.sum(got_rows[:, :, 1], axis=0)).reshape(-1)
    text_loss = joined(got_cols[:, 0], 0) - jnp.sum(got_cols[:, 1], axis=0)
    txt_pair_out, query_grad = kernel_call(
        join_body, (shape(txt_cots.shape, BF16), shape(queries.shape, BF16)), 2, 2
    )(txt_owner, place, got_out, got_q)
    return (image_loss, text_loss, img_pair_out, txt_pair_out, query_grad, key_grad, value_grad)


def solution(mesh):
    every = ("img", "txt")
    three, four = P(every, None, None), P(every, None, None, None)
    table = P("img", None)
    return jax.shard_map(
        on_device,
        mesh=mesh,
        in_specs=(P(every, None), P("txt", None), P(), three, three, three)
        + (table, table, table, table, four, four),
        out_specs=(P(every), P("txt"), four, four, three, three, three),
        check_vma=False,
    )
```

time: 811 us -> 189 us (0.23)
  matrix products: 298 us -> 0 us
  blocking collectives: 204 us -> 37 us
  local copies, waits for them, and re-layouts: 154 us -> 37.9 us
  Pallas kernels: 0 us -> 30.3 us
  loops' own time: 29.3 us -> 0 us
  other arithmetic: 17.8 us -> 1.31 us
  between operations: 15.5 us -> 1.53 us
  waiting for transfers between devices: 48.7 us -> 40 us
    dot_general x30 -> x0, matrix products: 293 us -> none  [the longest x3 91.5 us: attend_backward(): jnp.einsum('bhqp,bqhd->bphd', logit_term, query_part, preferred_element_t...]
    all_gather x3 -> x2, blocking collectives: 204 us -> 37 us  [the longest x1 31.5 us: on_device(): all_pictures = lax.all_gather(pictures, 'txt', axis=0, tiled=True)]
    gather x8 -> x0, local copies, waits for them, and re-layouts: 69.7 us -> none  [the longest x4 36.4 us: slot_pass(): block_keys = key_heads[block_images]]
    pallas_call x0 -> x5, Pallas kernels: none -> 30.3 us  [the longest x1 16.3 us: on_device(): kernel_call(functools.partial(text_body, n_txt), (shape(slot_shape, BF16)...]
    another operation x2 -> x0, loops' own time: 29.3 us -> none  [the longest x1 27.9 us: on_device(): lax.scan(slot_pass, (key_total, value_total), (slot_queries, slot_images,...]
    all_to_all x6 -> x4, waiting for transfers between devices: 48.6 us -> 19.4 us  [the longest x1 13.3 us: on_device(): got_out = lax.all_to_all(out, 'txt', 0, 0, tiled=True)]
    reshape x17 -> x0, local copies, waits for them, and re-layouts: 27.8 us -> none  [the longest x2 5.37 us: on_device(): image_queries.reshape(local_images, NEGS * caption, HEADS, head_dim)]
    ppermute x0 -> x7, waiting for transfers between devices: none -> 20.6 us  [swap(): return lax.ppermute(part, axis, [(s, s ^ mask) for s in range(size)])]
  transfers between devices with their start and end apart: 7 -> 11, of which waited for: 3 -> 3; matrix products, arithmetic and copies ran while one was open for 57% -> 7% of each run, Pallas kernels for 0% -> 16%
where the time goes in v1:
time: 189 us; the launch traced here: 185 us
  waiting for transfers between devices  40 us (21%)
  local copies, waits for them, and re-layouts  37.9 us (20%)
  starting transfers between devices  37.1 us (20%)
  blocking collectives  37 us (20%)
  Pallas kernels  30.3 us (16%)
    unnamed x92, local copies, waits for them, and re-layouts  31.6 us
    all_gather x1, blocking collectives, on_device(): all_pictures = lax.all_gather(pictures, 'txt', axis=0, tiled=True)  31.5 us
    ppermute x7, waiting for transfers between devices, swap(): return lax.ppermute(part, axis, [(s, s ^ mask) for s in range(size)])  20.6 us
    pallas_call x1, Pallas kernels, on_device(): kernel_call(functools.partial(text_body, n_txt), (shape(slot_shape, BF16)...  16.3 us
    all_to_all x1, waiting for transfers between devices, on_device(): got_out = lax.all_to_all(out, 'txt', 0, 0, tiled=True)  13.3 us
    all_to_all x1, starting transfers between devices, on_device(): got_out = lax.all_to_all(out, 'txt', 0, 0, tiled=True)  12.9 us
    pallas_call x1, Pallas kernels, on_device(): kernel_call(functools.partial(image_body, n_txt), (shape((local, NEGS, ca...  9.98 us
    ppermute x7, starting transfers between devices, swap(): return lax.ppermute(part, axis, [(s, s ^ mask) for s in range(size)])  9.95 us
  transfers between devices with their start and end apart: 11, of which 3 were waited for; matrix products, arithmetic and copies ran while one was open for 7% of the time, Pallas kernels for 16%

profile of v1, /device:TPU:0, one launch (start us, length us, event | category | flops | bytes accessed | tf_op | source)
XLA Modules:
  0.0 185.1 jit_solution(4901048263849186902)
XLA Ops:
  1.4 1.1 copy.54.cots
  2.5 0.8 shard_map.173
  3.3 1.6 copy.55
  5.0 7.4 %all-to-all-start.1 = ((bf16[8,2,35,768]{3,1,2,0:T(2,128)(2,1)}), bf16[8,2,35,768]{3,1,2,0:T(2,128)(2,1)}, u32[]{:S(2)}, u32[]{:S(2)}) async-start(bf16[8,2,35,768]{3,1,2,0:T(2,128)(2,1)} %copy.55), calls=%async_computation.1 | async-start | bytes 1720320 | tf_op jit(solution)/shard_map/all_to_all | solution.py:323
  12.4 3.0 %collective-permute-start.3 = (bf16[2,35,768]{2,1,0:T(8,128)(2,1)S(1)}, bf16[2,35,768]{2,1,0:T(8,128)(2,1)S(1)}, u32[]{:S(2)}, u32[]{:S(2)}) collective-permute-start(bf16[2,35,768]{2,1,0:T(8,128)(2,1)S(1)} %copy.49.refs_0_), channel_id=1, source_target_pairs={{0,4},{1,5},{2,6},{3,7},{4,0},{5,1},{6,2},{7,3},{8,12},{9,13},{10,... | collective-permute-start | bytes 322568 | tf_op jit(solution)/shard_map/ppermute | solution.py:284
  15.4 1.5 collective-permute-start
  16.8 1.5 collective-permute-start.1
  18.9 20.6 %collective-permute-done.3.refs_4_ = bf16[2,35,768]{2,1,0:T(8,128)(2,1)S(1)} collective-permute-done((bf16[2,35,768]{2,1,0:T(8,128)(2,1)S(1)}, bf16[2,35,768]{2,1,0:T(8,128)(2,1)S(1)}, u32[]{:S(2)}, u32[]{:S(2)}) %collective-permute-start.3) | collective-permute-done | bytes 107552 | tf_op jit(solution)/shard_map/ppermute | solution.py:284
  39.5 1.3 collective-permute-start.4
  41.4 2.2 %collective-permute-start.6 = (bf16[2,35,768]{2,1,0:T(8,128)(2,1)S(1)}, bf16[2,35,768]{2,1,0:T(8,128)(2,1)S(1)}, u32[]{:S(2)}, u32[]{:S(2)}) collective-permute-start(bf16[2,35,768]{2,1,0:T(8,128)(2,1)S(1)} %collective-permute-done.3.refs_4_), channel_id=1, source_target_pairs={{0,3},{1,2},{2,1},{3,0},{4,7},{5,6},{6,5},{7,4},{8,11},{9,10},{10,... | collective-permute-start | bytes 322568 | tf_op jit(solution)/shard_map/ppermute | solution.py:284
  43.6 31.5 %all_gather.9.images = bf16[1024,256]{1,0:T(8,128)(2,1)S(1)} all-gather(bf16[128,256]{1,0:T(8,128)(2,1)S(1)} %copy-done.35), channel_id=1, replica_groups=mesh['img'=4,'txt'=8] {'txt'}, dimensions={0}, use_global_device_ids=true | all-gather | bytes 589824 | tf_op jit(solution)/shard_map/all_gather | solution.py:321
  75.9 0.8 copy.50.refs_8_
  76.9 1.2 copy.52.refs_10_
  78.2 2.5 %shard_map.171 = (f32[8,2,128]{2,1,0:T(2,128)}, f32[2,512]{1,0:T(2,128)S(1)}) custom-call(s32[2]{0:T(128)S(1)} %pad_add_fusion.place, f32[1]{0:T(128)S(6)} %copy.74.softness, bf16[1024,256]{1,0:T(8,128)(2,1)S(1)} %all_gather.9.images, bf16[512,256]{1,0:T(8,128)(2,1)S(1)} %copy-done.31), custom_call_target="tpu_custom_call" | custom-call | flops 536870912 | bytes 1000000 | tf_op jit(solution)/shard_map/pallas_call | solution.py:343
  84.0 1.0 copy-done.12
  85.0 0.9 copy-done.14
  85.9 0.9 copy-done.17
  86.8 0.9 copy-done.20
  87.7 0.9 copy-done.23
  88.6 0.9 copy-done.26
  89.5 0.9 copy-done.29
  90.4 10.0 %shard_map.172 = (bf16[2,4,35,768]{3,2,1,0:T(8,128)(2,1)S(1)}, f32[2,768,256]{2,1,0:T(8,128)S(1)}, f32[2,768,256]{2,1,0:T(8,128)S(1)}, f32[2,1,768]{2,1,0:T(1,12...) custom-call(s32[16,4]{1,0:T(8,128)S(1)} %copy.47.owners, s32[16,4]{1,0:T(8,128)S(1)} %copy.48.slots, ...), custom_call_target="tpu_custom_call" | custom-call | flops 2210611200 | bytes 10000000 | tf_op jit(solution)/shard_map/pallas_call | solution.py:333
  100.4 1.3 copy-done
  101.7 1.1 copy-done.2
  102.9 0.8 copy-done.10
  103.7 3.3 %all-to-all-start = ((f32[8,1,2,128]{3,2,1,0:T(2,128)}), f32[8,1,2,128]{3,2,1,0:T(2,128)S(1)}, u32[]{:S(2)}, u32[]{:S(2)}) async-start(f32[8,1,2,128]{3,2,1,0:T(2,128)} %bitcast.3), calls=%async_computation | async-start | bytes 16384 | tf_op jit(solution)/shard_map/all_to_all | solution.py:382
  107.0 1.4 copy.59.refs_8_
  108.7 1.5 copy-done.1
  110.2 0.9 copy-done.21
  111.1 0.9 copy-done.24
  112.0 0.9 copy-done.27
  112.9 0.9 copy-done.30
  113.8 16.3 %shard_map.174 = (bf16[8,2,35,768]{3,2,1,0:T(8,128)(2,1)S(1)}, bf16[8,2,35,768]{3,2,1,0:T(8,128)(2,1)S(1)}, bf16[2,257,768]{2,1,0:T(8,128)(2,1)S(1)}, bf16[2,257,768]{2,1,0:T(8,128)(2,1)S(1)}) custom-call(s32[16,4]{1,0:T(8,128)S(1)} %copy.64.owners, s32[16,4]{1,0:T(8,128)S(1)} %copy.57.slots, s32[2]{0:T(128)S(1)} %pad_add_fusion.place, ...), custom_call_target="tpu_custom_call" | custom-call | flops 2210611200 | bytes 10000000 | tf_op jit(solution)/shard_map/pallas_call | solution.py:356
  130.1 0.9 copy-done.4
  131.0 0.9 copy-done.6
  131.9 0.9 copy-done.8
  132.8 1.6 copy.62
  134.4 12.9 %all-to-all-start.2 = ((bf16[8,2,35,768]{3,1,2,0:T(2,128)(2,1)}), bf16[8,2,35,768]{3,1,2,0:T(2,128)(2,1)S(1)}, u32[]{:S(2)}, u32[]{:S(2)}) async-start(bf16[8,2,35,768]{3,1,2,0:T(2,128)(2,1)} %copy.62), calls=%async_computation.2 | async-start | bytes 1720320 | tf_op jit(solution)/shard_map/all_to_all | solution.py:379
  147.3 1.6 copy.63
  148.9 13.3 %all-to-all-done.2 = bf16[8,2,35,768]{3,1,2,0:T(2,128)(2,1)S(1)} async-done(((bf16[8,2,35,768]{3,1,2,0:T(2,128)(2,1)}), bf16[8,2,35,768]{3,1,2,0:T(2,128)(2,1)S(1)}, u32[]{:S(2)}, u32[]{:S(2)}) %all-to-all-start.2) | async-done | bytes 860192 | tf_op jit(solution)/shard_map/all_to_all | solution.py:379
  162.1 3.5 %all-to-all-start.3 = ((bf16[8,2,35,768]{3,1,2,0:T(2,128)(2,1)}), bf16[8,2,35,768]{3,1,2,0:T(2,128)(2,1)S(1)}, u32[]{:S(2)}, u32[]{:S(2)}) async-start(bf16[8,2,35,768]{3,1,2,0:T(2,128)(2,1)} %copy.63), calls=%async_computation.3 | async-start | bytes 1720320 | tf_op jit(solution)/shard_map/all_to_all | solution.py:380
  165.7 5.5 %all-gather.1 = f32[4,2,512]{2,1,0:T(2,128)S(1)} all-gather(f32[1,2,512]{2,1,0:T(2,128)S(1)} %bitcast.13), channel_id=2, replica_groups=mesh['img'=4,'txt'=8] {'img'}, dimensions={0}, use_global_device_ids=true | all-gather | bytes 20480 | tf_op jit(solution)/shard_map/all_gather | solution.py:383
  172.4 0.9 copy.67
  173.3 1.5 copy.70
  174.8 1.5 copy.71
  176.4 6.1 %all-to-all-done.3 = bf16[8,2,35,768]{3,1,2,0:T(2,128)(2,1)S(1)} async-done(((bf16[8,2,35,768]{3,1,2,0:T(2,128)(2,1)}), bf16[8,2,35,768]{3,1,2,0:T(2,128)(2,1)S(1)}, u32[]{:S(2)}, u32[]{:S(2)}) %all-to-all-start.3) | async-done | bytes 860192 | tf_op jit(solution)/shard_map/all_to_all | solution.py:380
  182.6 0.8 shard_map.175
  183.5 0.9 copy.68
  (86 shorter events, 8.2 us)
Async XLA Ops:
  3.3 9.1 %copy-start.34 = (bf16[2,35,768]{2,0,1:T(2,128)(2,1)S(1)}, bf16[2,35,768]{2,0,1:T(2,128)(2,1)}, u32[]{:S(2)}) copy-start(bf16[2,35,768]{2,0,1:T(2,128)(2,1)} %param.15) | copy-start | bytes 322564
  3.3 40.3 %copy-start.35 = (bf16[128,256]{1,0:T(8,128)(2,1)S(1)}, bf16[128,256]{1,0:T(8,128)(2,1)}, u32[]{:S(2)}) copy-start(bf16[128,256]{1,0:T(8,128)(2,1)} %param.12) | copy-start | bytes 196612
  5.0 70.8 %copy-start.36 = (s32[16,4]{0,1:T(4,128)S(1)}, s32[16,4]{0,1:T(4,128)}, u32[]{:S(2)}) copy-start(s32[16,4]{0,1:T(4,128)} %param.18) | copy-start | bytes 772
  5.0 70.9 %copy-start.37 = (s32[16,4]{0,1:T(4,128)S(1)}, s32[16,4]{0,1:T(4,128)}, u32[]{:S(2)}) copy-start(s32[16,4]{0,1:T(4,128)} %param.19) | copy-start | bytes 772
  5.0 71.0 %copy-start.33 = (bf16[2,4,35,768]{3,1,2,0:T(4,128)(2,1)S(1)}, bf16[2,4,35,768]{3,1,2,0:T(4,128)(2,1)}, u32[]{:S(2)}) copy-start(bf16[2,4,35,768]{3,1,2,0:T(4,128)(2,1)} %param.22) | copy-start | bytes 1290244
  5.0 71.8 %copy-start.32 = (bf16[2,257,768]{2,0,1:T(2,128)(2,1)S(1)}, bf16[2,257,768]{2,0,1:T(2,128)(2,1)}, u32[]{:S(2)}) copy-start(bf16[2,257,768]{2,0,1:T(2,128)(2,1)} %param.16) | copy-start | bytes 2368516
  5.0 98.7 %all-to-all-start.1 = ((bf16[8,2,35,768]{3,1,2,0:T(2,128)(2,1)}), bf16[8,2,35,768]{3,1,2,0:T(2,128)(2,1)}, u32[]{:S(2)}, u32[]{:S(2)}) async-start(bf16[8,2,35,768]{3,1,2,0:T(2,128)(2,1)} %copy.55), calls=%async_computation.1 | async-start | bytes 1720320 | tf_op jit(solution)/shard_map/all_to_all | solution.py:323
  12.4 27.1 %collective-permute-start.3 = (bf16[2,35,768]{2,1,0:T(8,128)(2,1)S(1)}, bf16[2,35,768]{2,1,0:T(8,128)(2,1)S(1)}, u32[]{:S(2)}, u32[]{:S(2)}) collective-permute-start(bf16[2,35,768]{2,1,0:T(8,128)(2,1)S(1)} %copy.49.refs_0_), channel_id=1, source_target_pairs={{0,4},{1,5},{2,6},{3,7},{4,0},{5,1},{6,2},{7,3},{8,12},{9,13},{10,... | collective-permute-start | bytes 322568 | tf_op jit(solution)/shard_map/ppermute | solution.py:284
  15.4 25.4 %collective-permute-start = (bf16[2,35,768]{2,1,0:T(8,128)(2,1)S(1)}, bf16[2,35,768]{2,1,0:T(8,128)(2,1)S(1)}, u32[]{:S(2)}, u32[]{:S(2)}) collective-permute-start(bf16[2,35,768]{2,1,0:T(8,128)(2,1)S(1)} %copy.49.refs_0_), channel_id=1, source_target_pairs={{0,1},{1,0},{2,3},{3,2},{4,5},{5,4},{6,7},{7,6},{8,9},{9,8},{10,11... | collective-permute-start | bytes 322568 | tf_op jit(solution)/shard_map/ppermute | solution.py:284
  16.8 63.8 %collective-permute-start.1 = (bf16[2,35,768]{2,1,0:T(8,128)(2,1)S(1)}, bf16[2,35,768]{2,1,0:T(8,128)(2,1)S(1)}, u32[]{:S(2)}, u32[]{:S(2)}) collective-permute-start(bf16[2,35,768]{2,1,0:T(8,128)(2,1)S(1)} %copy.49.refs_0_), channel_id=1, source_target_pairs={{0,2},{1,3},{2,0},{3,1},{4,6},{5,7},{6,4},{7,5},{8,10},{9,11},{10,... | collective-permute-start | bytes 322568 | tf_op jit(solution)/shard_map/ppermute | solution.py:284
  18.3 63.0 %collective-permute-start.2 = (bf16[2,35,768]{2,1,0:T(8,128)(2,1)S(1)}, bf16[2,35,768]{2,1,0:T(8,128)(2,1)S(1)}, u32[]{:S(2)}, u32[]{:S(2)}) collective-permute-start(bf16[2,35,768]{2,1,0:T(8,128)(2,1)S(1)} %copy.49.refs_0_), channel_id=1, source_target_pairs={{0,3},{1,2},{2,1},{3,0},{4,7},{5,6},{6,5},{7,4},{8,11},{9,10},{10,... | collective-permute-start | bytes 322568 | tf_op jit(solution)/shard_map/ppermute | solution.py:284
  39.5 42.5 %collective-permute-start.4 = (bf16[2,35,768]{2,1,0:T(8,128)(2,1)S(1)}, bf16[2,35,768]{2,1,0:T(8,128)(2,1)S(1)}, u32[]{:S(2)}, u32[]{:S(2)}) collective-permute-start(bf16[2,35,768]{2,1,0:T(8,128)(2,1)S(1)} %collective-permute-done.3.refs_4_), channel_id=1, source_target_pairs={{0,1},{1,0},{2,3},{3,2},{4,5},{5,4},{6,7},{7,6},{8,9},{9,8},{10,11... | collective-permute-start | bytes 322568 | tf_op jit(solution)/shard_map/ppermute | solution.py:284
  40.8 41.8 %collective-permute-start.5 = (bf16[2,35,768]{2,1,0:T(8,128)(2,1)S(1)}, bf16[2,35,768]{2,1,0:T(8,128)(2,1)S(1)}, u32[]{:S(2)}, u32[]{:S(2)}) collective-permute-start(bf16[2,35,768]{2,1,0:T(8,128)(2,1)S(1)} %collective-permute-done.3.refs_4_), channel_id=1, source_target_pairs={{0,2},{1,3},{2,0},{3,1},{4,6},{5,7},{6,4},{7,5},{8,10},{9,11},{10,... | collective-permute-start | bytes 322568 | tf_op jit(solution)/shard_map/ppermute | solution.py:284
  41.4 41.9 %collective-permute-start.6 = (bf16[2,35,768]{2,1,0:T(8,128)(2,1)S(1)}, bf16[2,35,768]{2,1,0:T(8,128)(2,1)S(1)}, u32[]{:S(2)}, u32[]{:S(2)}) collective-permute-start(bf16[2,35,768]{2,1,0:T(8,128)(2,1)S(1)} %collective-permute-done.3.refs_4_), channel_id=1, source_target_pairs={{0,3},{1,2},{2,1},{3,0},{4,7},{5,6},{6,5},{7,4},{8,11},{9,10},{10,... | collective-permute-start | bytes 322568 | tf_op jit(solution)/shard_map/ppermute | solution.py:284
  76.8 1.3 copy-start.38
  76.8 1.4 copy-start.31
  80.7 0.7 copy-start.16
  82.0 0.7 copy-start.22
  82.6 0.7 copy-start.25
  83.3 0.7 copy-start.28
  84.0 1.0 copy-start.12
  85.0 0.9 copy-start.14
  85.9 0.9 copy-start.17
  86.8 0.9 copy-start.20
  87.7 0.9 copy-start.23
  88.6 0.9 copy-start.26
  89.5 0.9 copy-start.29
  100.4 1.3 copy-start
  101.7 1.2 copy-start.2
  102.9 0.8 copy-start.10
  103.7 30.7 %all-to-all-start = ((f32[8,1,2,128]{3,2,1,0:T(2,128)}), f32[8,1,2,128]{3,2,1,0:T(2,128)S(1)}, u32[]{:S(2)}, u32[]{:S(2)}) async-start(f32[8,1,2,128]{3,2,1,0:T(2,128)} %bitcast.3), calls=%async_computation | async-start | bytes 16384 | tf_op jit(solution)/shard_map/all_to_all | solution.py:382
  107.0 1.7 copy-start.3
  107.0 1.7 copy-start.15
  107.0 1.7 copy-start.18
  108.7 1.5 copy-start.1
  110.2 0.9 copy-start.21
  111.1 0.9 copy-start.24
  112.0 0.9 copy-start.27
  112.9 0.9 copy-start.30
  130.1 0.9 copy-start.4
  131.0 0.9 copy-start.6
  131.9 0.9 copy-start.8
  132.8 14.4 %copy-start.5 = (bf16[8,2,35,768]{3,2,1,0:T(8,128)(2,1)S(1)}, bf16[8,2,35,768]{3,2,1,0:T(8,128)(2,1)}, u32[]{:S(2)}) copy-start(bf16[8,2,35,768]{3,2,1,0:T(8,128)(2,1)} %copy-done.4) | copy-start | bytes 2580484
  134.4 27.7 %all-to-all-start.2 = ((bf16[8,2,35,768]{3,1,2,0:T(2,128)(2,1)}), bf16[8,2,35,768]{3,1,2,0:T(2,128)(2,1)S(1)}, u32[]{:S(2)}, u32[]{:S(2)}) async-start(bf16[8,2,35,768]{3,1,2,0:T(2,128)(2,1)} %copy.62), calls=%async_computation.2 | async-start | bytes 1720320 | tf_op jit(solution)/shard_map/all_to_all | solution.py:379
  147.3 25.2 %copy-start.11 = (bf16[2,4,35,768]{3,2,1,0:T(8,128)(2,1)S(1)}, bf16[2,4,35,768]{3,2,1,0:T(8,128)(2,1)}, u32[]{:S(2)}) copy-start(bf16[2,4,35,768]{3,2,1,0:T(8,128)(2,1)} %copy-done.10) | copy-start | bytes 1290244
  148.9 24.5 %copy-start.9 = (bf16[2,257,768]{2,1,0:T(8,128)(2,1)S(1)}, bf16[2,257,768]{2,1,0:T(8,128)(2,1)}, u32[]{:S(2)}) copy-start(bf16[2,257,768]{2,1,0:T(8,128)(2,1)} %copy-done.8) | copy-start | bytes 2368516
  162.1 20.4 %all-to-all-start.3 = ((bf16[8,2,35,768]{3,1,2,0:T(2,128)(2,1)}), bf16[8,2,35,768]{3,1,2,0:T(2,128)(2,1)S(1)}, u32[]{:S(2)}, u32[]{:S(2)}) async-start(bf16[8,2,35,768]{3,1,2,0:T(2,128)(2,1)} %copy.63), calls=%async_computation.3 | async-start | bytes 1720320 | tf_op jit(solution)/shard_map/all_to_all | solution.py:380
  165.7 9.2 %copy-start.7 = (bf16[2,257,768]{2,1,0:T(8,128)(2,1)S(1)}, bf16[2,257,768]{2,1,0:T(8,128)(2,1)}, u32[]{:S(2)}) copy-start(bf16[2,257,768]{2,1,0:T(8,128)(2,1)} %copy-done.6) | copy-start | bytes 2368516
  (2 other events, 1.3 us)

commit v2 on v1

v2 whole, which is shorter than its diff:
```python
import functools

import jax
import jax.numpy as jnp
from jax import lax
from jax.experimental import pallas as pl
from jax.experimental.pallas import tpu as pltpu
from jax.sharding import PartitionSpec as P

NEGS = 4
EPSILON = 1e-06
LANES = 128
SMEM = pl.BlockSpec(memory_space=pltpu.SMEM)
ANY = pl.BlockSpec(memory_space=pl.ANY)
VMEM = pl.BlockSpec(memory_space=pltpu.VMEM)
F32 = jnp.float32
BF16 = jnp.bfloat16
NT = (((1,), (1,)), ((), ()))
TN = (((0,), (0,)), ((), ()))
NN = (((1,), (0,)), ((), ()))
CHUNK = 3


def kernel_call(body, out_shape, n_smem, n_any, scratch=(), flops=0, nbytes=0, space=ANY, mib=56, **more):
    return pl.pallas_call(
        body,
        out_shape=out_shape,
        in_specs=[SMEM] * n_smem + [space] * n_any,
        out_specs=jax.tree.map(lambda _: space, out_shape),
        scratch_shapes=list(scratch),
        compiler_params=pltpu.CompilerParams(vmem_limit_bytes=mib * 1024 * 1024),
        cost_estimate=pl.CostEstimate(flops=flops, bytes_accessed=nbytes, transcendentals=0),
        **more,
    )


def start_copies(pairs, sems, first=0):
    copies = [pltpu.make_async_copy(a, b, sems.at[first + n]) for n, (a, b) in enumerate(pairs)]
    for copy in copies:
        copy.start()
    return copies


def wait_copies(copies):
    for copy in copies:
        copy.wait()


def dot(a, b, dims):
    return lax.dot_general(a, b, dims, preferred_element_type=F32)


def padded(rows):
    return (rows + 7) // 8 * 8


def tie(value, *others):
    def body(*refs):
        del refs

    return kernel_call(
        body,
        jax.ShapeDtypeStruct(value.shape, value.dtype),
        0,
        1 + len(others),
        mib=1,
        input_output_aliases={0: 0},
    )(value, *others)


def pack_body(queries, pictures, packed):
    captions, caption = queries.shape[:2]
    first, emb = packed.shape[0] - fold_rows(pictures.shape, packed.shape[1]), pictures.shape[1]
    pieces = [queries[row].astype(F32) for row in range(captions)]
    pieces.append(jnp.zeros((first - captions * caption, packed.shape[1]), F32))
    packed[0:first, :] = jnp.concatenate(pieces, axis=0).astype(BF16)
    packed[first:, :] = jnp.zeros((packed.shape[0] - first, packed.shape[1]), BF16)
    for fold, (start, count) in enumerate(folds(pictures.shape, packed.shape[1])):
        packed[first : first + count, fold * emb : (fold + 1) * emb] = pictures[start : start + count]


def fold_rows(shape, width):
    return -(-shape[0] // (width // shape[1] * 16)) * 16


def folds(shape, width):
    step = fold_rows(shape, width)
    return [(start, min(step, shape[0] - start)) for start in range(0, shape[0], step)]


def named(tables, of_captions, row, entry):
    first = 2 * NEGS * of_captions
    return tables[first + entry, row], tables[first + NEGS + entry, row]


def send_body(tables, place, cots, sent):
    rows, caption = cots.shape[0], cots.shape[2]
    for part in range(sent.shape[0]):
        pieces = []
        for row in range(rows):
            at = jnp.int32(0)
            for entry in range(NEGS):
                owner, _ = named(tables, 1, place[0] * rows + row, entry)
                at = jnp.where(owner == part, entry, at)
            pieces.append(cots[row, at].astype(F32))
        pieces.append(jnp.zeros((sent.shape[1] - rows * caption, sent.shape[2]), F32))
        sent[part] = jnp.concatenate(pieces, axis=0).astype(BF16)


def contrast_body(n_parts, rows, place, softness, *refs):
    parts, refs = refs[:n_parts], refs[n_parts:]
    texts, row_out, col_out, held, texts_in, unit_images, unit_texts, row_stats, col_stats, sems = refs
    emb, step = texts_in.shape[1], held.shape[1]
    lines = pl.ds(parts[0].shape[0] - step, step)
    wait_copies(
        start_copies(
            [(texts, texts_in)] + [(parts[n].at[lines], held.at[n]) for n in range(n_parts)], sems
        )
    )

    def unit(source):
        wide = source.astype(F32)
        factor = lax.rsqrt(jnp.sum(wide * wide, axis=-1, keepdims=True) + EPSILON)
        return (wide * factor).astype(BF16)

    unit_texts[...] = unit(texts_in[...])
    for part in range(n_parts):
        first = jnp.bitwise_xor(part, place[0]) * rows
        for fold, (start, count) in enumerate(folds((rows, emb), held.shape[2])):
            at = pl.ds(pl.multiple_of(first + start, 16), count)
            unit_images[at, :] = unit(held[part, 0:count, fold * emb : (fold + 1) * emb])
    undo = 1.0 / softness[0]
    n_images, n_texts = n_parts * rows, texts_in.shape[0]
    first_image, first_text = place[1] * n_images, place[0] * n_texts

    def stats(long, long_first, short, short_first):
        logits = dot(long, short, NT) * undo
        highest = jnp.max(logits, axis=0, keepdims=True)
        total = jnp.sum(jnp.exp(logits - highest), axis=0, keepdims=True)
        on_diag = (lax.broadcasted_iota(jnp.int32, logits.shape, 0) + long_first) == (
            lax.broadcasted_iota(jnp.int32, logits.shape, 1) + short_first
        )
        diag = jnp.sum(jnp.where(on_diag, logits, 0.0), axis=0, keepdims=True)
        return highest + jnp.log(total), diag

    for block in range(n_parts):
        first = block * rows
        found = stats(
            unit_texts[...], first_text, unit_images[first : first + rows, :], first_image + first
        )
        at = 0
        for value in found:
            for _ in range(3):
                piece = value.astype(BF16).astype(F32)
                row_stats[block, :, at : at + rows] = piece
                value = value - piece
                at += rows
    for block in range(n_texts // LANES):
        first = block * LANES
        found = stats(
            unit_images[...], first_image, unit_texts[first : first + LANES, :], first_text + first
        )
        for n, value in enumerate(found):
            col_stats[n : n + 1, first : first + LANES] = value
    wait_copies(start_copies([(row_stats, row_out), (col_stats, col_out)], sems))


def attend(chunks, queries, cots, keys, values, sums):
    half = LANES // 2
    tiles = [slice(n * LANES, (n + 1) * LANES) for n in range(keys.shape[2] // LANES)]
    work = [(chunk, lanes) for chunk in chunks for lanes in tiles]

    def stacked(ref, at, lanes):
        pieces = [ref[n, :, lanes] for n in at]
        pieces.append(jnp.zeros((LANES - len(at) * ref.shape[1], LANES), F32))
        tile = jnp.concatenate(pieces, axis=0)
        low = lax.broadcasted_iota(jnp.int32, tile.shape, 1) < half
        pair = jnp.concatenate([jnp.where(low, tile, 0.0), jnp.where(low, 0.0, tile)], axis=0)
        return pair.astype(BF16)

    def folded(pair):
        return jnp.transpose(jnp.concatenate([pair[:half, :LANES], pair[half:, LANES:]], axis=0))

    q = [stacked(queries, chunk[1], lanes) for chunk, lanes in work]
    logits = [dot(keys[chunk[0], :, lanes], q[n], NT) for n, (chunk, lanes) in enumerate(work)]
    if cots is not None:
        g = [stacked(cots, chunk[2], lanes) for chunk, lanes in work]
        terms = [dot(values[chunk[0], :, lanes], g[n], NT) for n, (chunk, lanes) in enumerate(work)]
    weights = []
    for logit in logits:
        shifted = jnp.exp(logit - jnp.max(logit, axis=0, keepdims=True))
        weights.append(shifted * (1.0 / jnp.sum(shifted, axis=0, keepdims=True)))
    rounded = [weight.astype(BF16) for weight in weights]
    outputs = [
        dot(values[chunk[0], :, lanes], rounded[n], TN) if chunk[3] is not None else None
        for n, (chunk, lanes) in enumerate(work)
    ]
    if cots is not None:
        key_sum, value_sum = sums
        value_terms = [dot(rounded[n], g[n], NN) for n in range(len(work))]
        logit_terms = []
        for weight, term in zip(weights, terms):
            inner = jnp.sum(weight * term, axis=0, keepdims=True)
            logit_terms.append((weight * (term - inner)).astype(BF16))
        q_terms = [dot(keys[chunk[0], :, lanes], logit_terms[n], TN) for n, (chunk, lanes) in enumerate(work)]
        key_terms = [dot(logit_terms[n], q[n], NN) for n in range(len(work))]
        for n, (chunk, lanes) in enumerate(work):
            key_sum[chunk[0], :, lanes] += key_terms[n]
            value_sum[chunk[0], :, lanes] += value_terms[n]
    for n, (chunk, lanes) in enumerate(work):
        if chunk[3] is not None:
            chunk[3](lanes, folded(outputs[n]))
        if chunk[4] is not None:
            chunk[4](lanes, folded(q_terms[n]) * 0.125)


def widen(source, wide, at, scale=1.0):
    caption = source.shape[0]
    wide[at, caption:, :] = jnp.zeros((wide.shape[1] - caption, wide.shape[2]), F32)
    wide[at, 0:caption, :] = source.astype(F32) * scale


def query_copies(parts, held):
    lines = pl.ds(0, held.shape[1])
    return [(part.at[lines], held.at[n]) for n, part in enumerate(parts)]


def widen_block(block, wide, first, captions, caption):
    for row in range(captions):
        wide[first + row, caption:, :] = jnp.zeros((wide.shape[1] - caption, wide.shape[2]), F32)
        wide[first + row, 0:caption, :] = block[row * caption : (row + 1) * caption]


def widen_queries(held, queries, captions, caption):
    n_parts = held.shape[0]
    for part in range(n_parts):
        widen_block(held[part].astype(F32) * 0.125, queries, part * captions, captions, caption)
    if queries.shape[0] > n_parts * captions:
        queries[n_parts * captions] = jnp.zeros(queries.shape[1:], F32)


def find_listed(tables, place, lists, counts, everyone):
    for image in range(counts.shape[0]):
        counts[image] = 0

        def clear(i, _, image=image):
            lists[image, i] = everyone
            return 0

        lax.fori_loop(0, lists.shape[1], clear, 0)

    def find(j, _):
        for entry in range(NEGS):
            owner, image = named(tables, 1, j, entry)

            @pl.when(owner == place[0])
            def _():
                lists[image, counts[image]] = j
                counts[image] = counts[image] + 1

        return 0

    lax.fori_loop(0, everyone, find, 0)


def each_pair_of_chunks(lists, counts, place, captions, everyone, work):
    images = counts.shape[0]
    needed = [(counts[image] + CHUNK - 1) // CHUNK for image in range(images)]

    def pair_step(pair, _):
        chunks = []
        for n in range(2):
            chunk = 2 * pair + n
            image, first, past = jnp.int32(0), jnp.int32(0), jnp.int32(0)
            for later in range(1, images):
                past = past + needed[later - 1]
                image = jnp.where(chunk >= past, later, image)
                first = jnp.where(chunk >= past, past, first)
            j = [lists[image, (chunk - first) * CHUNK + e] for e in range(CHUNK)]
            q_at = [
                jnp.where(
                    n < everyone,
                    jnp.bitwise_xor(n // captions, place[0]) * captions + n % captions,
                    everyone,
                )
                for n in j
            ]
            chunks.append((image, j, q_at))
        work(chunks)
        return 0

    lax.fori_loop(0, (sum(needed) + 1) // 2, pair_step, 0)


def image_body(n_parts, tables, place, *refs):
    parts, refs = refs[:n_parts], refs[n_parts:]
    (cots_in, keys_in, values_in, image_out, image_terms, key_out, value_out, text_out,
     held, queries, cots_held, cots, keys, values, image_outs, terms, sums, outs, blocks,
     lists, counts, sems) = refs
    images = captions = keys.shape[0]
    caption = cots_held.shape[2]
    rows = queries.shape[1]
    everyone = n_parts * captions
    copies = start_copies(
        query_copies(parts, held) + [(cots_in, cots_held), (keys_in, keys), (values_in, values)], sems
    )
    find_listed(tables, place, lists, counts, everyone)
    for total in (*sums, outs):
        total[...] = jnp.zeros_like(total)
    wait_copies(copies)
    widen_queries(held, queries, captions, caption)
    for image in range(images):
        for entry in range(NEGS):
            widen(cots_held[image, entry], cots, image * NEGS + entry)
    for first in range(0, NEGS, CHUNK):
        entries = range(first, min(first + CHUNK, NEGS))
        chunks = []
        for image in range(images):
            at = []
            for entry in entries:
                owner, slot = named(tables, 0, place[0] * images + image, entry)
                at.append(jnp.bitwise_xor(owner, place[0]) * captions + slot)

            def emit(ref, lanes, value, image=image, entries=entries):
                for n, e in enumerate(entries):
                    ref[image, e, :, lanes] = value[n * rows : n * rows + caption].astype(BF16)

            chunks.append(
                (
                    image, at, [image * NEGS + e for e in entries],
                    functools.partial(emit, image_outs), functools.partial(emit, terms),
                )
            )
        attend(chunks, queries, cots, keys, values, sums)
    copies = start_copies(
        [(image_outs, image_out), (terms, image_terms), *zip(sums, (key_out, value_out))], sems
    )

    def work(chunks):
        def emit_out(j, lanes, output):
            for e in range(CHUNK):
                outs[j[e], :, lanes] = output[e * rows : (e + 1) * rows]

        attend(
            [
                (image, q_at, None, functools.partial(emit_out, j), None)
                for image, j, q_at in chunks
            ],
            queries, None, keys, values, None,
        )

    each_pair_of_chunks(lists, counts, place, captions, everyone, work)
    for part in range(n_parts):
        pieces = [outs[part * captions + row, 0:caption, :] for row in range(captions)]
        pieces.append(jnp.zeros((blocks.shape[1] - captions * caption, blocks.shape[2]), F32))
        blocks[part] = jnp.concatenate(pieces, axis=0).astype(BF16)
        copies += start_copies([(blocks.at[part], text_out.at[part])], sems, 4 + part)
    wait_copies(copies)


def text_body(n_parts, tables, place, *refs):
    parts, refs = refs[:n_parts], refs[n_parts:]
    (cots_in, keys_in, values_in, stats_in, terms_in, key_in, value_in, q_out, key_grad, value_grad,
     held, queries, cots_held, cots, keys, values, stats, terms, q_sum, firsts, sums, grads,
     lists, counts, sems) = refs
    images = captions = keys.shape[0]
    caption = terms.shape[2]
    rows = queries.shape[1]
    everyone = n_parts * captions
    copies = start_copies(
        query_copies(parts, held) + [(cots_in, cots_held), (keys_in, keys), (values_in, values)], sems
    )
    later = start_copies(
        [(stats_in, stats), (terms_in, terms), *zip((key_in, value_in), firsts)], sems, len(copies)
    )
    find_listed(tables, place, lists, counts, everyone)
    for total in (*sums, q_sum):
        total[...] = jnp.zeros_like(total)
    wait_copies(copies)
    widen_queries(held, queries, captions, caption)
    for part in range(n_parts):
        widen_block(cots_held[part].astype(F32), cots, part * captions, captions, caption)
    cots[everyone] = jnp.zeros(cots.shape[1:], F32)

    def work(chunks):
        def emit_q(q_at, lanes, term):
            for e in range(CHUNK):
                q_sum[q_at[e], :, lanes] += term[e * rows : (e + 1) * rows].astype(BF16).astype(F32)

        attend(
            [(image, q_at, j, None, functools.partial(emit_q, q_at)) for image, j, q_at in chunks],
            queries, cots, keys, values, sums,
        )

    each_pair_of_chunks(lists, counts, place, captions, everyone, work)
    wait_copies(later)
    for image in range(images):
        for entry in range(NEGS):
            owner, slot = named(tables, 0, place[0] * images + image, entry)
            at = jnp.bitwise_xor(owner, place[0]) * captions + slot
            q_sum[at, 0:caption, :] += terms[image, entry].astype(F32)
    out = []
    for part in range(n_parts):
        first = jnp.bitwise_xor(part, place[0]) * captions
        pieces = [q_sum[first + row, 0:caption, :] for row in range(captions)]
        pieces.append(stats[part])
        pieces.append(jnp.zeros((cots_held.shape[1] - captions * caption - 1, stats.shape[2]), F32))
        cots_held[part] = jnp.concatenate(pieces, axis=0).astype(BF16)
        out += start_copies([(cots_held.at[part], q_out.at[part])], sems, part)
    for n, grad in enumerate((key_grad, value_grad)):
        for image in range(images):
            grads[n][image] = (sums[n][image] + firsts[n][image]).astype(BF16)
        out += start_copies([(grads[n], grad)], sems, n_parts + n)
    wait_copies(out)


def join_body(tables, place, got_out, got_q, cols, pair_out, q_grad, image_loss, text_loss):
    rows, caption = pair_out.shape[0], pair_out.shape[2]
    n_parts = got_q.shape[0]
    for row in range(rows):
        lines = slice(row * caption, (row + 1) * caption)
        for entry in range(NEGS):
            owner, _ = named(tables, 1, place[0] * rows + row, entry)
            block = got_out[owner].astype(F32)
            pair_out[row, entry] = block[lines].astype(BF16)
    total = got_q[0].astype(F32)
    for source in range(1, n_parts):
        total = total + got_q[source].astype(F32)
    for row in range(rows):
        q_grad[row] = total[row * caption : (row + 1) * caption].astype(BF16)

    def joined(parts):
        highest = functools.reduce(jnp.maximum, parts)
        return highest + jnp.log(sum(jnp.exp(part - highest) for part in parts))

    width = image_loss.shape[1]
    line = rows * caption
    lse, diag = [], jnp.zeros(image_loss.shape, F32)
    for source in range(n_parts):
        stats = got_q[source].astype(F32)[line : line + 1]
        pieces = [stats[:, n * width : (n + 1) * width] for n in range(6)]
        lse.append(pieces[0] + pieces[1] + pieces[2])
        diag = diag + (pieces[3] + pieces[4] + pieces[5])
    image_loss[...] = joined(lse) - diag
    n_cols = cols.shape[0]
    text_loss[...] = joined([cols[n, 0:1, :] for n in range(n_cols)]) - sum(
        cols[n, 1:2, :] for n in range(n_cols)
    )


def swap(part, axis, mask):
    return lax.ppermute(part, axis, [(s, s ^ mask) for s in range(lax.axis_size(axis))])


def gathered(block, axis):
    half = lax.axis_size(axis) // 2
    other = swap(block, axis, half)
    near = [block] + [swap(block, axis, mask) for mask in range(1, half)]
    far = [other] + [swap(other, axis, mask) for mask in range(1, half)]
    return near + far


def on_device(
    pictures,
    wordings,
    softness,
    queries,
    keys,
    values,
    img_owner,
    img_slot,
    txt_owner,
    txt_slot,
    img_cots,
    txt_cots,
):
    shape = jax.ShapeDtypeStruct
    vmem = pltpu.VMEM
    dma = lambda n: pltpu.SemaphoreType.DMA((n,))
    n_txt = lax.axis_size("txt")
    place = jnp.stack([lax.axis_index("txt"), lax.axis_index("img")]).astype(jnp.int32)
    local, caption, width = queries.shape
    patches = keys.shape[1]
    rows = padded(caption)
    everyone = n_txt * local
    block_shape = (n_txt, padded(local * caption + 1), width)
    wide_shape = (everyone + 1, rows, width)
    query_rows = -(-local * caption // 16) * 16
    held_shape = (n_txt, query_rows, width)
    pair_flops = 10 * caption * patches * width
    tables = jnp.concatenate([table.T for table in (img_owner, img_slot, txt_owner, txt_slot)], axis=0)
    sums = [vmem(keys.shape, F32), vmem(values.shape, F32)]
    lists = [pltpu.SMEM((local, everyone + 2 * CHUNK), jnp.int32), pltpu.SMEM((local,), jnp.int32)]

    step = fold_rows(pictures.shape, width)
    packed = kernel_call(pack_body, shape((query_rows + step, width), BF16), 0, 2, space=VMEM, mib=8)(
        queries, pictures
    )
    parts = gathered(packed, "txt")
    sent = kernel_call(send_body, shape(block_shape, BF16), 2, 1, space=VMEM, mib=12)(
        tables, place, txt_cots
    )
    ready = parts[1 : n_txt // 2] + parts[n_txt // 2 + 1 :]
    got_cots = lax.all_to_all(tie(sent, *ready, keys, values, img_cots), "txt", 0, 0, tiled=True)

    img_pair_out, image_terms, key_part, value_part, out = kernel_call(
        functools.partial(image_body, n_txt),
        (
            shape(img_cots.shape, BF16),
            shape(img_cots.shape, BF16),
            shape(keys.shape, F32),
            shape(values.shape, F32),
            shape(block_shape, BF16),
        ),
        2,
        n_txt + 3,
        [
            vmem(held_shape, BF16),
            vmem(wide_shape, F32),
            vmem(img_cots.shape, BF16),
            vmem((local * NEGS, rows, width), F32),
            vmem(keys.shape, BF16),
            vmem(values.shape, BF16),
            vmem(img_cots.shape, BF16),
            vmem(img_cots.shape, BF16),
            sums,
            vmem(wide_shape, F32),
            vmem(block_shape, BF16),
            *lists,
            dma(n_txt + 4),
        ],
        flops=6 * local * NEGS * pair_flops,
        nbytes=12_000_000,
    )(tables, place, *parts, img_cots, keys, values)
    got_out = lax.all_to_all(out, "txt", 0, 0, tiled=True)

    image_rows, n_texts, emb = pictures.shape[0], wordings.shape[0], wordings.shape[1]
    stats_shape = (n_txt, 1, 6 * image_rows)
    row_stats, col_stats = kernel_call(
        functools.partial(contrast_body, n_txt, image_rows),
        (shape(stats_shape, F32), shape((2, n_texts), F32)),
        2,
        n_txt + 1,
        [
            vmem((n_txt, step, width), BF16),
            vmem(wordings.shape, BF16),
            vmem((n_txt * image_rows, emb), BF16),
            vmem(wordings.shape, BF16),
            vmem(stats_shape, F32),
            vmem((2, n_texts), F32),
            dma(n_txt + 1),
        ],
        flops=4 * n_txt * image_rows * n_texts * emb,
        nbytes=1_000_000,
    )(place, softness, *parts, wordings)
    got_cols = lax.all_gather(col_stats, "img", axis=0)

    q_out, key_grad, value_grad = kernel_call(
        functools.partial(text_body, n_txt),
        (shape(block_shape, BF16), shape(keys.shape, BF16), shape(values.shape, BF16)),
        2,
        n_txt + 7,
        [
            vmem(held_shape, BF16),
            vmem(wide_shape, F32),
            vmem(block_shape, BF16),
            vmem(wide_shape, F32),
            vmem(keys.shape, BF16),
            vmem(values.shape, BF16),
            vmem(stats_shape, F32),
            vmem(img_cots.shape, BF16),
            vmem(wide_shape, F32),
            sums,
            sums,
            [vmem(keys.shape, BF16), vmem(values.shape, BF16)],
            *lists,
            dma(n_txt + 7),
        ],
        flops=4 * local * NEGS * pair_flops,
        nbytes=10_000_000,
    )(tables, place, *parts, got_cots, keys, values, row_stats, image_terms, key_part, value_part)
    got_q = lax.all_to_all(q_out, "txt", 0, 0, tiled=True)

    txt_pair_out, query_grad, image_loss, text_loss = kernel_call(
        join_body,
        (
            shape(txt_cots.shape, BF16),
            shape(queries.shape, BF16),
            shape((1, image_rows), F32),
            shape((1, n_texts), F32),
        ),
        2,
        3,
        space=VMEM,
        mib=16,
    )(tables, place, got_out, got_q, got_cols)
    return (
        image_loss.reshape(-1),
        text_loss.reshape(-1),
        img_pair_out,
        txt_pair_out,
        query_grad,
        key_grad,
        value_grad,
    )


def solution(mesh):
    every = ("img", "txt")
    three, four = P(every, None, None), P(every, None, None, None)
    table = P("img", None)
    return jax.shard_map(
        on_device,
        mesh=mesh,
        in_specs=(P(every, None), P("txt", None), P(), three, three, three)
        + (table, table, table, table, four, four),
        out_specs=(P(every), P("txt"), four, four, three, three, three),
        check_vma=False,
    )
```

time: 189 us -> 113 us (0.60); the launches traced: 185 us -> 112 us
  blocking collectives: 37 us -> 5.3 us
  local copies, waits for them, and re-layouts: 37.9 us -> 10.5 us
  starting transfers between devices: 37.1 us -> 23 us
  Pallas kernels: 30.3 us -> 34.1 us
  waiting for transfers between devices: 40 us -> 37.4 us
    all_gather x1 -> x0, blocking collectives: 31.5 us -> none  [on_device(): all_pictures = lax.all_gather(pictures, 'txt', axis=0, tiled=True)]
    unnamed x92 -> x66, local copies, waits for them, and re-layouts: 31.6 us -> 10.5 us
    all_to_all x1, starting transfers between devices: 12.9 us -> 3.73 us  [on_device(): got_out = lax.all_to_all(out, 'txt', 0, 0, tiled=True)]
    ppermute x7, waiting for transfers between devices: 20.6 us -> 11.8 us  [swap(): lax.ppermute(part, axis, [(s, s ^ mask) for s in range(lax.axis_size(axis...]
    all_to_all x1, waiting for transfers between devices: 13.3 us -> 4.95 us  [on_device(): got_out = lax.all_to_all(out, 'txt', 0, 0, tiled=True)]
    all_to_all x2 -> x1, waiting for transfers between devices: 0.01 us -> 7.63 us  [on_device(): lax.all_to_all(tie(sent, *ready, keys, values, img_cots), 'txt', 0, 0, ti...]
    all_to_all x1, waiting for transfers between devices: 6.1 us -> 13.1 us  [on_device(): got_q = lax.all_to_all(q_out, 'txt', 0, 0, tiled=True)]
    all_to_all x2 -> x1, starting transfers between devices: 10.7 us -> 4.65 us  [on_device(): lax.all_to_all(tie(sent, *ready, keys, values, img_cots), 'txt', 0, 0, ti...]
  transfers between devices with their start and end apart: 11 -> 10, of which waited for: 3 -> 8; matrix products, arithmetic and copies ran while one was open for 7% -> 5% of each run, Pallas kernels for 16% -> 29%
where the time goes in v2:
time: 113 us; the launch traced here: 112 us
  waiting for transfers between devices  37.4 us (33%)
  Pallas kernels  34.1 us (30%)
  starting transfers between devices  23 us (20%)
  local copies, waits for them, and re-layouts  10.5 us (9%)
  blocking collectives  5.3 us (5%)
  between operations  1.63 us (1%)
    pallas_call x1, Pallas kernels, on_device(): kernel_call(functools.partial(image_body, n_txt), (shape(img_cots.shape,...  14.4 us
    all_to_all x1, waiting for transfers between devices, on_device(): got_q = lax.all_to_all(q_out, 'txt', 0, 0, tiled=True)  13.1 us
    pallas_call x1, Pallas kernels, on_device(): kernel_call(functools.partial(text_body, n_txt), (shape(block_shape, BF16...  12 us
    ppermute x7, waiting for transfers between devices, swap(): lax.ppermute(part, axis, [(s, s ^ mask) for s in range(lax.axis_size(axis...  11.8 us
    ppermute x7, starting transfers between devices, swap(): lax.ppermute(part, axis, [(s, s ^ mask) for s in range(lax.axis_size(axis...  11.1 us
    unnamed x66, local copies, waits for them, and re-layouts  10.5 us
    all_to_all x1, waiting for transfers between devices, on_device(): lax.all_to_all(tie(sent, *ready, keys, values, img_cots), 'txt', 0, 0, ti...  7.63 us
    all_gather x1, blocking collectives, on_device(): got_cols = lax.all_gather(col_stats, 'img', axis=0)  5.3 us
  transfers between devices with their start and end apart: 10, of which 8 were waited for; matrix products, arithmetic and copies ran while one was open for 5% of the time, Pallas kernels for 29%

profile of v2, /device:TPU:0, one launch (start us, length us, event | category | flops | bytes accessed | tf_op | source)
XLA Modules:
  0.0 112.0 jit_solution(11858117407807885524)
XLA Ops:
  0.6 0.9 copy.35.queries
  1.5 0.0 copy-start.12
  1.6 0.8 copy-done.12
  2.4 0.0 copy-start.9
  2.4 0.0 copy-start.20
  2.4 4.1 %collective-permute-start.3 = (bf16[128,768]{1,0:T(8,128)(2,1)S(1)}, bf16[128,768]{1,0:T(8,128)(2,1)S(1)}, u32[]{:S(2)}, u32[]{:S(2)}) collective-permute-start(bf16[128,768]{1,0:T(8,128)(2,1)S(1)} %shard_map.171.refs_0_), channel_id=1, source_target_pairs={{0,4},{1,5},{2,6},{3,7},{4,0},{5,1},{6,2},{7,3},{8,12},{9,13},{10,... | collective-permute-start | bytes 589832 | tf_op jit(solution)/shard_map/ppermute | solution.py:452
  6.5 1.5 %collective-permute-start = (bf16[128,768]{1,0:T(8,128)(2,1)S(1)}, bf16[128,768]{1,0:T(8,128)(2,1)S(1)}, u32[]{:S(2)}, u32[]{:S(2)}) collective-permute-start(bf16[128,768]{1,0:T(8,128)(2,1)S(1)} %shard_map.171.refs_0_), channel_id=1, source_target_pairs={{0,1},{1,0},{2,3},{3,2},{4,5},{5,4},{6,7},{7,6},{8,9},{9,8},{10,11... | collective-permute-start | bytes 589832 | tf_op jit(solution)/shard_map/ppermute | solution.py:452
  8.0 1.6 %collective-permute-start.1 = (bf16[128,768]{1,0:T(8,128)(2,1)S(1)}, bf16[128,768]{1,0:T(8,128)(2,1)S(1)}, u32[]{:S(2)}, u32[]{:S(2)}) collective-permute-start(bf16[128,768]{1,0:T(8,128)(2,1)S(1)} %shard_map.171.refs_0_), channel_id=1, source_target_pairs={{0,2},{1,3},{2,0},{3,1},{4,6},{5,7},{6,4},{7,5},{8,10},{9,11},{10,... | collective-permute-start | bytes 589832 | tf_op jit(solution)/shard_map/ppermute | solution.py:452
  9.6 0.4 collective-permute-start.2
  10.0 1.2 %copy.37.refs_9_.refs_7_ = bf16[2,257,768]{2,1,0:T(8,128)(2,1)S(1)} copy(bf16[2,257,768]{2,0,1:T(2,128)(2,1)} %param.16) | data formatting | bytes 1579008 | tf_op args[4]
  11.3 0.0 copy-start.21
  11.3 0.0 copy-start.23
  11.3 0.0 copy-start.24
  11.3 0.0 copy-start.25
  11.3 0.0 copy-start.26
  11.3 0.1 copy.38.refs_10_.refs_8_
  11.4 0.1 copy.36.refs_8_.refs_9_
  11.5 1.1 copy-done.21
  12.6 0.1 copy.39.cots
  12.6 3.1 %collective-permute-done.3.refs_4_ = bf16[128,768]{1,0:T(8,128)(2,1)S(1)} collective-permute-done((bf16[128,768]{1,0:T(8,128)(2,1)S(1)}, bf16[128,768]{1,0:T(8,128)(2,1)S(1)}, u32[]{:S(2)}, u32[]{:S(2)}) %collective-permute-start.3) | collective-permute-done | bytes 196640 | tf_op jit(solution)/shard_map/ppermute | solution.py:452
  15.8 1.5 %collective-permute-start.4 = (bf16[128,768]{1,0:T(8,128)(2,1)S(1)}, bf16[128,768]{1,0:T(8,128)(2,1)S(1)}, u32[]{:S(2)}, u32[]{:S(2)}) collective-permute-start(bf16[128,768]{1,0:T(8,128)(2,1)S(1)} %collective-permute-done.3.refs_4_), channel_id=1, source_target_pairs={{0,1},{1,0},{2,3},{3,2},{4,5},{5,4},{6,7},{7,6},{8,9},{9,8},{10,11... | collective-permute-start | bytes 589832 | tf_op jit(solution)/shard_map/ppermute | solution.py:452
  17.3 0.6 collective-permute-start.5
  17.9 1.3 %collective-permute-start.6 = (bf16[128,768]{1,0:T(8,128)(2,1)S(1)}, bf16[128,768]{1,0:T(8,128)(2,1)S(1)}, u32[]{:S(2)}, u32[]{:S(2)}) collective-permute-start(bf16[128,768]{1,0:T(8,128)(2,1)S(1)} %collective-permute-done.3.refs_4_), channel_id=1, source_target_pairs={{0,3},{1,2},{2,1},{3,0},{4,7},{5,6},{6,5},{7,4},{8,11},{9,10},{10,... | collective-permute-start | bytes 589832 | tf_op jit(solution)/shard_map/ppermute | solution.py:452
  19.3 0.1 pad_add_fusion.1.place
  19.4 1.8 %shard_map.173.refs_0_ = bf16[8,72,768]{2,1,0:T(8,128)(2,1)} custom-call(s32[16,16]{1,0:T(8,128)S(1)} %pad_add_fusion.tables, s32[2]{0:T(128)S(1)} %pad_add_fusion.1.place, bf16[2,4,35,768]{3,2,1,0:T(8,128)(2,1)S(1)} %copy.39.cots), custom_call_target="tpu_custom_call" | custom-call | tf_op jit(solution)/shard_map/pallas_call | solution.py:500
  21.2 2.0 %collective-permute-done.2.refs_3_ = bf16[128,768]{1,0:T(8,128)(2,1)S(1)} collective-permute-done((bf16[128,768]{1,0:T(8,128)(2,1)S(1)}, bf16[128,768]{1,0:T(8,128)(2,1)S(1)}, u32[]{:S(2)}, u32[]{:S(2)}) %collective-permute-start.2) | collective-permute-done | bytes 196640 | tf_op jit(solution)/shard_map/ppermute | solution.py:452
  23.2 2.8 %collective-permute-done.4.refs_5_.refs_4_ = bf16[128,768]{1,0:T(8,128)(2,1)S(1)} collective-permute-done((bf16[128,768]{1,0:T(8,128)(2,1)S(1)}, bf16[128,768]{1,0:T(8,128)(2,1)S(1)}, u32[]{:S(2)}, u32[]{:S(2)}) %collective-permute-start.4) | collective-permute-done | bytes 196640 | tf_op jit(solution)/shard_map/ppermute | solution.py:452
  26.0 1.3 %collective-permute-done.5.refs_6_.refs_5_ = bf16[128,768]{1,0:T(8,128)(2,1)S(1)} collective-permute-done((bf16[128,768]{1,0:T(8,128)(2,1)S(1)}, bf16[128,768]{1,0:T(8,128)(2,1)S(1)}, u32[]{:S(2)}, u32[]{:S(2)}) %collective-permute-start.5) | collective-permute-done | bytes 196640 | tf_op jit(solution)/shard_map/ppermute | solution.py:452
  27.3 2.5 %collective-permute-done.6.refs_7_.refs_6_ = bf16[128,768]{1,0:T(8,128)(2,1)S(1)} collective-permute-done((bf16[128,768]{1,0:T(8,128)(2,1)S(1)}, bf16[128,768]{1,0:T(8,128)(2,1)S(1)}, u32[]{:S(2)}, u32[]{:S(2)}) %collective-permute-start.6) | collective-permute-done | bytes 196640 | tf_op jit(solution)/shard_map/ppermute | solution.py:452
  29.9 0.6 copy-done.8
  30.5 4.7 %all-to-all-start.1 = ((bf16[8,72,768]{2,1,0:T(8,128)(2,1)}), bf16[8,72,768]{2,1,0:T(8,128)(2,1)S(1)}, u32[]{:S(2)}, u32[]{:S(2)}) async-start(bf16[8,72,768]{2,1,0:T(8,128)(2,1)} %shard_map.174), calls=%async_computation.1 | async-start | bytes 1769472 | tf_op jit(solution)/shard_map/all_to_all | solution.py:504
  35.2 14.4 %shard_map.172 = (bf16[2,4,35,768]{3,2,1,0:T(8,128)(2,1)}, bf16[2,4,35,768]{3,2,1,0:T(8,128)(2,1)}, f32[2,257,768]{2,1,0:T(8,128)}, f32[2,257,768]{2,1,0:T(8,128)}, bf16[8,72,768]{2,1,0:T(8,128)(2,1)}) custom-call(s32[16,16]{1,0:T(8,128)} %copy-done.10, s32[2]{0:T(128)} %copy-done.13, bf16[128,768]{1,0:T(8,128)(2,1)} %copy-done.9, ...), custom_call_target="tpu_custom_call" | custom-call | flops 3315916800 | bytes 12000000 | tf_op jit(solution)/shard_map/pallas_call | solution.py:506
  49.6 7.6 %all-to-all-done.1.refs_8_ = bf16[8,72,768]{2,1,0:T(8,128)(2,1)S(1)} async-done(((bf16[8,72,768]{2,1,0:T(8,128)(2,1)}), bf16[8,72,768]{2,1,0:T(8,128)(2,1)S(1)}, u32[]{:S(2)}, u32[]{:S(2)}) %all-to-all-start.1) | async-done | bytes 884768 | tf_op jit(solution)/shard_map/all_to_all | solution.py:504
  57.2 3.7 %all-to-all-start = ((bf16[8,72,768]{2,1,0:T(8,128)(2,1)}), bf16[8,72,768]{2,1,0:T(8,128)(2,1)S(1)}, u32[]{:S(2)}, u32[]{:S(2)}) async-start(bf16[8,72,768]{2,1,0:T(8,128)(2,1)} %get-tuple-element.21), calls=%async_computation | async-start | bytes 1769472 | tf_op jit(solution)/shard_map/all_to_all | solution.py:535
  61.6 4.6 %shard_map.175 = (f32[8,1,768]{2,1,0:T(1,128)}, f32[2,512]{1,0:T(2,128)}) custom-call(s32[2]{0:T(128)} %copy-done.13, f32[1]{0:T(128)S(6)} %copy.51.softness, bf16[128,768]{1,0:T(8,128)(2,1)} %copy-done.9, bf16[128,768]{1,0:T(8,128)(2,1)} %copy-done.3, bf16[128,768]{1,0:T(8,128)(2,1)} %copy-done.4, bf16[128,768]{1,0:T(8,128)(2,1)} %copy-done.5, ...), custom_call_target="tpu_custom_call" | custom-call | flops 536870912 | bytes 1000000 | tf_op jit(solution)/shard_map/pallas_call | solution.py:539
  66.1 12.0 %shard_map.176 = (bf16[8,72,768]{2,1,0:T(8,128)(2,1)}, bf16[2,257,768]{2,1,0:T(8,128)(2,1)}, bf16[2,257,768]{2,1,0:T(8,128)(2,1)}) custom-call(s32[16,16]{1,0:T(8,128)} %copy-done.10, s32[2]{0:T(128)} %copy-done.13, bf16[128,768]{1,0:T(8,128)(2,1)} %copy-done.9, bf16[128,768]{1,0:T(8,128)(2,1)} %copy-done.3, bf16[128,768]{1,0:T(8,128)(2,1)} %copy-done.4, ...), custom_call_target="tpu_custom_call" | custom-call | flops 2210611200 | bytes 10000000 | tf_op jit(solution)/shard_map/pallas_call | solution.py:558
  78.2 0.0 copy-start.19
  78.2 0.0 copy-start.22
  78.2 4.9 %all-to-all-done.got_out = bf16[8,72,768]{2,1,0:T(8,128)(2,1)S(1)} async-done(((bf16[8,72,768]{2,1,0:T(8,128)(2,1)}), bf16[8,72,768]{2,1,0:T(8,128)(2,1)S(1)}, u32[]{:S(2)}, u32[]{:S(2)}) %all-to-all-start) | async-done | bytes 884768 | tf_op jit(solution)/shard_map/all_to_all | solution.py:535
  83.2 3.6 %all-to-all-start.2 = ((bf16[8,72,768]{2,1,0:T(8,128)(2,1)}), bf16[8,72,768]{2,1,0:T(8,128)(2,1)S(1)}, u32[]{:S(2)}, u32[]{:S(2)}) async-start(bf16[8,72,768]{2,1,0:T(8,128)(2,1)} %get-tuple-element.26), calls=%async_computation.2 | async-start | bytes 1769472 | tf_op jit(solution)/shard_map/all_to_all | solution.py:582
  86.7 0.9 copy.45
  87.7 5.3 %all-gather.1.cols = f32[4,2,512]{2,1,0:T(2,128)S(1)} all-gather(f32[1,2,512]{2,1,0:T(2,128)S(1)} %bitcast.9), channel_id=2, replica_groups=mesh['img'=4,'txt'=8] {'img'}, dimensions={0}, use_global_device_ids=true | all-gather | bytes 20480 | tf_op jit(solution)/shard_map/all_gather | solution.py:556
  93.0 1.5 %copy.48 = bf16[2,257,768]{2,0,1:T(2,128)(2,1)} copy(bf16[2,257,768]{2,1,0:T(8,128)(2,1)S(1)} %copy-done.17) | data formatting | bytes 1579008
  94.5 1.5 %copy.49 = bf16[2,257,768]{2,0,1:T(2,128)(2,1)} copy(bf16[2,257,768]{2,1,0:T(8,128)(2,1)S(1)} %copy-done.16) | data formatting | bytes 1579008
  96.0 13.1 %all-to-all-done.2.got_q = bf16[8,72,768]{2,1,0:T(8,128)(2,1)S(1)} async-done(((bf16[8,72,768]{2,1,0:T(8,128)(2,1)}), bf16[8,72,768]{2,1,0:T(8,128)(2,1)S(1)}, u32[]{:S(2)}, u32[]{:S(2)}) %all-to-all-start.2) | async-done | bytes 884768 | tf_op jit(solution)/shard_map/all_to_all | solution.py:582
  109.1 1.3 %shard_map.177 = (bf16[2,4,35,768]{3,2,1,0:T(8,128)(2,1)S(1)}, bf16[2,35,768]{2,1,0:T(8,128)(2,1)S(1)}, f32[1,128]{1,0:T(1,128)}, f32[1,512]{1,0:T(1,128)}) custom-call(s32[16,16]{1,0:T(8,128)S(1)} %copy-done.11, s32[2]{0:T(128)S(1)} %copy-done.14, bf16[8,72,768]{2,1,0:T(8,128)(2,1)S(1)} %all-to-all-done.got_out, ...), custom_call_target="tpu_custom_call" | custom-call | tf_op jit(solution)/shard_map/pallas_call | solution.py:584
  110.4 0.9 copy.46
  111.3 0.7 copy.47
  (48 shorter events, 0.1 us)
Async XLA Ops:
  1.5 0.8 copy-start.12
  2.4 8.9 %copy-start.18 = (bf16[2,257,768]{2,0,1:T(2,128)(2,1)S(1)}, bf16[2,257,768]{2,0,1:T(2,128)(2,1)}, u32[]{:S(2)}) copy-start(bf16[2,257,768]{2,0,1:T(2,128)(2,1)} %param.17) | copy-start | bytes 2368516
  2.4 9.1 %copy-start.9 = (bf16[128,768]{1,0:T(8,128)(2,1)}, bf16[128,768]{1,0:T(8,128)(2,1)S(1)}, u32[]{:S(2)}) copy-start(bf16[128,768]{1,0:T(8,128)(2,1)S(1)} %shard_map.171.refs_0_) | copy-start | bytes 589828
  2.4 9.0 %copy-start.20 = (bf16[2,4,35,768]{3,1,2,0:T(4,128)(2,1)S(1)}, bf16[2,4,35,768]{3,1,2,0:T(4,128)(2,1)}, u32[]{:S(2)}) copy-start(bf16[2,4,35,768]{3,1,2,0:T(4,128)(2,1)} %param.22) | copy-start | bytes 1290244
  2.4 13.3 %collective-permute-start.3 = (bf16[128,768]{1,0:T(8,128)(2,1)S(1)}, bf16[128,768]{1,0:T(8,128)(2,1)S(1)}, u32[]{:S(2)}, u32[]{:S(2)}) collective-permute-start(bf16[128,768]{1,0:T(8,128)(2,1)S(1)} %shard_map.171.refs_0_), channel_id=1, source_target_pairs={{0,4},{1,5},{2,6},{3,7},{4,0},{5,1},{6,2},{7,3},{8,12},{9,13},{10,... | collective-permute-start | bytes 589832 | tf_op jit(solution)/shard_map/ppermute | solution.py:452
  6.5 11.4 %collective-permute-start = (bf16[128,768]{1,0:T(8,128)(2,1)S(1)}, bf16[128,768]{1,0:T(8,128)(2,1)S(1)}, u32[]{:S(2)}, u32[]{:S(2)}) collective-permute-start(bf16[128,768]{1,0:T(8,128)(2,1)S(1)} %shard_map.171.refs_0_), channel_id=1, source_target_pairs={{0,1},{1,0},{2,3},{3,2},{4,5},{5,4},{6,7},{7,6},{8,9},{9,8},{10,11... | collective-permute-start | bytes 589832 | tf_op jit(solution)/shard_map/ppermute | solution.py:452
  8.0 13.1 %collective-permute-start.1 = (bf16[128,768]{1,0:T(8,128)(2,1)S(1)}, bf16[128,768]{1,0:T(8,128)(2,1)S(1)}, u32[]{:S(2)}, u32[]{:S(2)}) collective-permute-start(bf16[128,768]{1,0:T(8,128)(2,1)S(1)} %shard_map.171.refs_0_), channel_id=1, source_target_pairs={{0,2},{1,3},{2,0},{3,1},{4,6},{5,7},{6,4},{7,5},{8,10},{9,11},{10,... | collective-permute-start | bytes 589832 | tf_op jit(solution)/shard_map/ppermute | solution.py:452
  9.6 13.5 %collective-permute-start.2 = (bf16[128,768]{1,0:T(8,128)(2,1)S(1)}, bf16[128,768]{1,0:T(8,128)(2,1)S(1)}, u32[]{:S(2)}, u32[]{:S(2)}) collective-permute-start(bf16[128,768]{1,0:T(8,128)(2,1)S(1)} %shard_map.171.refs_0_), channel_id=1, source_target_pairs={{0,3},{1,2},{2,1},{3,0},{4,7},{5,6},{6,5},{7,4},{8,11},{9,10},{10,... | collective-permute-start | bytes 589832 | tf_op jit(solution)/shard_map/ppermute | solution.py:452
  11.3 18.6 %copy-start = (bf16[2,257,768]{2,1,0:T(8,128)(2,1)}, bf16[2,257,768]{2,1,0:T(8,128)(2,1)S(1)}, u32[]{:S(2)}) copy-start(bf16[2,257,768]{2,1,0:T(8,128)(2,1)S(1)} %copy.37.refs_9_.refs_7_) | copy-start | bytes 2368516
  11.3 1.3 %copy-start.21 = (bf16[2,4,35,768]{3,1,2,0:T(4,128)(2,1)S(1)}, bf16[2,4,35,768]{3,1,2,0:T(4,128)(2,1)}, u32[]{:S(2)}) copy-start(bf16[2,4,35,768]{3,1,2,0:T(4,128)(2,1)} %param.23) | copy-start | bytes 1290244
  11.3 8.1 %copy-start.23 = (s32[16,4]{0,1:T(4,128)S(1)}, s32[16,4]{0,1:T(4,128)}, u32[]{:S(2)}) copy-start(s32[16,4]{0,1:T(4,128)} %param.21) | copy-start | bytes 772
  11.3 8.0 %copy-start.24 = (s32[16,4]{0,1:T(4,128)S(1)}, s32[16,4]{0,1:T(4,128)}, u32[]{:S(2)}) copy-start(s32[16,4]{0,1:T(4,128)} %param.20) | copy-start | bytes 772
  11.3 8.0 %copy-start.25 = (s32[16,4]{0,1:T(4,128)S(1)}, s32[16,4]{0,1:T(4,128)}, u32[]{:S(2)}) copy-start(s32[16,4]{0,1:T(4,128)} %param.19) | copy-start | bytes 772
  11.3 8.0 %copy-start.26 = (s32[16,4]{0,1:T(4,128)S(1)}, s32[16,4]{0,1:T(4,128)}, u32[]{:S(2)}) copy-start(s32[16,4]{0,1:T(4,128)} %param.18) | copy-start | bytes 772
  11.4 18.4 %copy-start.1 = (bf16[2,257,768]{2,1,0:T(8,128)(2,1)}, bf16[2,257,768]{2,1,0:T(8,128)(2,1)S(1)}, u32[]{:S(2)}) copy-start(bf16[2,257,768]{2,1,0:T(8,128)(2,1)S(1)} %copy.38.refs_10_.refs_8_) | copy-start | bytes 2368516
  12.6 17.3 %copy-start.2 = (bf16[2,4,35,768]{3,2,1,0:T(8,128)(2,1)}, bf16[2,4,35,768]{3,2,1,0:T(8,128)(2,1)S(1)}, u32[]{:S(2)}) copy-start(bf16[2,4,35,768]{3,2,1,0:T(8,128)(2,1)S(1)} %copy.36.refs_8_.refs_9_) | copy-start | bytes 1290244
  15.8 14.1 %copy-start.27 = (bf16[128,768]{1,0:T(8,128)(2,1)}, bf16[128,768]{1,0:T(8,128)(2,1)S(1)}, u32[]{:S(2)}) copy-start(bf16[128,768]{1,0:T(8,128)(2,1)S(1)} %collective-permute-done.3.refs_4_) | copy-start | bytes 589828
  15.8 10.2 %collective-permute-start.4 = (bf16[128,768]{1,0:T(8,128)(2,1)S(1)}, bf16[128,768]{1,0:T(8,128)(2,1)S(1)}, u32[]{:S(2)}, u32[]{:S(2)}) collective-permute-start(bf16[128,768]{1,0:T(8,128)(2,1)S(1)} %collective-permute-done.3.refs_4_), channel_id=1, source_target_pairs={{0,1},{1,0},{2,3},{3,2},{4,5},{5,4},{6,7},{7,6},{8,9},{9,8},{10,11... | collective-permute-start | bytes 589832 | tf_op jit(solution)/shard_map/ppermute | solution.py:452
  17.3 10.0 %collective-permute-start.5 = (bf16[128,768]{1,0:T(8,128)(2,1)S(1)}, bf16[128,768]{1,0:T(8,128)(2,1)S(1)}, u32[]{:S(2)}, u32[]{:S(2)}) collective-permute-start(bf16[128,768]{1,0:T(8,128)(2,1)S(1)} %collective-permute-done.3.refs_4_), channel_id=1, source_target_pairs={{0,2},{1,3},{2,0},{3,1},{4,6},{5,7},{6,4},{7,5},{8,10},{9,11},{10,... | collective-permute-start | bytes 589832 | tf_op jit(solution)/shard_map/ppermute | solution.py:452
  17.9 11.9 %copy-start.3 = (bf16[128,768]{1,0:T(8,128)(2,1)}, bf16[128,768]{1,0:T(8,128)(2,1)S(1)}, u32[]{:S(2)}) copy-start(bf16[128,768]{1,0:T(8,128)(2,1)S(1)} %collective-permute-done.refs_1_) | copy-start | bytes 589828
  17.9 11.9 %collective-permute-start.6 = (bf16[128,768]{1,0:T(8,128)(2,1)S(1)}, bf16[128,768]{1,0:T(8,128)(2,1)S(1)}, u32[]{:S(2)}, u32[]{:S(2)}) collective-permute-start(bf16[128,768]{1,0:T(8,128)(2,1)S(1)} %collective-permute-done.3.refs_4_), channel_id=1, source_target_pairs={{0,3},{1,2},{2,1},{3,0},{4,7},{5,6},{6,5},{7,4},{8,11},{9,10},{10,... | collective-permute-start | bytes 589832 | tf_op jit(solution)/shard_map/ppermute | solution.py:452
  19.3 10.5 %copy-start.13 = (s32[2]{0:T(128)}, s32[2]{0:T(128)S(1)}, u32[]{:S(2)}) copy-start(s32[2]{0:T(128)S(1)} %pad_add_fusion.1.place) | copy-start | bytes 28
  19.4 10.5 %copy-start.10 = (s32[16,16]{1,0:T(8,128)}, s32[16,16]{1,0:T(8,128)S(1)}, u32[]{:S(2)}) copy-start(s32[16,16]{1,0:T(8,128)S(1)} %pad_add_fusion.tables) | copy-start | bytes 3076
  21.2 8.7 %copy-start.4 = (bf16[128,768]{1,0:T(8,128)(2,1)}, bf16[128,768]{1,0:T(8,128)(2,1)S(1)}, u32[]{:S(2)}) copy-start(bf16[128,768]{1,0:T(8,128)(2,1)S(1)} %collective-permute-done.1.refs_2_) | copy-start | bytes 589828
  23.2 6.7 %copy-start.5 = (bf16[128,768]{1,0:T(8,128)(2,1)}, bf16[128,768]{1,0:T(8,128)(2,1)S(1)}, u32[]{:S(2)}) copy-start(bf16[128,768]{1,0:T(8,128)(2,1)S(1)} %collective-permute-done.2.refs_3_) | copy-start | bytes 589828
  26.0 3.9 %copy-start.6 = (bf16[128,768]{1,0:T(8,128)(2,1)}, bf16[128,768]{1,0:T(8,128)(2,1)S(1)}, u32[]{:S(2)}) copy-start(bf16[128,768]{1,0:T(8,128)(2,1)S(1)} %collective-permute-done.4.refs_5_.refs_4_) | copy-start | bytes 589828
  27.3 2.6 %copy-start.7 = (bf16[128,768]{1,0:T(8,128)(2,1)}, bf16[128,768]{1,0:T(8,128)(2,1)S(1)}, u32[]{:S(2)}) copy-start(bf16[128,768]{1,0:T(8,128)(2,1)S(1)} %collective-permute-done.5.refs_6_.refs_5_) | copy-start | bytes 589828
  29.8 0.7 copy-start.8
  30.5 26.7 %all-to-all-start.1 = ((bf16[8,72,768]{2,1,0:T(8,128)(2,1)}), bf16[8,72,768]{2,1,0:T(8,128)(2,1)S(1)}, u32[]{:S(2)}, u32[]{:S(2)}) async-start(bf16[8,72,768]{2,1,0:T(8,128)(2,1)} %shard_map.174), calls=%async_computation.1 | async-start | bytes 1769472 | tf_op jit(solution)/shard_map/all_to_all | solution.py:504
  57.2 9.0 %copy-start.15 = (bf16[8,72,768]{2,1,0:T(8,128)(2,1)}, bf16[8,72,768]{2,1,0:T(8,128)(2,1)S(1)}, u32[]{:S(2)}) copy-start(bf16[8,72,768]{2,1,0:T(8,128)(2,1)S(1)} %all-to-all-done.1.refs_8_) | copy-start | bytes 2654212
  57.2 26.0 %all-to-all-start = ((bf16[8,72,768]{2,1,0:T(8,128)(2,1)}), bf16[8,72,768]{2,1,0:T(8,128)(2,1)S(1)}, u32[]{:S(2)}, u32[]{:S(2)}) async-start(bf16[8,72,768]{2,1,0:T(8,128)(2,1)} %get-tuple-element.21), calls=%async_computation | async-start | bytes 1769472 | tf_op jit(solution)/shard_map/all_to_all | solution.py:535
  78.2 8.6 %copy-start.19 = (bf16[2,4,35,768]{3,2,1,0:T(8,128)(2,1)S(1)}, bf16[2,4,35,768]{3,2,1,0:T(8,128)(2,1)}, u32[]{:S(2)}) copy-start(bf16[2,4,35,768]{3,2,1,0:T(8,128)(2,1)} %get-tuple-element.44) | copy-start | bytes 1290244
  78.2 9.5 %copy-start.22 = (f32[2,512]{1,0:T(2,128)S(1)}, f32[2,512]{1,0:T(2,128)}, u32[]{:S(2)}) copy-start(f32[2,512]{1,0:T(2,128)} %get-tuple-element.27) | copy-start | bytes 12292
  78.2 14.8 %copy-start.17 = (bf16[2,257,768]{2,1,0:T(8,128)(2,1)S(1)}, bf16[2,257,768]{2,1,0:T(8,128)(2,1)}, u32[]{:S(2)}) copy-start(bf16[2,257,768]{2,1,0:T(8,128)(2,1)} %get-tuple-element.47) | copy-start | bytes 2368516
  83.2 25.9 %all-to-all-start.2 = ((bf16[8,72,768]{2,1,0:T(8,128)(2,1)}), bf16[8,72,768]{2,1,0:T(8,128)(2,1)S(1)}, u32[]{:S(2)}, u32[]{:S(2)}) async-start(bf16[8,72,768]{2,1,0:T(8,128)(2,1)} %get-tuple-element.26), calls=%async_computation.2 | async-start | bytes 1769472 | tf_op jit(solution)/shard_map/all_to_all | solution.py:582
  86.7 7.8 %copy-start.16 = (bf16[2,257,768]{2,1,0:T(8,128)(2,1)S(1)}, bf16[2,257,768]{2,1,0:T(8,128)(2,1)}, u32[]{:S(2)}) copy-start(bf16[2,257,768]{2,1,0:T(8,128)(2,1)} %get-tuple-element.48) | copy-start | bytes 2368516
  87.7 21.4 %copy-start.11 = (s32[16,16]{1,0:T(8,128)S(1)}, s32[16,16]{1,0:T(8,128)}, u32[]{:S(2)}) copy-start(s32[16,16]{1,0:T(8,128)} %copy-done.10) | copy-start | bytes 3076
  87.7 21.4 %copy-start.14 = (s32[2]{0:T(128)S(1)}, s32[2]{0:T(128)}, u32[]{:S(2)}) copy-start(s32[2]{0:T(128)} %copy-done.13) | copy-start | bytes 28

commit v3 on v2

--- a/solution.py
+++ b/solution.py
@@ -21,11 +21,11 @@
 CHUNK = 3
 
 
-def kernel_call(body, out_shape, n_smem, n_any, scratch=(), flops=0, nbytes=0, space=ANY, mib=56, **more):
+def kernel_call(body, out_shape, n_smem, n_any, scratch=(), flops=0, nbytes=0, space=ANY, mib=60, n_after=0, **more):
     return pl.pallas_call(
         body,
         out_shape=out_shape,
-        in_specs=[SMEM] * n_smem + [space] * n_any,
+        in_specs=[SMEM] * n_smem + [space] * n_any + [ANY] * n_after,
         out_specs=jax.tree.map(lambda _: space, out_shape),
         scratch_shapes=list(scratch),
         compiler_params=pltpu.CompilerParams(vmem_limit_bytes=mib * 1024 * 1024),
@@ -63,20 +63,20 @@
         jax.ShapeDtypeStruct(value.shape, value.dtype),
         0,
         1 + len(others),
-        mib=1,
         input_output_aliases={0: 0},
     )(value, *others)
 
 
-def pack_body(queries, pictures, packed):
+def pack_body(queries, pictures, packed, both):
     captions, caption = queries.shape[:2]
-    first, emb = packed.shape[0] - fold_rows(pictures.shape, packed.shape[1]), pictures.shape[1]
+    first, emb = packed.shape[0], pictures.shape[1]
     pieces = [queries[row].astype(F32) for row in range(captions)]
     pieces.append(jnp.zeros((first - captions * caption, packed.shape[1]), F32))
-    packed[0:first, :] = jnp.concatenate(pieces, axis=0).astype(BF16)
-    packed[first:, :] = jnp.zeros((packed.shape[0] - first, packed.shape[1]), BF16)
+    packed[...] = jnp.concatenate(pieces, axis=0).astype(BF16)
+    both[0:first, :] = packed[...]
+    both[first:, :] = jnp.zeros((both.shape[0] - first, packed.shape[1]), BF16)
     for fold, (start, count) in enumerate(folds(pictures.shape, packed.shape[1])):
-        packed[first : first + count, fold * emb : (fold + 1) * emb] = pictures[start : start + count]
+        both[first : first + count, fold * emb : (fold + 1) * emb] = pictures[start : start + count]
 
 
 def fold_rows(shape, width):
@@ -93,7 +93,8 @@
     return tables[first + entry, row], tables[first + NEGS + entry, row]
 
 
-def send_body(tables, place, cots, sent):
+def send_body(tables, place, cots, *refs):
+    sent = refs[-1]
     rows, caption = cots.shape[0], cots.shape[2]
     for part in range(sent.shape[0]):
         pieces = []
@@ -107,16 +108,28 @@
         sent[part] = jnp.concatenate(pieces, axis=0).astype(BF16)
 
 
-def contrast_body(n_parts, rows, place, softness, *refs):
-    parts, refs = refs[:n_parts], refs[n_parts:]
-    texts, row_out, col_out, held, texts_in, unit_images, unit_texts, row_stats, col_stats, sems = refs
-    emb, step = texts_in.shape[1], held.shape[1]
-    lines = pl.ds(parts[0].shape[0] - step, step)
-    wait_copies(
-        start_copies(
-            [(texts, texts_in)] + [(parts[n].at[lines], held.at[n]) for n in range(n_parts)], sems
-        )
-    )
+def in_pieces(values):
+    pieces = []
+    for value in values:
+        for _ in range(3):
+            pieces.append(value.astype(BF16).astype(F32))
+            value = value - pieces[-1]
+    return jnp.concatenate(pieces, axis=1)
+
+
+def from_pieces(line):
+    width = line.shape[1] // 6
+    pieces = [line[:, n * width : (n + 1) * width] for n in range(6)]
+    return pieces[0] + pieces[1] + pieces[2], pieces[3] + pieces[4] + pieces[5]
+
+
+def joined(parts):
+    highest = functools.reduce(jnp.maximum, parts)
+    return highest + jnp.log(sum(jnp.exp(part - highest) for part in parts))
+
+
+def contrast(n_parts, place, softness, near_in, images_in, texts_in, unit_images, unit_texts, row_stats, col_stats):
+    rows, emb = images_in.shape[1:]
 
     def unit(source):
         wide = source.astype(F32)
@@ -124,45 +137,35 @@
         return (wide * factor).astype(BF16)
 
     unit_texts[...] = unit(texts_in[...])
+    for part in range(n_parts // 2):
+        for fold, (start, count) in enumerate(folds((rows, emb), near_in.shape[2])):
+            images_in[part, start : start + count, :] = near_in[part, 0:count, fold * emb : (fold + 1) * emb]
     for part in range(n_parts):
         first = jnp.bitwise_xor(part, place[0]) * rows
-        for fold, (start, count) in enumerate(folds((rows, emb), held.shape[2])):
-            at = pl.ds(pl.multiple_of(first + start, 16), count)
-            unit_images[at, :] = unit(held[part, 0:count, fold * emb : (fold + 1) * emb])
+        unit_images[pl.ds(pl.multiple_of(first, 16), rows), :] = unit(images_in[part])
     undo = 1.0 / softness[0]
     n_images, n_texts = n_parts * rows, texts_in.shape[0]
     first_image, first_text = place[1] * n_images, place[0] * n_texts
 
-    def stats(long, long_first, short, short_first):
-        logits = dot(long, short, NT) * undo
-        highest = jnp.max(logits, axis=0, keepdims=True)
-        total = jnp.sum(jnp.exp(logits - highest), axis=0, keepdims=True)
-        on_diag = (lax.broadcasted_iota(jnp.int32, logits.shape, 0) + long_first) == (
-            lax.broadcasted_iota(jnp.int32, logits.shape, 1) + short_first
-        )
-        diag = jnp.sum(jnp.where(on_diag, logits, 0.0), axis=0, keepdims=True)
-        return highest + jnp.log(total), diag
-
-    for block in range(n_parts):
-        first = block * rows
-        found = stats(
-            unit_texts[...], first_text, unit_images[first : first + rows, :], first_image + first
-        )
-        at = 0
-        for value in found:
-            for _ in range(3):
-                piece = value.astype(BF16).astype(F32)
-                row_stats[block, :, at : at + rows] = piece
-                value = value - piece
-                at += rows
-    for block in range(n_texts // LANES):
-        first = block * LANES
-        found = stats(
-            unit_images[...], first_image, unit_texts[first : first + LANES, :], first_text + first
-        )
+    def stats(long, long_first, short, short_first, count):
+        blocks = range(0, short.shape[0], count)
+        logits = [dot(long[...], short[at : at + count, :], NT) * undo for at in blocks]
+        highest = [jnp.max(block, axis=0, keepdims=True) for block in logits]
+        total = [
+            jnp.sum(jnp.exp(block - top), axis=0, keepdims=True) for block, top in zip(logits, highest)
+        ]
+        for at, block, top, whole in zip(blocks, logits, highest, total):
+            on_diag = (lax.broadcasted_iota(jnp.int32, block.shape, 0) + long_first) == (
+                lax.broadcasted_iota(jnp.int32, block.shape, 1) + (short_first + at)
+            )
+            diag = jnp.sum(jnp.where(on_diag, block, 0.0), axis=0, keepdims=True)
+            yield at, (top + jnp.log(whole), diag)
+
+    for at, found in stats(unit_texts, first_text, unit_images, first_image, rows):
+        row_stats[at // rows] = in_pieces(found)
+    for at, found in stats(unit_images, first_image, unit_texts, first_text, LANES):
         for n, value in enumerate(found):
-            col_stats[n : n + 1, first : first + LANES] = value
-    wait_copies(start_copies([(row_stats, row_out), (col_stats, col_out)], sems))
+            col_stats[n : n + 1, at : at + LANES] = value
 
 
 def attend(chunks, queries, cots, keys, values, sums):
@@ -358,25 +361,39 @@
     wait_copies(copies)
 
 
-def text_body(n_parts, tables, place, *refs):
-    parts, refs = refs[:n_parts], refs[n_parts:]
-    (cots_in, keys_in, values_in, stats_in, terms_in, key_in, value_in, q_out, key_grad, value_grad,
-     held, queries, cots_held, cots, keys, values, stats, terms, q_sum, firsts, sums, grads,
-     lists, counts, sems) = refs
+def text_body(n_parts, tables, place, softness, *refs):
+    half = n_parts // 2
+    parts, pictures, refs = refs[:n_parts], refs[n_parts : n_parts + half], refs[n_parts + half :]
+    (texts, cots_in, keys_in, values_in, terms_in, key_in, value_in), refs = refs[:7], refs[7:]
+    q_out, refs = refs[:half], refs[half:]
+    (key_grad, value_grad, col_out,
+     held, queries, cots_held, cots, keys, values, terms, q_sum, firsts, sums, grads,
+     near_in, images_in, texts_in, unit_images, unit_texts, row_stats, col_stats, lists, counts, sems) = refs
     images = captions = keys.shape[0]
     caption = terms.shape[2]
     rows = queries.shape[1]
     everyone = n_parts * captions
+    soon = start_copies(
+        [(texts, texts_in)]
+        + [(part.at[pl.ds(held.shape[1], near_in.shape[1])], near_in.at[n]) for n, part in enumerate(parts[:half])]
+        + [(picture, images_in.at[half + n]) for n, picture in enumerate(pictures)],
+        sems,
+    )
     copies = start_copies(
-        query_copies(parts, held) + [(cots_in, cots_held), (keys_in, keys), (values_in, values)], sems
-    )
-    later = start_copies(
-        [(stats_in, stats), (terms_in, terms), *zip((key_in, value_in), firsts)], sems, len(copies)
+        query_copies(parts, held) + [(cots_in, cots_held), (keys_in, keys), (values_in, values)],
+        sems,
+        len(soon),
     )
     find_listed(tables, place, lists, counts, everyone)
     for total in (*sums, q_sum):
         total[...] = jnp.zeros_like(total)
+    wait_copies(soon)
+    contrast(
+        n_parts, place, softness, near_in, images_in, texts_in, unit_images, unit_texts, row_stats, col_stats
+    )
     wait_copies(copies)
+    later = start_copies([(terms_in, terms), *zip((key_in, value_in), firsts)], sems)
+    out = start_copies([(col_stats, col_out)], sems, len(soon))
     widen_queries(held, queries, captions, caption)
     for part in range(n_parts):
         widen_block(cots_held[part].astype(F32), cots, part * captions, captions, caption)
@@ -399,14 +416,14 @@
             owner, slot = named(tables, 0, place[0] * images + image, entry)
             at = jnp.bitwise_xor(owner, place[0]) * captions + slot
             q_sum[at, 0:caption, :] += terms[image, entry].astype(F32)
-    out = []
+    block_rows = cots_held.shape[1]
     for part in range(n_parts):
-        first = jnp.bitwise_xor(part, place[0]) * captions
-        pieces = [q_sum[first + row, 0:caption, :] for row in range(captions)]
-        pieces.append(stats[part])
-        pieces.append(jnp.zeros((cots_held.shape[1] - captions * caption - 1, stats.shape[2]), F32))
+        target = jnp.bitwise_xor(part, place[0])
+        pieces = [q_sum[part * captions + row, 0:caption, :] for row in range(captions)]
+        pieces.append(row_stats[target])
+        pieces.append(jnp.zeros((block_rows - captions * caption - 1, cots_held.shape[2]), F32))
         cots_held[part] = jnp.concatenate(pieces, axis=0).astype(BF16)
-        out += start_copies([(cots_held.at[part], q_out.at[part])], sems, part)
+        out += start_copies([(cots_held.at[part], q_out[part % half].at[part // half])], sems, part)
     for n, grad in enumerate((key_grad, value_grad)):
         for image in range(images):
             grads[n][image] = (sums[n][image] + firsts[n][image]).astype(BF16)
@@ -414,34 +431,35 @@
     wait_copies(out)
 
 
-def join_body(tables, place, got_out, got_q, cols, pair_out, q_grad, image_loss, text_loss):
+def add_lines(blocks, lines):
+    total = blocks[0].astype(F32)
+    for block in blocks[1:]:
+        total = total + block.astype(F32)
+    found = [from_pieces(block[lines : lines + 1].astype(F32)) for block in blocks]
+    return total[0:lines], joined([lse for lse, _ in found]), sum(diag for _, diag in found)
+
+
+def half_body(lines, after, *refs):
+    del after
+    blocks, kept, sent = refs[:-2], refs[-2], refs[-1]
+    for side, out in enumerate((kept, sent)):
+        total, lse, diag = add_lines([block[side] for block in blocks], lines)
+        rest = jnp.zeros((out.shape[0] - lines - 1, out.shape[1]), F32)
+        out[...] = jnp.concatenate([total, in_pieces([lse, diag]), rest], axis=0).astype(out.dtype)
+
+
+def join_body(tables, place, got_out, kept, got_q, cols, pair_out, q_grad, image_loss, text_loss):
     rows, caption = pair_out.shape[0], pair_out.shape[2]
-    n_parts = got_q.shape[0]
     for row in range(rows):
         lines = slice(row * caption, (row + 1) * caption)
         for entry in range(NEGS):
             owner, _ = named(tables, 1, place[0] * rows + row, entry)
             block = got_out[owner].astype(F32)
             pair_out[row, entry] = block[lines].astype(BF16)
-    total = got_q[0].astype(F32)
-    for source in range(1, n_parts):
-        total = total + got_q[source].astype(F32)
+    total, lse, diag = add_lines([kept[...], got_q[...]], rows * caption)
     for row in range(rows):
         q_grad[row] = total[row * caption : (row + 1) * caption].astype(BF16)
-
-    def joined(parts):
-        highest = functools.reduce(jnp.maximum, parts)
-        return highest + jnp.log(sum(jnp.exp(part - highest) for part in parts))
-
-    width = image_loss.shape[1]
-    line = rows * caption
-    lse, diag = [], jnp.zeros(image_loss.shape, F32)
-    for source in range(n_parts):
-        stats = got_q[source].astype(F32)[line : line + 1]
-        pieces = [stats[:, n * width : (n + 1) * width] for n in range(6)]
-        lse.append(pieces[0] + pieces[1] + pieces[2])
-        diag = diag + (pieces[3] + pieces[4] + pieces[5])
-    image_loss[...] = joined(lse) - diag
+    image_loss[...] = lse - diag
     n_cols = cols.shape[0]
     text_loss[...] = joined([cols[n, 0:1, :] for n in range(n_cols)]) - sum(
         cols[n, 1:2, :] for n in range(n_cols)
@@ -482,7 +500,7 @@
     local, caption, width = queries.shape
     patches = keys.shape[1]
     rows = padded(caption)
-    everyone = n_txt * local
+    everyone, half = n_txt * local, n_txt // 2
     block_shape = (n_txt, padded(local * caption + 1), width)
     wide_shape = (everyone + 1, rows, width)
     query_rows = -(-local * caption // 16) * 16
@@ -493,16 +511,27 @@
     lists = [pltpu.SMEM((local, everyone + 2 * CHUNK), jnp.int32), pltpu.SMEM((local,), jnp.int32)]
 
     step = fold_rows(pictures.shape, width)
-    packed = kernel_call(pack_body, shape((query_rows + step, width), BF16), 0, 2, space=VMEM, mib=8)(
-        queries, pictures
-    )
-    parts = gathered(packed, "txt")
-    sent = kernel_call(send_body, shape(block_shape, BF16), 2, 1, space=VMEM, mib=12)(
-        tables, place, txt_cots
-    )
-    ready = parts[1 : n_txt // 2] + parts[n_txt // 2 + 1 :]
-    got_cots = lax.all_to_all(tie(sent, *ready, keys, values, img_cots), "txt", 0, 0, tiled=True)
-
+    packed, both = kernel_call(
+        pack_body,
+        (shape((query_rows, width), BF16), shape((query_rows + step, width), BF16)),
+        0,
+        2,
+        space=VMEM,
+        mib=8,
+    )(queries, pictures)
+    other = swap(packed, "txt", half)
+    near = [both] + [swap(both, "txt", mask) for mask in range(1, half)]
+    parts = near + [other] + [swap(other, "txt", mask) for mask in range(1, half)]
+    other_pictures = swap(pictures, "txt", half)
+    far_pictures = [other_pictures] + [swap(other_pictures, "txt", mask) for mask in range(1, half)]
+    after = (*parts[1:], *far_pictures)
+    sent = kernel_call(
+        send_body, shape(block_shape, BF16), 2, 1, space=VMEM, mib=12, n_after=len(after)
+    )(tables, place, txt_cots, *after)
+    got_cots = lax.all_to_all(sent, "txt", 0, 0, tiled=True)
+
+    image_rows, n_texts, emb = pictures.shape[0], wordings.shape[0], wordings.shape[1]
+    stats_shape = (n_txt, 1, 6 * image_rows)
     img_pair_out, image_terms, key_part, value_part, out = kernel_call(
         functools.partial(image_body, n_txt),
         (
@@ -534,32 +563,12 @@
     )(tables, place, *parts, img_cots, keys, values)
     got_out = lax.all_to_all(out, "txt", 0, 0, tiled=True)
 
-    image_rows, n_texts, emb = pictures.shape[0], wordings.shape[0], wordings.shape[1]
-    stats_shape = (n_txt, 1, 6 * image_rows)
-    row_stats, col_stats = kernel_call(
-        functools.partial(contrast_body, n_txt, image_rows),
-        (shape(stats_shape, F32), shape((2, n_texts), F32)),
-        2,
-        n_txt + 1,
-        [
-            vmem((n_txt, step, width), BF16),
-            vmem(wordings.shape, BF16),
-            vmem((n_txt * image_rows, emb), BF16),
-            vmem(wordings.shape, BF16),
-            vmem(stats_shape, F32),
-            vmem((2, n_texts), F32),
-            dma(n_txt + 1),
-        ],
-        flops=4 * n_txt * image_rows * n_texts * emb,
-        nbytes=1_000_000,
-    )(place, softness, *parts, wordings)
-    got_cols = lax.all_gather(col_stats, "img", axis=0)
-
-    q_out, key_grad, value_grad = kernel_call(
+    *q_out, key_grad, value_grad, col_stats = kernel_call(
         functools.partial(text_body, n_txt),
-        (shape(block_shape, BF16), shape(keys.shape, BF16), shape(values.shape, BF16)),
-        2,
-        n_txt + 7,
+        [shape((2,) + block_shape[1:], BF16)] * half
+        + [shape(keys.shape, BF16), shape(values.shape, BF16), shape((2, n_texts), F32)],
+        3,
+        n_txt + half + 7,
         [
             vmem(held_shape, BF16),
             vmem(wide_shape, F32),
@@ -567,19 +576,39 @@
             vmem(wide_shape, F32),
             vmem(keys.shape, BF16),
             vmem(values.shape, BF16),
-            vmem(stats_shape, F32),
             vmem(img_cots.shape, BF16),
             vmem(wide_shape, F32),
             sums,
             sums,
             [vmem(keys.shape, BF16), vmem(values.shape, BF16)],
+            vmem((half, step, width), BF16),
+            vmem((n_txt,) + pictures.shape, BF16),
+            vmem(wordings.shape, BF16),
+            vmem((n_txt * image_rows, emb), BF16),
+            vmem(wordings.shape, BF16),
+            vmem(stats_shape, F32),
+            vmem((2, n_texts), F32),
             *lists,
-            dma(n_txt + 7),
+            dma(2 * n_txt + 4),
         ],
         flops=4 * local * NEGS * pair_flops,
         nbytes=10_000_000,
-    )(tables, place, *parts, got_cots, keys, values, row_stats, image_terms, key_part, value_part)
-    got_q = lax.all_to_all(q_out, "txt", 0, 0, tiled=True)
+    )(
+        tables, place, softness, *parts, *far_pictures, wordings, got_cots, keys, values,
+        image_terms, key_part, value_part,
+    )
+    got_cols = lax.all_gather(tie(col_stats, q_out[0]), "img", axis=0)
+    near = [q_out[0]] + [swap(block, "txt", 1 + n) for n, block in enumerate(q_out[1:])]
+    kept, across = kernel_call(
+        functools.partial(half_body, local * caption),
+        (shape(block_shape[1:], F32), shape(block_shape[1:], BF16)),
+        0,
+        1 + half,
+        space=VMEM,
+        mib=12,
+        nbytes=2_000_000,
+    )(got_cols, *near)
+    got_q = swap(across, "txt", half)
 
     txt_pair_out, query_grad, image_loss, text_loss = kernel_call(
         join_body,
@@ -590,10 +619,10 @@
             shape((1, n_texts), F32),
         ),
         2,
-        3,
+        4,
         space=VMEM,
         mib=16,
-    )(tables, place, got_out, got_q, got_cols)
+    )(tables, place, got_out, kept, got_q, got_cols)
     return (
         image_loss.reshape(-1),
         text_loss.reshape(-1),

time: 113 us -> 101 us (0.89)
  waiting for transfers between devices: 37.4 us -> 12.3 us
  starting transfers between devices: 23 us -> 31.5 us
  local copies, waits for them, and re-layouts: 10.5 us -> 13.3 us
  Pallas kernels: 34.1 us -> 35.8 us
    all_to_all x2 -> x1, waiting for transfers between devices: 20.7 us -> 0.21 us  [on_device(): got_cots = lax.all_to_all(sent, 'txt', 0, 0, tiled=True)]
    ppermute x7 -> x15, starting transfers between devices: 11.1 us -> 23.3 us  [swap(): lax.ppermute(part, axis, [(s, s ^ mask) for s in range(lax.axis_size(axis...]
    all_to_all x1, waiting for transfers between devices: 4.95 us -> 0.01 us  [on_device(): got_out = lax.all_to_all(out, 'txt', 0, 0, tiled=True)]
    all_to_all x2 -> x1, starting transfers between devices: 8.2 us -> 3.99 us  [on_device(): got_cots = lax.all_to_all(sent, 'txt', 0, 0, tiled=True)]
    unnamed x66 -> x58, local copies, waits for them, and re-layouts: 10.5 us -> 13.3 us
    pallas_call x1, Pallas kernels: 14.4 us -> 16 us  [on_device(): kernel_call(functools.partial(image_body, n_txt), (shape(img_cots.shape,...]
    ppermute x7 -> x15, waiting for transfers between devices: 11.8 us -> 12 us  [swap(): lax.ppermute(part, axis, [(s, s ^ mask) for s in range(lax.axis_size(axis...]
  transfers between devices with their start and end apart: 10 -> 17, of which waited for: 8 -> 8; matrix products, arithmetic and copies ran while one was open for 5% -> 10% of each run, Pallas kernels for 29% -> 33%
where the time goes in v3:
time: 101 us
  Pallas kernels  35.8 us (35%)
  starting transfers between devices  31.5 us (31%)
  local copies, waits for them, and re-layouts  13.3 us (13%)
  waiting for transfers between devices  12.3 us (12%)
  blocking collectives  5.38 us (5%)
  between operations  1.53 us (2%)
    ppermute x15, starting transfers between devices, swap(): lax.ppermute(part, axis, [(s, s ^ mask) for s in range(lax.axis_size(axis...  23.3 us
    pallas_call x1, Pallas kernels, on_device(): kernel_call(functools.partial(text_body, n_txt), [shape((2,) + block_shap...  16.6 us
    pallas_call x1, Pallas kernels, on_device(): kernel_call(functools.partial(image_body, n_txt), (shape(img_cots.shape,...  16 us
    unnamed x58, local copies, waits for them, and re-layouts  13.3 us
    ppermute x15, waiting for transfers between devices, swap(): lax.ppermute(part, axis, [(s, s ^ mask) for s in range(lax.axis_size(axis...  12 us
    all_gather x1, blocking collectives, on_device(): got_cols = lax.all_gather(tie(col_stats, q_out[0]), 'img', axis=0)  5.38 us
    all_to_all x1, starting transfers between devices, on_device(): got_out = lax.all_to_all(out, 'txt', 0, 0, tiled=True)  4.21 us
    all_to_all x1, starting transfers between devices, on_device(): got_cots = lax.all_to_all(sent, 'txt', 0, 0, tiled=True)  3.99 us
  transfers between devices with their start and end apart: 17, of which 8 were waited for; matrix products, arithmetic and copies ran while one was open for 10% of the time, Pallas kernels for 33%

profile of v3, /device:TPU:0, one launch (start us, length us, event | category | flops | bytes accessed | tf_op | source)
XLA Modules:
  0.0 100.6 jit_solution(10407506781427359687)
XLA Ops:
  0.6 0.9 copy.32.queries
  1.5 0.0 copy-start.10
  1.6 0.8 copy-done.10
  2.4 4.0 %collective-permute-start.2 = (bf16[128,768]{1,0:T(8,128)(2,1)S(1)}, bf16[128,768]{1,0:T(8,128)(2,1)S(1)}, u32[]{:S(2)}, u32[]{:S(2)}) collective-permute-start(bf16[128,768]{1,0:T(8,128)(2,1)S(1)} %get-tuple-element.27.refs_0_), channel_id=1, source_target_pairs={{0,3},{1,2},{2,1},{3,0},{4,7},{5,6},{6,5},{7,4},{8,11},{9,10},{10,... | collective-permute-start | bytes 589832 | tf_op jit(solution)/shard_map/ppermute | solution.py:470
  6.4 2.6 %collective-permute-start.7 = (bf16[128,256]{1,0:T(8,128)(2,1)S(1)}, bf16[128,256]{1,0:T(8,128)(2,1)S(1)}, u32[]{:S(2)}, u32[]{:S(2)}) collective-permute-start(bf16[128,256]{1,0:T(8,128)(2,1)S(1)} %copy-done.10), channel_id=1, source_target_pairs={{0,4},{1,5},{2,6},{3,7},{4,0},{5,1},{6,2},{7,3},{8,12},{9,13},{10,... | collective-permute-start | bytes 196616 | tf_op jit(solution)/shard_map/ppermute | solution.py:470
  9.0 0.3 collective-permute-start.3
  9.4 3.8 %collective-permute-done.7.refs_7_.refs_8_ = bf16[128,256]{1,0:T(8,128)(2,1)S(1)} collective-permute-done((bf16[128,256]{1,0:T(8,128)(2,1)S(1)}, bf16[128,256]{1,0:T(8,128)(2,1)S(1)}, u32[]{:S(2)}, u32[]{:S(2)}) %collective-permute-start.7) | collective-permute-done | bytes 65568 | tf_op jit(solution)/shard_map/ppermute | solution.py:470
  13.2 3.5 %collective-permute-start.10 = (bf16[128,256]{1,0:T(8,128)(2,1)S(1)}, bf16[128,256]{1,0:T(8,128)(2,1)S(1)}, u32[]{:S(2)}, u32[]{:S(2)}) collective-permute-start(bf16[128,256]{1,0:T(8,128)(2,1)S(1)} %collective-permute-done.7.refs_7_.refs_8_), channel_id=1, source_target_pairs={{0,3},{1,2},{2,1},{3,0},{4,7},{5,6},{6,5},{7,4},{8,11},{9,10},{10,... | collective-permute-start | bytes 196616 | tf_op jit(solution)/shard_map/ppermute | solution.py:470
  16.7 0.1 collective-permute-start.9
  16.8 1.4 %collective-permute-start.8 = (bf16[128,256]{1,0:T(8,128)(2,1)S(1)}, bf16[128,256]{1,0:T(8,128)(2,1)S(1)}, u32[]{:S(2)}, u32[]{:S(2)}) collective-permute-start(bf16[128,256]{1,0:T(8,128)(2,1)S(1)} %collective-permute-done.7.refs_7_.refs_8_), channel_id=1, source_target_pairs={{0,1},{1,0},{2,3},{3,2},{4,5},{5,4},{6,7},{7,6},{8,9},{9,8},{10,11... | collective-permute-start | bytes 196616 | tf_op jit(solution)/shard_map/ppermute | solution.py:470
  18.2 2.0 %collective-permute-start.1 = (bf16[128,768]{1,0:T(8,128)(2,1)S(1)}, bf16[128,768]{1,0:T(8,128)(2,1)S(1)}, u32[]{:S(2)}, u32[]{:S(2)}) collective-permute-start(bf16[128,768]{1,0:T(8,128)(2,1)S(1)} %get-tuple-element.27.refs_0_), channel_id=1, source_target_pairs={{0,2},{1,3},{2,0},{3,1},{4,6},{5,7},{6,4},{7,5},{8,10},{9,11},{10,... | collective-permute-start | bytes 589832 | tf_op jit(solution)/shard_map/ppermute | solution.py:470
  20.3 1.0 collective-permute-start
  21.2 0.5 collective-permute-done.9.refs_9_.refs_10_
  21.7 2.4 %collective-permute-start.6 = (bf16[80,768]{1,0:T(8,128)(2,1)S(1)}, bf16[80,768]{1,0:T(8,128)(2,1)S(1)}, u32[]{:S(2)}, u32[]{:S(2)}) collective-permute-start(bf16[80,768]{1,0:T(8,128)(2,1)S(1)} %collective-permute-done.3.refs_4_.refs_3_), channel_id=1, source_target_pairs={{0,3},{1,2},{2,1},{3,0},{4,7},{5,6},{6,5},{7,4},{8,11},{9,10},{10,... | collective-permute-start | bytes 368648 | tf_op jit(solution)/shard_map/ppermute | solution.py:470
  24.1 1.1 %collective-permute-start.5 = (bf16[80,768]{1,0:T(8,128)(2,1)S(1)}, bf16[80,768]{1,0:T(8,128)(2,1)S(1)}, u32[]{:S(2)}, u32[]{:S(2)}) collective-permute-start(bf16[80,768]{1,0:T(8,128)(2,1)S(1)} %collective-permute-done.3.refs_4_.refs_3_), channel_id=1, source_target_pairs={{0,2},{1,3},{2,0},{3,1},{4,6},{5,7},{6,4},{7,5},{8,10},{9,11},{10,... | collective-permute-start | bytes 368648 | tf_op jit(solution)/shard_map/ppermute | solution.py:470
  25.2 1.2 %collective-permute-start.4 = (bf16[80,768]{1,0:T(8,128)(2,1)S(1)}, bf16[80,768]{1,0:T(8,128)(2,1)S(1)}, u32[]{:S(2)}, u32[]{:S(2)}) collective-permute-start(bf16[80,768]{1,0:T(8,128)(2,1)S(1)} %collective-permute-done.3.refs_4_.refs_3_), channel_id=1, source_target_pairs={{0,1},{1,0},{2,3},{3,2},{4,5},{5,4},{6,7},{7,6},{8,9},{9,8},{10,11... | collective-permute-start | bytes 368648 | tf_op jit(solution)/shard_map/ppermute | solution.py:470
  26.5 0.1 pad_add_fusion.1.place
  26.5 1.1 %copy.36.cots = bf16[2,4,35,768]{3,2,1,0:T(8,128)(2,1)S(1)} copy(bf16[2,4,35,768]{3,1,2,0:T(4,128)(2,1)} %param.23) | data formatting | bytes 860160 | tf_op args[11]
  27.6 0.7 pad_add_fusion.tables
  28.4 0.7 collective-permute-done.refs_1_.refs_0_
  29.1 0.2 collective-permute-done.5.refs_6_.refs_5_
  29.2 1.2 %collective-permute-done.4.refs_5_.refs_4_ = bf16[80,768]{1,0:T(8,128)(2,1)S(1)} collective-permute-done((bf16[80,768]{1,0:T(8,128)(2,1)S(1)}, bf16[80,768]{1,0:T(8,128)(2,1)S(1)}, u32[]{:S(2)}, u32[]{:S(2)}) %collective-permute-start.4) | collective-permute-done | bytes 122912 | tf_op jit(solution)/shard_map/ppermute | solution.py:470
  30.4 1.8 %shard_map.173 = bf16[8,72,768]{2,1,0:T(8,128)(2,1)} custom-call(s32[16,16]{1,0:T(8,128)S(1)} %pad_add_fusion.tables, s32[2]{0:T(128)S(1)} %pad_add_fusion.1.place, bf16[2,4,35,768]{3,2,1,0:T(8,128)(2,1)S(1)} %copy.36.cots, bf16[128,768]{1,0:T(8,128)(2,1)S(1)} %collective-permute-done.refs_1_.refs_0_, ...), custom_call_target="tpu_custom_call" | custom-call | tf_op jit(solution)/shard_map/pallas_call | solution.py:528
  32.2 0.0 copy-start.21
  32.3 4.0 %all-to-all-start.1 = ((bf16[8,72,768]{2,1,0:T(8,128)(2,1)}), bf16[8,72,768]{2,1,0:T(8,128)(2,1)S(1)}, u32[]{:S(2)}, u32[]{:S(2)}) async-start(bf16[8,72,768]{2,1,0:T(8,128)(2,1)} %shard_map.173), calls=%async_computation.1 | async-start | bytes 1769472 | tf_op jit(solution)/shard_map/all_to_all | solution.py:531
  36.3 1.9 %copy.33.refs_8_ = bf16[2,4,35,768]{3,2,1,0:T(8,128)(2,1)} copy(bf16[2,4,35,768]{3,1,2,0:T(4,128)(2,1)} %param.22) | data formatting | bytes 860160 | tf_op args[10]
  38.2 1.0 copy.34.refs_9_.refs_14_
  39.2 1.0 %copy.35.refs_10_.refs_15_ = bf16[2,257,768]{2,1,0:T(8,128)(2,1)} copy(bf16[2,257,768]{2,0,1:T(2,128)(2,1)S(1)} %copy-done.22) | data formatting | bytes 1579008 | tf_op args[5]
  40.2 16.0 %shard_map.172 = (bf16[2,4,35,768]{3,2,1,0:T(8,128)(2,1)}, bf16[2,4,35,768]{3,2,1,0:T(8,128)(2,1)}, f32[2,257,768]{2,1,0:T(8,128)}, f32[2,257,768]{2,1,0:T(8,128)}, bf16[8,72,768]{2,1,0:T(8,128)(2,1)}) custom-call(s32[16,16]{1,0:T(8,128)} %copy-done.8, s32[2]{0:T(128)} %copy-done.15, bf16[128,768]{1,0:T(8,128)(2,1)} %copy-done.17, ...), custom_call_target="tpu_custom_call" | custom-call | flops 3315916800 | bytes 12000000 | tf_op jit(solution)/shard_map/pallas_call | solution.py:535
  56.2 0.2 all-to-all-done.1.refs_13_
  56.4 4.2 %all-to-all-start = ((bf16[8,72,768]{2,1,0:T(8,128)(2,1)}), bf16[8,72,768]{2,1,0:T(8,128)(2,1)S(1)}, u32[]{:S(2)}, u32[]{:S(2)}) async-start(bf16[8,72,768]{2,1,0:T(8,128)(2,1)} %get-tuple-element.29), calls=%async_computation | async-start | bytes 1769472 | tf_op jit(solution)/shard_map/all_to_all | solution.py:564
  61.2 0.0 copy-start.23
  61.3 16.6 %shard_map.174 = (bf16[2,72,768]{2,1,0:T(8,128)(2,1)}, bf16[2,72,768]{2,1,0:T(8,128)(2,1)}, bf16[2,72,768]{2,1,0:T(8,128)(2,1)}, bf16[2,72,768]{2,1,0:T(8,128)(2...) custom-call(s32[16,16]{1,0:T(8,128)} %copy-done.8, s32[2]{0:T(128)} %copy-done.15, ...), custom_call_target="tpu_custom_call" | custom-call | flops 2210611200 | bytes 10000000 | tf_op jit(solution)/shard_map/pallas_call | solution.py:566
  77.9 0.1 collective-permute-start.11
  78.0 0.1 collective-permute-start.12
  78.1 3.4 %collective-permute-start.13 = (bf16[2,72,768]{2,1,0:T(8,128)(2,1)}, bf16[2,72,768]{2,1,0:T(8,128)(2,1)S(1)}, u32[]{:S(2)}, u32[]{:S(2)}) collective-permute-start(bf16[2,72,768]{2,1,0:T(8,128)(2,1)} %get-tuple-element.37), channel_id=1, source_target_pairs={{0,3},{1,2},{2,1},{3,0},{4,7},{5,6},{6,5},{7,4},{8,11},{9,10},{10,... | collective-permute-start | bytes 663560 | tf_op jit(solution)/shard_map/ppermute | solution.py:470
  81.5 5.4 %all-gather.1.after.cols = f32[4,2,512]{2,1,0:T(2,128)S(1)} all-gather(f32[1,2,512]{2,1,0:T(2,128)} %bitcast.9), channel_id=2, replica_groups=mesh['img'=4,'txt'=8] {'img'}, dimensions={0}, use_global_device_ids=true | all-gather | bytes 20480 | tf_op jit(solution)/shard_map/all_gather | solution.py:600
  86.8 3.5 %collective-permute-done.13.refs_3_ = bf16[2,72,768]{2,1,0:T(8,128)(2,1)S(1)} collective-permute-done((bf16[2,72,768]{2,1,0:T(8,128)(2,1)}, bf16[2,72,768]{2,1,0:T(8,128)(2,1)S(1)}, u32[]{:S(2)}, u32[]{:S(2)}) %collective-permute-start.13) | collective-permute-done | bytes 221216 | tf_op jit(solution)/shard_map/ppermute | solution.py:470
  90.3 0.9 copy-done
  91.3 0.1 shard_map.176
  91.4 0.1 collective-permute-start.14
  91.5 0.9 copy.39
  92.4 1.5 %copy.42 = bf16[2,257,768]{2,0,1:T(2,128)(2,1)} copy(bf16[2,257,768]{2,1,0:T(8,128)(2,1)S(1)} %copy-done.20) | data formatting | bytes 1579008
  93.9 1.5 %copy.43 = bf16[2,257,768]{2,0,1:T(2,128)(2,1)} copy(bf16[2,257,768]{2,1,0:T(8,128)(2,1)S(1)} %copy-done.19) | data formatting | bytes 1579008
  95.4 2.3 %collective-permute-done.14.got_q = bf16[72,768]{1,0:T(8,128)(2,1)S(1)} collective-permute-done((bf16[72,768]{1,0:T(8,128)(2,1)S(1)}, bf16[72,768]{1,0:T(8,128)(2,1)S(1)}, u32[]{:S(2)}, u32[]{:S(2)}) %collective-permute-start.14) | collective-permute-done | bytes 110624 | tf_op jit(solution)/shard_map/ppermute | solution.py:470
  97.7 1.3 %shard_map.177 = (bf16[2,4,35,768]{3,2,1,0:T(8,128)(2,1)S(1)}, bf16[2,35,768]{2,1,0:T(8,128)(2,1)S(1)}, f32[1,128]{1,0:T(1,128)}, f32[1,512]{1,0:T(1,128)}) custom-call(s32[16,16]{1,0:T(8,128)S(1)} %copy-done.9, s32[2]{0:T(128)S(1)} %copy-done.16, bf16[8,72,768]{2,1,0:T(8,128)(2,1)S(1)} %all-to-all-done.got_out, f32[72,768]{1,0:T(8,128)S(1)} %get-tuple-element.38.kept, ...), custom_call_target="tpu_custom_call" | custom-call | tf_op jit(solution)/shard_map/pallas_call | solution.py:613
  99.0 0.7 copy.41
  99.7 0.9 copy.40
  (54 shorter events, 0.1 us)
Async XLA Ops:
  1.5 0.8 copy-start.10
  2.4 29.7 %copy-start.17 = (bf16[128,768]{1,0:T(8,128)(2,1)}, bf16[128,768]{1,0:T(8,128)(2,1)S(1)}, u32[]{:S(2)}) copy-start(bf16[128,768]{1,0:T(8,128)(2,1)S(1)} %get-tuple-element.27.refs_0_) | copy-start | bytes 589828
  2.4 22.8 %collective-permute-start.2 = (bf16[128,768]{1,0:T(8,128)(2,1)S(1)}, bf16[128,768]{1,0:T(8,128)(2,1)S(1)}, u32[]{:S(2)}, u32[]{:S(2)}) collective-permute-start(bf16[128,768]{1,0:T(8,128)(2,1)S(1)} %get-tuple-element.27.refs_0_), channel_id=1, source_target_pairs={{0,3},{1,2},{2,1},{3,0},{4,7},{5,6},{6,5},{7,4},{8,11},{9,10},{10,... | collective-permute-start | bytes 589832 | tf_op jit(solution)/shard_map/ppermute | solution.py:470
  6.4 6.8 %collective-permute-start.7 = (bf16[128,256]{1,0:T(8,128)(2,1)S(1)}, bf16[128,256]{1,0:T(8,128)(2,1)S(1)}, u32[]{:S(2)}, u32[]{:S(2)}) collective-permute-start(bf16[128,256]{1,0:T(8,128)(2,1)S(1)} %copy-done.10), channel_id=1, source_target_pairs={{0,4},{1,5},{2,6},{3,7},{4,0},{5,1},{6,2},{7,3},{8,12},{9,13},{10,... | collective-permute-start | bytes 196616 | tf_op jit(solution)/shard_map/ppermute | solution.py:470
  9.0 9.2 %collective-permute-start.3 = (bf16[80,768]{1,0:T(8,128)(2,1)S(1)}, bf16[80,768]{1,0:T(8,128)(2,1)S(1)}, u32[]{:S(2)}, u32[]{:S(2)}) collective-permute-start(bf16[80,768]{1,0:T(8,128)(2,1)S(1)} %get-tuple-element.28), channel_id=1, source_target_pairs={{0,4},{1,5},{2,6},{3,7},{4,0},{5,1},{6,2},{7,3},{8,12},{9,13},{10,... | collective-permute-start | bytes 368648 | tf_op jit(solution)/shard_map/ppermute | solution.py:470
  13.2 18.9 %copy-start.11 = (bf16[128,256]{1,0:T(8,128)(2,1)}, bf16[128,256]{1,0:T(8,128)(2,1)S(1)}, u32[]{:S(2)}) copy-start(bf16[128,256]{1,0:T(8,128)(2,1)S(1)} %collective-permute-done.7.refs_7_.refs_8_) | copy-start | bytes 196612
  13.2 7.0 %collective-permute-start.10 = (bf16[128,256]{1,0:T(8,128)(2,1)S(1)}, bf16[128,256]{1,0:T(8,128)(2,1)S(1)}, u32[]{:S(2)}, u32[]{:S(2)}) collective-permute-start(bf16[128,256]{1,0:T(8,128)(2,1)S(1)} %collective-permute-done.7.refs_7_.refs_8_), channel_id=1, source_target_pairs={{0,3},{1,2},{2,1},{3,0},{4,7},{5,6},{6,5},{7,4},{8,11},{9,10},{10,... | collective-permute-start | bytes 196616 | tf_op jit(solution)/shard_map/ppermute | solution.py:470
  16.7 5.0 %collective-permute-start.9 = (bf16[128,256]{1,0:T(8,128)(2,1)S(1)}, bf16[128,256]{1,0:T(8,128)(2,1)S(1)}, u32[]{:S(2)}, u32[]{:S(2)}) collective-permute-start(bf16[128,256]{1,0:T(8,128)(2,1)S(1)} %collective-permute-done.7.refs_7_.refs_8_), channel_id=1, source_target_pairs={{0,2},{1,3},{2,0},{3,1},{4,6},{5,7},{6,4},{7,5},{8,10},{9,11},{10,... | collective-permute-start | bytes 196616 | tf_op jit(solution)/shard_map/ppermute | solution.py:470
  16.8 7.3 %collective-permute-start.8 = (bf16[128,256]{1,0:T(8,128)(2,1)S(1)}, bf16[128,256]{1,0:T(8,128)(2,1)S(1)}, u32[]{:S(2)}, u32[]{:S(2)}) collective-permute-start(bf16[128,256]{1,0:T(8,128)(2,1)S(1)} %collective-permute-done.7.refs_7_.refs_8_), channel_id=1, source_target_pairs={{0,1},{1,0},{2,3},{3,2},{4,5},{5,4},{6,7},{7,6},{8,9},{9,8},{10,11... | collective-permute-start | bytes 196616 | tf_op jit(solution)/shard_map/ppermute | solution.py:470
  18.2 13.9 %copy-start.4 = (bf16[80,768]{1,0:T(8,128)(2,1)}, bf16[80,768]{1,0:T(8,128)(2,1)S(1)}, u32[]{:S(2)}) copy-start(bf16[80,768]{1,0:T(8,128)(2,1)S(1)} %collective-permute-done.3.refs_4_.refs_3_) | copy-start | bytes 368644
  18.2 10.1 %collective-permute-start.1 = (bf16[128,768]{1,0:T(8,128)(2,1)S(1)}, bf16[128,768]{1,0:T(8,128)(2,1)S(1)}, u32[]{:S(2)}, u32[]{:S(2)}) collective-permute-start(bf16[128,768]{1,0:T(8,128)(2,1)S(1)} %get-tuple-element.27.refs_0_), channel_id=1, source_target_pairs={{0,2},{1,3},{2,0},{3,1},{4,6},{5,7},{6,4},{7,5},{8,10},{9,11},{10,... | collective-permute-start | bytes 589832 | tf_op jit(solution)/shard_map/ppermute | solution.py:470
  20.3 11.9 %copy-start.12 = (bf16[128,256]{1,0:T(8,128)(2,1)}, bf16[128,256]{1,0:T(8,128)(2,1)S(1)}, u32[]{:S(2)}) copy-start(bf16[128,256]{1,0:T(8,128)(2,1)S(1)} %collective-permute-done.10.refs_10_.refs_11_) | copy-start | bytes 196612
  20.3 8.8 %collective-permute-start = (bf16[128,768]{1,0:T(8,128)(2,1)S(1)}, bf16[128,768]{1,0:T(8,128)(2,1)S(1)}, u32[]{:S(2)}, u32[]{:S(2)}) collective-permute-start(bf16[128,768]{1,0:T(8,128)(2,1)S(1)} %get-tuple-element.27.refs_0_), channel_id=1, source_target_pairs={{0,1},{1,0},{2,3},{3,2},{4,5},{5,4},{6,7},{7,6},{8,9},{9,8},{10,11... | collective-permute-start | bytes 589832 | tf_op jit(solution)/shard_map/ppermute | solution.py:470
  21.7 10.5 %copy-start.13 = (bf16[128,256]{1,0:T(8,128)(2,1)}, bf16[128,256]{1,0:T(8,128)(2,1)S(1)}, u32[]{:S(2)}) copy-start(bf16[128,256]{1,0:T(8,128)(2,1)S(1)} %collective-permute-done.9.refs_9_.refs_10_) | copy-start | bytes 196612
  21.7 7.4 %collective-permute-start.6 = (bf16[80,768]{1,0:T(8,128)(2,1)S(1)}, bf16[80,768]{1,0:T(8,128)(2,1)S(1)}, u32[]{:S(2)}, u32[]{:S(2)}) collective-permute-start(bf16[80,768]{1,0:T(8,128)(2,1)S(1)} %collective-permute-done.3.refs_4_.refs_3_), channel_id=1, source_target_pairs={{0,3},{1,2},{2,1},{3,0},{4,7},{5,6},{6,5},{7,4},{8,11},{9,10},{10,... | collective-permute-start | bytes 368648 | tf_op jit(solution)/shard_map/ppermute | solution.py:470
  24.1 8.0 %copy-start.14 = (bf16[128,256]{1,0:T(8,128)(2,1)}, bf16[128,256]{1,0:T(8,128)(2,1)S(1)}, u32[]{:S(2)}) copy-start(bf16[128,256]{1,0:T(8,128)(2,1)S(1)} %collective-permute-done.8.refs_8_.refs_9_) | copy-start | bytes 196612
  24.1 5.1 %collective-permute-start.5 = (bf16[80,768]{1,0:T(8,128)(2,1)S(1)}, bf16[80,768]{1,0:T(8,128)(2,1)S(1)}, u32[]{:S(2)}, u32[]{:S(2)}) collective-permute-start(bf16[80,768]{1,0:T(8,128)(2,1)S(1)} %collective-permute-done.3.refs_4_.refs_3_), channel_id=1, source_target_pairs={{0,2},{1,3},{2,0},{3,1},{4,6},{5,7},{6,4},{7,5},{8,10},{9,11},{10,... | collective-permute-start | bytes 368648 | tf_op jit(solution)/shard_map/ppermute | solution.py:470
  25.2 7.0 %copy-start.1 = (bf16[128,768]{1,0:T(8,128)(2,1)}, bf16[128,768]{1,0:T(8,128)(2,1)S(1)}, u32[]{:S(2)}) copy-start(bf16[128,768]{1,0:T(8,128)(2,1)S(1)} %collective-permute-done.2.refs_3_.refs_2_) | copy-start | bytes 589828
  25.2 5.1 %collective-permute-start.4 = (bf16[80,768]{1,0:T(8,128)(2,1)S(1)}, bf16[80,768]{1,0:T(8,128)(2,1)S(1)}, u32[]{:S(2)}, u32[]{:S(2)}) collective-permute-start(bf16[80,768]{1,0:T(8,128)(2,1)S(1)} %collective-permute-done.3.refs_4_.refs_3_), channel_id=1, source_target_pairs={{0,1},{1,0},{2,3},{3,2},{4,5},{5,4},{6,7},{7,6},{8,9},{9,8},{10,11... | collective-permute-start | bytes 368648 | tf_op jit(solution)/shard_map/ppermute | solution.py:470
  26.5 5.7 %copy-start.15 = (s32[2]{0:T(128)}, s32[2]{0:T(128)S(1)}, u32[]{:S(2)}) copy-start(s32[2]{0:T(128)S(1)} %pad_add_fusion.1.place) | copy-start | bytes 28
  28.3 3.9 %copy-start.8 = (s32[16,16]{1,0:T(8,128)}, s32[16,16]{1,0:T(8,128)S(1)}, u32[]{:S(2)}) copy-start(s32[16,16]{1,0:T(8,128)S(1)} %pad_add_fusion.tables) | copy-start | bytes 3076
  28.4 3.9 %copy-start.2 = (bf16[128,768]{1,0:T(8,128)(2,1)}, bf16[128,768]{1,0:T(8,128)(2,1)S(1)}, u32[]{:S(2)}) copy-start(bf16[128,768]{1,0:T(8,128)(2,1)S(1)} %collective-permute-done.1.refs_2_.refs_1_) | copy-start | bytes 589828
  29.1 3.2 %copy-start.3 = (bf16[128,768]{1,0:T(8,128)(2,1)}, bf16[128,768]{1,0:T(8,128)(2,1)S(1)}, u32[]{:S(2)}) copy-start(bf16[128,768]{1,0:T(8,128)(2,1)S(1)} %collective-permute-done.refs_1_.refs_0_) | copy-start | bytes 589828
  29.1 3.2 %copy-start.5 = (bf16[80,768]{1,0:T(8,128)(2,1)}, bf16[80,768]{1,0:T(8,128)(2,1)S(1)}, u32[]{:S(2)}) copy-start(bf16[80,768]{1,0:T(8,128)(2,1)S(1)} %collective-permute-done.6.refs_7_.refs_6_) | copy-start | bytes 368644
  29.2 3.1 %copy-start.6 = (bf16[80,768]{1,0:T(8,128)(2,1)}, bf16[80,768]{1,0:T(8,128)(2,1)S(1)}, u32[]{:S(2)}) copy-start(bf16[80,768]{1,0:T(8,128)(2,1)S(1)} %collective-permute-done.5.refs_6_.refs_5_) | copy-start | bytes 368644
  30.4 1.9 %copy-start.7 = (bf16[80,768]{1,0:T(8,128)(2,1)}, bf16[80,768]{1,0:T(8,128)(2,1)S(1)}, u32[]{:S(2)}) copy-start(bf16[80,768]{1,0:T(8,128)(2,1)S(1)} %collective-permute-done.4.refs_5_.refs_4_) | copy-start | bytes 368644
  32.2 6.0 %copy-start.21 = (bf16[2,257,768]{2,0,1:T(2,128)(2,1)S(1)}, bf16[2,257,768]{2,0,1:T(2,128)(2,1)}, u32[]{:S(2)}) copy-start(bf16[2,257,768]{2,0,1:T(2,128)(2,1)} %param.16) | copy-start | bytes 2368516
  32.3 24.1 %all-to-all-start.1 = ((bf16[8,72,768]{2,1,0:T(8,128)(2,1)}), bf16[8,72,768]{2,1,0:T(8,128)(2,1)S(1)}, u32[]{:S(2)}, u32[]{:S(2)}) async-start(bf16[8,72,768]{2,1,0:T(8,128)(2,1)} %shard_map.173), calls=%async_computation.1 | async-start | bytes 1769472 | tf_op jit(solution)/shard_map/all_to_all | solution.py:531
  36.3 2.9 %copy-start.22 = (bf16[2,257,768]{2,0,1:T(2,128)(2,1)S(1)}, bf16[2,257,768]{2,0,1:T(2,128)(2,1)}, u32[]{:S(2)}) copy-start(bf16[2,257,768]{2,0,1:T(2,128)(2,1)} %param.17) | copy-start | bytes 2368516
  56.4 4.9 %copy-start.18 = (bf16[8,72,768]{2,1,0:T(8,128)(2,1)}, bf16[8,72,768]{2,1,0:T(8,128)(2,1)S(1)}, u32[]{:S(2)}) copy-start(bf16[8,72,768]{2,1,0:T(8,128)(2,1)S(1)} %all-to-all-done.1.refs_13_) | copy-start | bytes 2654212
  56.4 39.0 %all-to-all-start = ((bf16[8,72,768]{2,1,0:T(8,128)(2,1)}), bf16[8,72,768]{2,1,0:T(8,128)(2,1)S(1)}, u32[]{:S(2)}, u32[]{:S(2)}) async-start(bf16[8,72,768]{2,1,0:T(8,128)(2,1)} %get-tuple-element.29), calls=%async_computation | async-start | bytes 1769472 | tf_op jit(solution)/shard_map/all_to_all | solution.py:564
  61.2 30.2 %copy-start.23 = (bf16[2,4,35,768]{3,2,1,0:T(8,128)(2,1)S(1)}, bf16[2,4,35,768]{3,2,1,0:T(8,128)(2,1)}, u32[]{:S(2)}) copy-start(bf16[2,4,35,768]{3,2,1,0:T(8,128)(2,1)} %get-tuple-element.56) | copy-start | bytes 1290244
  77.9 8.9 %collective-permute-start.11 = (bf16[2,72,768]{2,1,0:T(8,128)(2,1)}, bf16[2,72,768]{2,1,0:T(8,128)(2,1)S(1)}, u32[]{:S(2)}, u32[]{:S(2)}) collective-permute-start(bf16[2,72,768]{2,1,0:T(8,128)(2,1)} %get-tuple-element.35), channel_id=1, source_target_pairs={{0,1},{1,0},{2,3},{3,2},{4,5},{5,4},{6,7},{7,6},{8,9},{9,8},{10,11... | collective-permute-start | bytes 663560 | tf_op jit(solution)/shard_map/ppermute | solution.py:470
  78.0 8.9 %collective-permute-start.12 = (bf16[2,72,768]{2,1,0:T(8,128)(2,1)}, bf16[2,72,768]{2,1,0:T(8,128)(2,1)S(1)}, u32[]{:S(2)}, u32[]{:S(2)}) collective-permute-start(bf16[2,72,768]{2,1,0:T(8,128)(2,1)} %get-tuple-element.36), channel_id=1, source_target_pairs={{0,2},{1,3},{2,0},{3,1},{4,6},{5,7},{6,4},{7,5},{8,10},{9,11},{10,... | collective-permute-start | bytes 663560 | tf_op jit(solution)/shard_map/ppermute | solution.py:470
  78.1 12.3 %collective-permute-start.13 = (bf16[2,72,768]{2,1,0:T(8,128)(2,1)}, bf16[2,72,768]{2,1,0:T(8,128)(2,1)S(1)}, u32[]{:S(2)}, u32[]{:S(2)}) collective-permute-start(bf16[2,72,768]{2,1,0:T(8,128)(2,1)} %get-tuple-element.37), channel_id=1, source_target_pairs={{0,3},{1,2},{2,1},{3,0},{4,7},{5,6},{6,5},{7,4},{8,11},{9,10},{10,... | collective-permute-start | bytes 663560 | tf_op jit(solution)/shard_map/ppermute | solution.py:470
  90.3 0.9 copy-start
  91.3 1.2 %copy-start.20 = (bf16[2,257,768]{2,1,0:T(8,128)(2,1)S(1)}, bf16[2,257,768]{2,1,0:T(8,128)(2,1)}, u32[]{:S(2)}) copy-start(bf16[2,257,768]{2,1,0:T(8,128)(2,1)} %get-tuple-element.59) | copy-start | bytes 2368516
  91.3 2.7 %copy-start.19 = (bf16[2,257,768]{2,1,0:T(8,128)(2,1)S(1)}, bf16[2,257,768]{2,1,0:T(8,128)(2,1)}, u32[]{:S(2)}) copy-start(bf16[2,257,768]{2,1,0:T(8,128)(2,1)} %get-tuple-element.60) | copy-start | bytes 2368516
  91.4 6.3 %collective-permute-start.14 = (bf16[72,768]{1,0:T(8,128)(2,1)S(1)}, bf16[72,768]{1,0:T(8,128)(2,1)S(1)}, u32[]{:S(2)}, u32[]{:S(2)}) collective-permute-start(bf16[72,768]{1,0:T(8,128)(2,1)S(1)} %get-tuple-element.39), channel_id=1, source_target_pairs={{0,4},{1,5},{2,6},{3,7},{4,0},{5,1},{6,2},{7,3},{8,12},{9,13},{10,... | collective-permute-start | bytes 331784 | tf_op jit(solution)/shard_map/ppermute | solution.py:470
  92.4 5.3 %copy-start.9 = (s32[16,16]{1,0:T(8,128)S(1)}, s32[16,16]{1,0:T(8,128)}, u32[]{:S(2)}) copy-start(s32[16,16]{1,0:T(8,128)} %copy-done.8) | copy-start | bytes 3076
  92.4 5.3 %copy-start.16 = (s32[2]{0:T(128)S(1)}, s32[2]{0:T(128)}, u32[]{:S(2)}) copy-start(s32[2]{0:T(128)} %copy-done.15) | copy-start | bytes 28

commit v4 on v3

--- a/solution.py
+++ b/solution.py
@@ -21,12 +21,12 @@
 CHUNK = 3
 
 
-def kernel_call(body, out_shape, n_smem, n_any, scratch=(), flops=0, nbytes=0, space=ANY, mib=60, n_after=0, **more):
+def kernel_call(body, out_shape, n_smem, n_any, scratch=(), flops=0, nbytes=0, space=ANY, mib=60, n_after=0, outs=None, **more):
     return pl.pallas_call(
         body,
         out_shape=out_shape,
         in_specs=[SMEM] * n_smem + [space] * n_any + [ANY] * n_after,
-        out_specs=jax.tree.map(lambda _: space, out_shape),
+        out_specs=outs if outs is not None else jax.tree.map(lambda _: space, out_shape),
         scratch_shapes=list(scratch),
         compiler_params=pltpu.CompilerParams(vmem_limit_bytes=mib * 1024 * 1024),
         cost_estimate=pl.CostEstimate(flops=flops, bytes_accessed=nbytes, transcendentals=0),
@@ -67,16 +67,20 @@
     )(value, *others)
 
 
-def pack_body(queries, pictures, packed, both):
+def pack_body(queries, packed):
     captions, caption = queries.shape[:2]
+    pieces = [queries[row].astype(F32) for row in range(captions)]
+    pieces.append(jnp.zeros((packed.shape[0] - captions * caption, packed.shape[1]), F32))
+    packed[...] = jnp.concatenate(pieces, axis=0).astype(BF16)
+
+
+def both_body(packed, pictures, both, again):
     first, emb = packed.shape[0], pictures.shape[1]
-    pieces = [queries[row].astype(F32) for row in range(captions)]
-    pieces.append(jnp.zeros((first - captions * caption, packed.shape[1]), F32))
-    packed[...] = jnp.concatenate(pieces, axis=0).astype(BF16)
     both[0:first, :] = packed[...]
     both[first:, :] = jnp.zeros((both.shape[0] - first, packed.shape[1]), BF16)
     for fold, (start, count) in enumerate(folds(pictures.shape, packed.shape[1])):
         both[first : first + count, fold * emb : (fold + 1) * emb] = pictures[start : start + count]
+    again[...] = pictures[...]
 
 
 def fold_rows(shape, width):
@@ -93,10 +97,10 @@
     return tables[first + entry, row], tables[first + NEGS + entry, row]
 
 
-def send_body(tables, place, cots, *refs):
-    sent = refs[-1]
+def send_body(tables, place, cots, sent, blocks, sems):
     rows, caption = cots.shape[0], cots.shape[2]
-    for part in range(sent.shape[0]):
+    copies = []
+    for part in range(blocks.shape[0]):
         pieces = []
         for row in range(rows):
             at = jnp.int32(0)
@@ -104,8 +108,10 @@
                 owner, _ = named(tables, 1, place[0] * rows + row, entry)
                 at = jnp.where(owner == part, entry, at)
             pieces.append(cots[row, at].astype(F32))
-        pieces.append(jnp.zeros((sent.shape[1] - rows * caption, sent.shape[2]), F32))
-        sent[part] = jnp.concatenate(pieces, axis=0).astype(BF16)
+        pieces.append(jnp.zeros((blocks.shape[1] - rows * caption, blocks.shape[2]), F32))
+        blocks[part] = jnp.concatenate(pieces, axis=0).astype(BF16)
+        copies += start_copies([(blocks.at[part], sent.at[part])], sems, part)
+    wait_copies(copies)
 
 
 def in_pieces(values):
@@ -295,21 +301,34 @@
     lax.fori_loop(0, (sum(needed) + 1) // 2, pair_step, 0)
 
 
-def image_body(n_parts, tables, place, *refs):
-    parts, refs = refs[:n_parts], refs[n_parts:]
-    (cots_in, keys_in, values_in, image_out, image_terms, key_out, value_out, text_out,
+def image_body(n_parts, tables, place, softness, *refs):
+    half = n_parts // 2
+    parts, pictures, refs = refs[:n_parts], refs[n_parts : n_parts + half], refs[n_parts + half :]
+    (texts, cots_in, keys_in, values_in, image_out, image_terms, key_out, value_out, text_out, row_out, col_out,
      held, queries, cots_held, cots, keys, values, image_outs, terms, sums, outs, blocks,
-     lists, counts, sems) = refs
+     near_in, images_in, texts_in, unit_images, unit_texts, row_stats, col_stats, lists, counts, sems) = refs
     images = captions = keys.shape[0]
     caption = cots_held.shape[2]
     rows = queries.shape[1]
     everyone = n_parts * captions
+    soon = start_copies(
+        [(texts, texts_in)]
+        + [(part.at[pl.ds(held.shape[1], near_in.shape[1])], near_in.at[n]) for n, part in enumerate(parts[:half])]
+        + [(picture, images_in.at[half + n]) for n, picture in enumerate(pictures)],
+        sems,
+    )
     copies = start_copies(
-        query_copies(parts, held) + [(cots_in, cots_held), (keys_in, keys), (values_in, values)], sems
+        query_copies(parts, held) + [(cots_in, cots_held), (keys_in, keys), (values_in, values)],
+        sems,
+        len(soon),
     )
     find_listed(tables, place, lists, counts, everyone)
     for total in (*sums, outs):
         total[...] = jnp.zeros_like(total)
+    wait_copies(soon)
+    contrast(
+        n_parts, place, softness, near_in, images_in, texts_in, unit_images, unit_texts, row_stats, col_stats
+    )
     wait_copies(copies)
     widen_queries(held, queries, captions, caption)
     for image in range(images):
@@ -336,7 +355,9 @@
             )
         attend(chunks, queries, cots, keys, values, sums)
     copies = start_copies(
-        [(image_outs, image_out), (terms, image_terms), *zip(sums, (key_out, value_out))], sems
+        [(image_outs, image_out), (terms, image_terms), *zip(sums, (key_out, value_out))]
+        + [(row_stats, row_out), (col_stats, col_out)],
+        sems,
     )
 
     def work(chunks):
@@ -357,43 +378,34 @@
         pieces = [outs[part * captions + row, 0:caption, :] for row in range(captions)]
         pieces.append(jnp.zeros((blocks.shape[1] - captions * caption, blocks.shape[2]), F32))
         blocks[part] = jnp.concatenate(pieces, axis=0).astype(BF16)
-        copies += start_copies([(blocks.at[part], text_out.at[part])], sems, 4 + part)
+        copies += start_copies([(blocks.at[part], text_out.at[part])], sems, 6 + part)
     wait_copies(copies)
 
 
-def text_body(n_parts, tables, place, softness, *refs):
+def text_body(n_parts, tables, place, *refs):
     half = n_parts // 2
-    parts, pictures, refs = refs[:n_parts], refs[n_parts : n_parts + half], refs[n_parts + half :]
-    (texts, cots_in, keys_in, values_in, terms_in, key_in, value_in), refs = refs[:7], refs[7:]
+    parts, refs = refs[:n_parts], refs[n_parts:]
+    (cots_in, keys_in, values_in, stats_in, terms_in, key_in, value_in), refs = refs[:7], refs[7:]
     q_out, refs = refs[:half], refs[half:]
-    (key_grad, value_grad, col_out,
-     held, queries, cots_held, cots, keys, values, terms, q_sum, firsts, sums, grads,
-     near_in, images_in, texts_in, unit_images, unit_texts, row_stats, col_stats, lists, counts, sems) = refs
+    (key_grad, value_grad,
+     held, queries, cots_held, cots, keys, values, row_stats, terms, q_sum, firsts, sums, grads,
+     lists, counts, sems) = refs
     images = captions = keys.shape[0]
     caption = terms.shape[2]
     rows = queries.shape[1]
     everyone = n_parts * captions
-    soon = start_copies(
-        [(texts, texts_in)]
-        + [(part.at[pl.ds(held.shape[1], near_in.shape[1])], near_in.at[n]) for n, part in enumerate(parts[:half])]
-        + [(picture, images_in.at[half + n]) for n, picture in enumerate(pictures)],
-        sems,
-    )
     copies = start_copies(
         query_copies(parts, held) + [(cots_in, cots_held), (keys_in, keys), (values_in, values)],
         sems,
-        len(soon),
     )
     find_listed(tables, place, lists, counts, everyone)
     for total in (*sums, q_sum):
         total[...] = jnp.zeros_like(total)
-    wait_copies(soon)
-    contrast(
-        n_parts, place, softness, near_in, images_in, texts_in, unit_images, unit_texts, row_stats, col_stats
-    )
     wait_copies(copies)
-    later = start_copies([(terms_in, terms), *zip((key_in, value_in), firsts)], sems)
-    out = start_copies([(col_stats, col_out)], sems, len(soon))
+    later = start_copies(
+        [(stats_in, row_stats), (terms_in, terms), *zip((key_in, value_in), firsts)], sems
+    )
+    out = []
     widen_queries(held, queries, captions, caption)
     for part in range(n_parts):
         widen_block(cots_held[part].astype(F32), cots, part * captions, captions, caption)
@@ -448,7 +460,7 @@
         out[...] = jnp.concatenate([total, in_pieces([lse, diag]), rest], axis=0).astype(out.dtype)
 
 
-def join_body(tables, place, got_out, kept, got_q, cols, pair_out, q_grad, image_loss, text_loss):
+def pair_out_body(tables, place, got_out, pair_out):
     rows, caption = pair_out.shape[0], pair_out.shape[2]
     for row in range(rows):
         lines = slice(row * caption, (row + 1) * caption)
@@ -456,6 +468,10 @@
             owner, _ = named(tables, 1, place[0] * rows + row, entry)
             block = got_out[owner].astype(F32)
             pair_out[row, entry] = block[lines].astype(BF16)
+
+
+def join_body(kept, got_q, cols, q_grad, image_loss, text_loss):
+    rows, caption = q_grad.shape[:2]
     total, lse, diag = add_lines([kept[...], got_q[...]], rows * caption)
     for row in range(rows):
         q_grad[row] = total[row * caption : (row + 1) * caption].astype(BF16)
@@ -511,28 +527,36 @@
     lists = [pltpu.SMEM((local, everyone + 2 * CHUNK), jnp.int32), pltpu.SMEM((local,), jnp.int32)]
 
     step = fold_rows(pictures.shape, width)
-    packed, both = kernel_call(
-        pack_body,
-        (shape((query_rows, width), BF16), shape((query_rows + step, width), BF16)),
+    packed = kernel_call(pack_body, shape((query_rows, width), BF16), 0, 1, space=VMEM, mib=8)(queries)
+    both, again = kernel_call(
+        both_body,
+        (shape((query_rows + step, width), BF16), shape(pictures.shape, BF16)),
         0,
         2,
         space=VMEM,
         mib=8,
-    )(queries, pictures)
+    )(packed, pictures)
     other = swap(packed, "txt", half)
     near = [both] + [swap(both, "txt", mask) for mask in range(1, half)]
     parts = near + [other] + [swap(other, "txt", mask) for mask in range(1, half)]
-    other_pictures = swap(pictures, "txt", half)
+    other_pictures = swap(again, "txt", half)
     far_pictures = [other_pictures] + [swap(other_pictures, "txt", mask) for mask in range(1, half)]
-    after = (*parts[1:], *far_pictures)
     sent = kernel_call(
-        send_body, shape(block_shape, BF16), 2, 1, space=VMEM, mib=12, n_after=len(after)
-    )(tables, place, txt_cots, *after)
-    got_cots = lax.all_to_all(sent, "txt", 0, 0, tiled=True)
+        send_body,
+        shape(block_shape, BF16),
+        2,
+        1,
+        [vmem(block_shape, BF16), dma(n_txt)],
+        space=VMEM,
+        mib=12,
+        outs=ANY,
+    )(tables, place, txt_cots)
+    ready = tie(sent, *parts[1:], *far_pictures, keys, values, img_cots)
+    got_cots = lax.all_to_all(ready, "txt", 0, 0, tiled=True)
 
     image_rows, n_texts, emb = pictures.shape[0], wordings.shape[0], wordings.shape[1]
     stats_shape = (n_txt, 1, 6 * image_rows)
-    img_pair_out, image_terms, key_part, value_part, out = kernel_call(
+    img_pair_out, image_terms, key_part, value_part, out, row_stats, col_stats = kernel_call(
         functools.partial(image_body, n_txt),
         (
             shape(img_cots.shape, BF16),
@@ -540,9 +564,11 @@
             shape(keys.shape, F32),
             shape(values.shape, F32),
             shape(block_shape, BF16),
+            shape(stats_shape, F32),
+            shape((2, n_texts), F32),
         ),
-        2,
-        n_txt + 3,
+        3,
+        n_txt + half + 4,
         [
             vmem(held_shape, BF16),
             vmem(wide_shape, F32),
@@ -555,32 +581,6 @@
             sums,
             vmem(wide_shape, F32),
             vmem(block_shape, BF16),
-            *lists,
-            dma(n_txt + 4),
-        ],
-        flops=6 * local * NEGS * pair_flops,
-        nbytes=12_000_000,
-    )(tables, place, *parts, img_cots, keys, values)
-    got_out = lax.all_to_all(out, "txt", 0, 0, tiled=True)
-
-    *q_out, key_grad, value_grad, col_stats = kernel_call(
-        functools.partial(text_body, n_txt),
-        [shape((2,) + block_shape[1:], BF16)] * half
-        + [shape(keys.shape, BF16), shape(values.shape, BF16), shape((2, n_texts), F32)],
-        3,
-        n_txt + half + 7,
-        [
-            vmem(held_shape, BF16),
-            vmem(wide_shape, F32),
-            vmem(block_shape, BF16),
-            vmem(wide_shape, F32),
-            vmem(keys.shape, BF16),
-            vmem(values.shape, BF16),
-            vmem(img_cots.shape, BF16),
-            vmem(wide_shape, F32),
-            sums,
-            sums,
-            [vmem(keys.shape, BF16), vmem(values.shape, BF16)],
             vmem((half, step, width), BF16),
             vmem((n_txt,) + pictures.shape, BF16),
             vmem(wordings.shape, BF16),
@@ -589,13 +589,39 @@
             vmem(stats_shape, F32),
             vmem((2, n_texts), F32),
             *lists,
+            dma(2 * n_txt + 6),
+        ],
+        flops=6 * local * NEGS * pair_flops,
+        nbytes=12_000_000,
+    )(tables, place, softness, *parts, *far_pictures, wordings, img_cots, keys, values)
+    got_out = lax.all_to_all(out, "txt", 0, 0, tiled=True)
+
+    *q_out, key_grad, value_grad = kernel_call(
+        functools.partial(text_body, n_txt),
+        [shape((2,) + block_shape[1:], BF16)] * half
+        + [shape(keys.shape, BF16), shape(values.shape, BF16)],
+        2,
+        n_txt + 7,
+        [
+            vmem(held_shape, BF16),
+            vmem(wide_shape, F32),
+            vmem(block_shape, BF16),
+            vmem(wide_shape, F32),
+            vmem(keys.shape, BF16),
+            vmem(values.shape, BF16),
+            vmem(stats_shape, F32),
+            vmem(img_cots.shape, BF16),
+            vmem(wide_shape, F32),
+            sums,
+            sums,
+            [vmem(keys.shape, BF16), vmem(values.shape, BF16)],
+            *lists,
             dma(2 * n_txt + 4),
         ],
         flops=4 * local * NEGS * pair_flops,
         nbytes=10_000_000,
     )(
-        tables, place, softness, *parts, *far_pictures, wordings, got_cots, keys, values,
-        image_terms, key_part, value_part,
+        tables, place, *parts, got_cots, keys, values, row_stats, image_terms, key_part, value_part
     )
     got_cols = lax.all_gather(tie(col_stats, q_out[0]), "img", axis=0)
     near = [q_out[0]] + [swap(block, "txt", 1 + n) for n, block in enumerate(q_out[1:])]
@@ -610,19 +636,18 @@
     )(got_cols, *near)
     got_q = swap(across, "txt", half)
 
-    txt_pair_out, query_grad, image_loss, text_loss = kernel_call(
+    txt_pair_out = kernel_call(
+        pair_out_body, shape(txt_cots.shape, BF16), 2, 1, space=VMEM, mib=12, nbytes=2_000_000
+    )(tables, place, got_out)
+    query_grad, image_loss, text_loss = kernel_call(
         join_body,
-        (
-            shape(txt_cots.shape, BF16),
-            shape(queries.shape, BF16),
-            shape((1, image_rows), F32),
-            shape((1, n_texts), F32),
-        ),
-        2,
-        4,
+        (shape(queries.shape, BF16), shape((1, image_rows), F32), shape((1, n_texts), F32)),
+        0,
+        3,
         space=VMEM,
-        mib=16,
-    )(tables, place, got_out, kept, got_q, got_cols)
+        mib=12,
+        nbytes=1_000_000,
+    )(kept, got_q, got_cols)
     return (
         image_loss.reshape(-1),
         text_loss.reshape(-1),

time: 101 us -> 97.8 us (0.968)
  Pallas kernels: 35.8 us -> 26.6 us
  starting transfers between devices: 31.5 us -> 38.3 us
  local copies, waits for them, and re-layouts: 13.3 us -> 14.6 us
  waiting for transfers between devices: 12.3 us -> 11.2 us
    pallas_call x1, Pallas kernels: 16.6 us -> 8.62 us  [on_device(): kernel_call(functools.partial(text_body, n_txt), [shape((2,) + block_shap...]
    ppermute x15, starting transfers between devices: 23.3 us -> 30.2 us  [swap(): lax.ppermute(part, axis, [(s, s ^ mask) for s in range(lax.axis_size(axis...]
    ppermute x15, waiting for transfers between devices: 12 us -> 8.08 us  [swap(): lax.ppermute(part, axis, [(s, s ^ mask) for s in range(lax.axis_size(axis...]
    all_to_all x1, waiting for transfers between devices: 0.21 us -> 3.09 us  [on_device(): got_cots = lax.all_to_all(ready, 'txt', 0, 0, tiled=True)]
    pallas_call x1, Pallas kernels: 16 us -> 14.3 us  [on_device(): kernel_call(functools.partial(image_body, n_txt), (shape(img_cots.shape,...]
    unnamed x58 -> x70, local copies, waits for them, and re-layouts: 13.3 us -> 14.6 us
    pallas_call x3 -> x5, Pallas kernels: 3.08 us -> 3.58 us  [the longest x1 2.17 us: on_device(): kernel_call(send_body, shape(block_shape, BF16), 2, 1, [vmem(block_shape,...]
  transfers between devices with their start and end apart: 17 -> 17, of which waited for: 8 -> 5; matrix products, arithmetic and copies ran while one was open for 10% -> 9% of each run, Pallas kernels for 33% -> 27%
where the time goes in v4:
time: 97.8 us; the launch traced here: 97.7 us
  starting transfers between devices  38.3 us (39%)
  Pallas kernels  26.6 us (27%)
  local copies, waits for them, and re-layouts  14.6 us (15%)
  waiting for transfers between devices  11.2 us (11%)
  blocking collectives  5.36 us (5%)
  between operations  1.61 us (2%)
    ppermute x15, starting transfers between devices, swap(): lax.ppermute(part, axis, [(s, s ^ mask) for s in range(lax.axis_size(axis...  30.2 us
    unnamed x70, local copies, waits for them, and re-layouts  14.6 us
    pallas_call x1, Pallas kernels, on_device(): kernel_call(functools.partial(image_body, n_txt), (shape(img_cots.shape,...  14.3 us
    pallas_call x1, Pallas kernels, on_device(): kernel_call(functools.partial(text_body, n_txt), [shape((2,) + block_shap...  8.62 us
    ppermute x15, waiting for transfers between devices, swap(): lax.ppermute(part, axis, [(s, s ^ mask) for s in range(lax.axis_size(axis...  8.08 us
    all_gather x1, blocking collectives, on_device(): got_cols = lax.all_gather(tie(col_stats, q_out[0]), 'img', axis=0)  5.36 us
    all_to_all x1, starting transfers between devices, on_device(): got_out = lax.all_to_all(out, 'txt', 0, 0, tiled=True)  4.52 us
    all_to_all x1, starting transfers between devices, on_device(): got_cots = lax.all_to_all(ready, 'txt', 0, 0, tiled=True)  3.55 us
  transfers between devices with their start and end apart: 17, of which 5 were waited for; matrix products, arithmetic and copies ran while one was open for 9% of the time, Pallas kernels for 27%

profile of v4, /device:TPU:0, one launch (start us, length us, event | category | flops | bytes accessed | tf_op | source)
XLA Modules:
  0.0 97.7 jit_solution(13359004967762106944)
XLA Ops:
  0.6 1.0 copy.36.queries
  1.6 0.8 copy-done.4
  2.5 4.0 %collective-permute-start.2 = (bf16[128,768]{1,0:T(8,128)(2,1)S(1)}, bf16[128,768]{1,0:T(8,128)(2,1)S(1)}, u32[]{:S(2)}, u32[]{:S(2)}) collective-permute-start(bf16[128,768]{1,0:T(8,128)(2,1)S(1)} %get-tuple-element.27.refs_0_), channel_id=1, source_target_pairs={{0,3},{1,2},{2,1},{3,0},{4,7},{5,6},{6,5},{7,4},{8,11},{9,10},{10,... | collective-permute-start | bytes 589832 | tf_op jit(solution)/shard_map/ppermute | solution.py:486
  6.5 2.6 %collective-permute-start.7 = (bf16[128,256]{1,0:T(8,128)(2,1)S(1)}, bf16[128,256]{1,0:T(8,128)(2,1)S(1)}, u32[]{:S(2)}, u32[]{:S(2)}) collective-permute-start(bf16[128,256]{1,0:T(8,128)(2,1)S(1)} %get-tuple-element.28), channel_id=1, source_target_pairs={{0,4},{1,5},{2,6},{3,7},{4,0},{5,1},{6,2},{7,3},{8,12},{9,13},{10,... | collective-permute-start | bytes 196616 | tf_op jit(solution)/shard_map/ppermute | solution.py:486
  9.1 0.3 collective-permute-start.3
  9.5 3.8 %collective-permute-done.7.refs_8_ = bf16[128,256]{1,0:T(8,128)(2,1)S(1)} collective-permute-done((bf16[128,256]{1,0:T(8,128)(2,1)S(1)}, bf16[128,256]{1,0:T(8,128)(2,1)S(1)}, u32[]{:S(2)}, u32[]{:S(2)}) %collective-permute-start.7) | collective-permute-done | bytes 65568 | tf_op jit(solution)/shard_map/ppermute | solution.py:486
  13.3 3.5 %collective-permute-start.10 = (bf16[128,256]{1,0:T(8,128)(2,1)S(1)}, bf16[128,256]{1,0:T(8,128)(2,1)S(1)}, u32[]{:S(2)}, u32[]{:S(2)}) collective-permute-start(bf16[128,256]{1,0:T(8,128)(2,1)S(1)} %collective-permute-done.7.refs_8_), channel_id=1, source_target_pairs={{0,3},{1,2},{2,1},{3,0},{4,7},{5,6},{6,5},{7,4},{8,11},{9,10},{10,... | collective-permute-start | bytes 196616 | tf_op jit(solution)/shard_map/ppermute | solution.py:486
  16.8 0.1 collective-permute-start.9
  16.9 1.4 %collective-permute-start.8 = (bf16[128,256]{1,0:T(8,128)(2,1)S(1)}, bf16[128,256]{1,0:T(8,128)(2,1)S(1)}, u32[]{:S(2)}, u32[]{:S(2)}) collective-permute-start(bf16[128,256]{1,0:T(8,128)(2,1)S(1)} %collective-permute-done.7.refs_8_), channel_id=1, source_target_pairs={{0,1},{1,0},{2,3},{3,2},{4,5},{5,4},{6,7},{7,6},{8,9},{9,8},{10,11... | collective-permute-start | bytes 196616 | tf_op jit(solution)/shard_map/ppermute | solution.py:486
  18.3 2.0 %collective-permute-start.1 = (bf16[128,768]{1,0:T(8,128)(2,1)S(1)}, bf16[128,768]{1,0:T(8,128)(2,1)S(1)}, u32[]{:S(2)}, u32[]{:S(2)}) collective-permute-start(bf16[128,768]{1,0:T(8,128)(2,1)S(1)} %get-tuple-element.27.refs_0_), channel_id=1, source_target_pairs={{0,2},{1,3},{2,0},{3,1},{4,6},{5,7},{6,4},{7,5},{8,10},{9,11},{10,... | collective-permute-start | bytes 589832 | tf_op jit(solution)/shard_map/ppermute | solution.py:486
  20.3 1.0 collective-permute-start
  21.3 0.5 collective-permute-done.9.refs_10_
  21.8 2.4 %collective-permute-start.6 = (bf16[80,768]{1,0:T(8,128)(2,1)S(1)}, bf16[80,768]{1,0:T(8,128)(2,1)S(1)}, u32[]{:S(2)}, u32[]{:S(2)}) collective-permute-start(bf16[80,768]{1,0:T(8,128)(2,1)S(1)} %collective-permute-done.3.refs_4_), channel_id=1, source_target_pairs={{0,3},{1,2},{2,1},{3,0},{4,7},{5,6},{6,5},{7,4},{8,11},{9,10},{10,... | collective-permute-start | bytes 368648 | tf_op jit(solution)/shard_map/ppermute | solution.py:486
  24.2 1.1 %collective-permute-start.5 = (bf16[80,768]{1,0:T(8,128)(2,1)S(1)}, bf16[80,768]{1,0:T(8,128)(2,1)S(1)}, u32[]{:S(2)}, u32[]{:S(2)}) collective-permute-start(bf16[80,768]{1,0:T(8,128)(2,1)S(1)} %collective-permute-done.3.refs_4_), channel_id=1, source_target_pairs={{0,2},{1,3},{2,0},{3,1},{4,6},{5,7},{6,4},{7,5},{8,10},{9,11},{10,... | collective-permute-start | bytes 368648 | tf_op jit(solution)/shard_map/ppermute | solution.py:486
  25.3 1.2 %collective-permute-start.4 = (bf16[80,768]{1,0:T(8,128)(2,1)S(1)}, bf16[80,768]{1,0:T(8,128)(2,1)S(1)}, u32[]{:S(2)}, u32[]{:S(2)}) collective-permute-start(bf16[80,768]{1,0:T(8,128)(2,1)S(1)} %collective-permute-done.3.refs_4_), channel_id=1, source_target_pairs={{0,1},{1,0},{2,3},{3,2},{4,5},{5,4},{6,7},{7,6},{8,9},{9,8},{10,11... | collective-permute-start | bytes 368648 | tf_op jit(solution)/shard_map/ppermute | solution.py:486
  26.5 0.1 pad_add_fusion.1.place
  26.6 1.9 %copy.37.refs_13_.refs_14_ = bf16[2,4,35,768]{3,2,1,0:T(8,128)(2,1)} copy(bf16[2,4,35,768]{3,1,2,0:T(4,128)(2,1)} %param.22) | data formatting | bytes 860160 | tf_op args[10]
  28.5 0.1 copy.40.cots
  28.7 1.0 %copy.38.refs_14_.refs_12_.refs_9_ = bf16[2,257,768]{2,1,0:T(8,128)(2,1)} copy(bf16[2,257,768]{2,0,1:T(2,128)(2,1)S(1)} %copy-done.11) | data formatting | bytes 1579008 | tf_op args[4]
  29.7 1.0 %copy.39.refs_15_.refs_13_.refs_10_ = bf16[2,257,768]{2,1,0:T(8,128)(2,1)} copy(bf16[2,257,768]{2,0,1:T(2,128)(2,1)S(1)} %copy-done.12) | data formatting | bytes 1579008 | tf_op args[5]
  30.7 2.2 %shard_map.174.refs_0_ = bf16[8,72,768]{2,1,0:T(8,128)(2,1)S(1)} custom-call(s32[16,16]{1,0:T(8,128)S(1)} %pad_add_fusion.tables, s32[2]{0:T(128)S(1)} %pad_add_fusion.1.place, bf16[2,4,35,768]{3,2,1,0:T(8,128)(2,1)S(1)} %copy.40.cots), custom_call_target="tpu_custom_call" | custom-call | tf_op jit(solution)/shard_map/pallas_call | solution.py:544
  32.9 0.9 copy-done
  33.9 0.6 copy-done.16
  34.5 0.1 copy-done.17
  34.6 0.0 copy-done.19
  34.6 0.0 copy-done.20
  34.7 0.6 copy-done.21
  35.3 3.6 %all-to-all-start = ((bf16[8,72,768]{2,1,0:T(8,128)(2,1)}), bf16[8,72,768]{2,1,0:T(8,128)(2,1)S(1)}, u32[]{:S(2)}, u32[]{:S(2)}) async-start(bf16[8,72,768]{2,1,0:T(8,128)(2,1)} %shard_map.175), calls=%async_computation | async-start | bytes 1769472 | tf_op jit(solution)/shard_map/all_to_all | solution.py:555
  39.5 14.3 %shard_map.173 = (bf16[2,4,35,768]{3,2,1,0:T(8,128)(2,1)}, bf16[2,4,35,768]{3,2,1,0:T(8,128)(2,1)}, f32[2,257,768]{2,1,0:T(8,128)}, f32[2,257,768]{2,1,0:T(8,128...) custom-call(s32[16,16]{1,0:T(8,128)} %copy-done.2, s32[2]{0:T(128)} %copy-done.5, ...), custom_call_target="tpu_custom_call" | custom-call | flops 3315916800 | bytes 12000000 | tf_op jit(solution)/shard_map/pallas_call | solution.py:559
  53.8 3.1 %all-to-all-done.refs_8_ = bf16[8,72,768]{2,1,0:T(8,128)(2,1)S(1)} async-done(((bf16[8,72,768]{2,1,0:T(8,128)(2,1)}), bf16[8,72,768]{2,1,0:T(8,128)(2,1)S(1)}, u32[]{:S(2)}, u32[]{:S(2)}) %all-to-all-start) | async-done | bytes 884768 | tf_op jit(solution)/shard_map/all_to_all | solution.py:555
  56.9 4.5 %all-to-all-start.1 = ((bf16[8,72,768]{2,1,0:T(8,128)(2,1)}), bf16[8,72,768]{2,1,0:T(8,128)(2,1)S(1)}, u32[]{:S(2)}, u32[]{:S(2)}) async-start(bf16[8,72,768]{2,1,0:T(8,128)(2,1)} %get-tuple-element.43), calls=%async_computation.1 | async-start | bytes 1769472 | tf_op jit(solution)/shard_map/all_to_all | solution.py:597
  61.4 8.6 %shard_map.176 = (bf16[2,72,768]{2,1,0:T(8,128)(2,1)}, bf16[2,72,768]{2,1,0:T(8,128)(2,1)}, bf16[2,72,768]{2,1,0:T(8,128)(2,1)}, bf16[2,72,768]{2,1,0:T(8,128)(2...) custom-call(s32[16,16]{1,0:T(8,128)} %copy-done.2, s32[2]{0:T(128)} %copy-done.5, ...), custom_call_target="tpu_custom_call" | custom-call | flops 2210611200 | bytes 10000000 | tf_op jit(solution)/shard_map/pallas_call | solution.py:599
  70.0 5.5 %collective-permute-start.11 = (bf16[2,72,768]{2,1,0:T(8,128)(2,1)}, bf16[2,72,768]{2,1,0:T(8,128)(2,1)S(1)}, u32[]{:S(2)}, u32[]{:S(2)}) collective-permute-start(bf16[2,72,768]{2,1,0:T(8,128)(2,1)} %get-tuple-element.35), channel_id=1, source_target_pairs={{0,1},{1,0},{2,3},{3,2},{4,5},{5,4},{6,7},{7,6},{8,9},{9,8},{10,11... | collective-permute-start | bytes 663560 | tf_op jit(solution)/shard_map/ppermute | solution.py:486
  75.6 3.5 %collective-permute-start.12 = (bf16[2,72,768]{2,1,0:T(8,128)(2,1)}, bf16[2,72,768]{2,1,0:T(8,128)(2,1)S(1)}, u32[]{:S(2)}, u32[]{:S(2)}) collective-permute-start(bf16[2,72,768]{2,1,0:T(8,128)(2,1)} %get-tuple-element.36), channel_id=1, source_target_pairs={{0,2},{1,3},{2,0},{3,1},{4,6},{5,7},{6,4},{7,5},{8,10},{9,11},{10,... | collective-permute-start | bytes 663560 | tf_op jit(solution)/shard_map/ppermute | solution.py:486
  79.1 1.4 %collective-permute-start.13 = (bf16[2,72,768]{2,1,0:T(8,128)(2,1)}, bf16[2,72,768]{2,1,0:T(8,128)(2,1)S(1)}, u32[]{:S(2)}, u32[]{:S(2)}) collective-permute-start(bf16[2,72,768]{2,1,0:T(8,128)(2,1)} %get-tuple-element.37), channel_id=1, source_target_pairs={{0,3},{1,2},{2,1},{3,0},{4,7},{5,6},{6,5},{7,4},{8,11},{9,10},{10,... | collective-permute-start | bytes 663560 | tf_op jit(solution)/shard_map/ppermute | solution.py:486
  80.5 5.4 %all-gather.1.after.cols = f32[4,2,512]{2,1,0:T(2,128)S(1)} all-gather(f32[1,2,512]{2,1,0:T(2,128)} %bitcast.9), channel_id=2, replica_groups=mesh['img'=4,'txt'=8] {'img'}, dimensions={0}, use_global_device_ids=true | all-gather | bytes 20480 | tf_op jit(solution)/shard_map/all_gather | solution.py:626
  85.8 2.6 %collective-permute-done.13.refs_3_ = bf16[2,72,768]{2,1,0:T(8,128)(2,1)S(1)} collective-permute-done((bf16[2,72,768]{2,1,0:T(8,128)(2,1)}, bf16[2,72,768]{2,1,0:T(8,128)(2,1)S(1)}, u32[]{:S(2)}, u32[]{:S(2)}) %collective-permute-start.13) | collective-permute-done | bytes 221216 | tf_op jit(solution)/shard_map/ppermute | solution.py:486
  88.5 0.9 copy-done.1
  89.4 0.1 shard_map.178
  89.5 0.1 collective-permute-start.14
  89.6 0.9 copy.46
  90.6 0.8 shard_map.180
  91.3 0.9 copy.47
  92.3 1.5 %copy.49 = bf16[2,257,768]{2,0,1:T(2,128)(2,1)} copy(bf16[2,257,768]{2,1,0:T(8,128)(2,1)S(1)} %copy-done.10) | data formatting | bytes 1579008
  93.8 1.5 %copy.50 = bf16[2,257,768]{2,0,1:T(2,128)(2,1)} copy(bf16[2,257,768]{2,1,0:T(8,128)(2,1)S(1)} %copy-done.9) | data formatting | bytes 1579008
  95.3 1.1 %collective-permute-done.14.got_q = bf16[72,768]{1,0:T(8,128)(2,1)S(1)} collective-permute-done((bf16[72,768]{1,0:T(8,128)(2,1)S(1)}, bf16[72,768]{1,0:T(8,128)(2,1)S(1)}, u32[]{:S(2)}, u32[]{:S(2)}) %collective-permute-start.14) | collective-permute-done | bytes 110624 | tf_op jit(solution)/shard_map/ppermute | solution.py:486
  96.4 0.6 shard_map.179
  97.0 0.7 copy.48
  (69 shorter events, 0.2 us)
Async XLA Ops:
  0.6 27.9 %copy-start.14 = (bf16[2,4,35,768]{3,1,2,0:T(4,128)(2,1)S(1)}, bf16[2,4,35,768]{3,1,2,0:T(4,128)(2,1)}, u32[]{:S(2)}) copy-start(bf16[2,4,35,768]{3,1,2,0:T(4,128)(2,1)} %param.23) | copy-start | bytes 1290244
  1.6 0.8 copy-start.4
  2.5 26.1 %copy-start.11 = (bf16[2,257,768]{2,0,1:T(2,128)(2,1)S(1)}, bf16[2,257,768]{2,0,1:T(2,128)(2,1)}, u32[]{:S(2)}) copy-start(bf16[2,257,768]{2,0,1:T(2,128)(2,1)} %param.16) | copy-start | bytes 2368516
  2.5 27.1 %copy-start.7 = (bf16[128,768]{1,0:T(8,128)(2,1)}, bf16[128,768]{1,0:T(8,128)(2,1)S(1)}, u32[]{:S(2)}) copy-start(bf16[128,768]{1,0:T(8,128)(2,1)S(1)} %get-tuple-element.27.refs_0_) | copy-start | bytes 589828
  2.5 22.8 %collective-permute-start.2 = (bf16[128,768]{1,0:T(8,128)(2,1)S(1)}, bf16[128,768]{1,0:T(8,128)(2,1)S(1)}, u32[]{:S(2)}, u32[]{:S(2)}) collective-permute-start(bf16[128,768]{1,0:T(8,128)(2,1)S(1)} %get-tuple-element.27.refs_0_), channel_id=1, source_target_pairs={{0,3},{1,2},{2,1},{3,0},{4,7},{5,6},{6,5},{7,4},{8,11},{9,10},{10,... | collective-permute-start | bytes 589832 | tf_op jit(solution)/shard_map/ppermute | solution.py:486
  6.5 6.8 %collective-permute-start.7 = (bf16[128,256]{1,0:T(8,128)(2,1)S(1)}, bf16[128,256]{1,0:T(8,128)(2,1)S(1)}, u32[]{:S(2)}, u32[]{:S(2)}) collective-permute-start(bf16[128,256]{1,0:T(8,128)(2,1)S(1)} %get-tuple-element.28), channel_id=1, source_target_pairs={{0,4},{1,5},{2,6},{3,7},{4,0},{5,1},{6,2},{7,3},{8,12},{9,13},{10,... | collective-permute-start | bytes 196616 | tf_op jit(solution)/shard_map/ppermute | solution.py:486
  9.1 9.2 %collective-permute-start.3 = (bf16[80,768]{1,0:T(8,128)(2,1)S(1)}, bf16[80,768]{1,0:T(8,128)(2,1)S(1)}, u32[]{:S(2)}, u32[]{:S(2)}) collective-permute-start(bf16[80,768]{1,0:T(8,128)(2,1)S(1)} %shard_map.171.packed), channel_id=1, source_target_pairs={{0,4},{1,5},{2,6},{3,7},{4,0},{5,1},{6,2},{7,3},{8,12},{9,13},{10,... | collective-permute-start | bytes 368648 | tf_op jit(solution)/shard_map/ppermute | solution.py:486
  13.3 16.3 %copy-start.22 = (bf16[128,256]{1,0:T(8,128)(2,1)}, bf16[128,256]{1,0:T(8,128)(2,1)S(1)}, u32[]{:S(2)}) copy-start(bf16[128,256]{1,0:T(8,128)(2,1)S(1)} %collective-permute-done.7.refs_8_) | copy-start | bytes 196612
  13.3 7.0 %collective-permute-start.10 = (bf16[128,256]{1,0:T(8,128)(2,1)S(1)}, bf16[128,256]{1,0:T(8,128)(2,1)S(1)}, u32[]{:S(2)}, u32[]{:S(2)}) collective-permute-start(bf16[128,256]{1,0:T(8,128)(2,1)S(1)} %collective-permute-done.7.refs_8_), channel_id=1, source_target_pairs={{0,3},{1,2},{2,1},{3,0},{4,7},{5,6},{6,5},{7,4},{8,11},{9,10},{10,... | collective-permute-start | bytes 196616 | tf_op jit(solution)/shard_map/ppermute | solution.py:486
  16.8 5.0 %collective-permute-start.9 = (bf16[128,256]{1,0:T(8,128)(2,1)S(1)}, bf16[128,256]{1,0:T(8,128)(2,1)S(1)}, u32[]{:S(2)}, u32[]{:S(2)}) collective-permute-start(bf16[128,256]{1,0:T(8,128)(2,1)S(1)} %collective-permute-done.7.refs_8_), channel_id=1, source_target_pairs={{0,2},{1,3},{2,0},{3,1},{4,6},{5,7},{6,4},{7,5},{8,10},{9,11},{10,... | collective-permute-start | bytes 196616 | tf_op jit(solution)/shard_map/ppermute | solution.py:486
  16.9 7.3 %collective-permute-start.8 = (bf16[128,256]{1,0:T(8,128)(2,1)S(1)}, bf16[128,256]{1,0:T(8,128)(2,1)S(1)}, u32[]{:S(2)}, u32[]{:S(2)}) collective-permute-start(bf16[128,256]{1,0:T(8,128)(2,1)S(1)} %collective-permute-done.7.refs_8_), channel_id=1, source_target_pairs={{0,1},{1,0},{2,3},{3,2},{4,5},{5,4},{6,7},{7,6},{8,9},{9,8},{10,11... | collective-permute-start | bytes 196616 | tf_op jit(solution)/shard_map/ppermute | solution.py:486
  18.3 11.3 %copy-start.18 = (bf16[80,768]{1,0:T(8,128)(2,1)}, bf16[80,768]{1,0:T(8,128)(2,1)S(1)}, u32[]{:S(2)}) copy-start(bf16[80,768]{1,0:T(8,128)(2,1)S(1)} %collective-permute-done.3.refs_4_) | copy-start | bytes 368644
  18.3 15.5 %collective-permute-start.1 = (bf16[128,768]{1,0:T(8,128)(2,1)S(1)}, bf16[128,768]{1,0:T(8,128)(2,1)S(1)}, u32[]{:S(2)}, u32[]{:S(2)}) collective-permute-start(bf16[128,768]{1,0:T(8,128)(2,1)S(1)} %get-tuple-element.27.refs_0_), channel_id=1, source_target_pairs={{0,2},{1,3},{2,0},{3,1},{4,6},{5,7},{6,4},{7,5},{8,10},{9,11},{10,... | collective-permute-start | bytes 589832 | tf_op jit(solution)/shard_map/ppermute | solution.py:486
  20.3 9.3 %copy-start.23 = (bf16[128,256]{1,0:T(8,128)(2,1)}, bf16[128,256]{1,0:T(8,128)(2,1)S(1)}, u32[]{:S(2)}) copy-start(bf16[128,256]{1,0:T(8,128)(2,1)S(1)} %collective-permute-done.10.refs_11_) | copy-start | bytes 196612
  20.3 13.5 %collective-permute-start = (bf16[128,768]{1,0:T(8,128)(2,1)S(1)}, bf16[128,768]{1,0:T(8,128)(2,1)S(1)}, u32[]{:S(2)}, u32[]{:S(2)}) collective-permute-start(bf16[128,768]{1,0:T(8,128)(2,1)S(1)} %get-tuple-element.27.refs_0_), channel_id=1, source_target_pairs={{0,1},{1,0},{2,3},{3,2},{4,5},{5,4},{6,7},{7,6},{8,9},{9,8},{10,11... | collective-permute-start | bytes 589832 | tf_op jit(solution)/shard_map/ppermute | solution.py:486
  21.8 7.9 %copy-start.24 = (bf16[128,256]{1,0:T(8,128)(2,1)}, bf16[128,256]{1,0:T(8,128)(2,1)S(1)}, u32[]{:S(2)}) copy-start(bf16[128,256]{1,0:T(8,128)(2,1)S(1)} %collective-permute-done.9.refs_10_) | copy-start | bytes 196612
  21.8 12.1 %collective-permute-start.6 = (bf16[80,768]{1,0:T(8,128)(2,1)S(1)}, bf16[80,768]{1,0:T(8,128)(2,1)S(1)}, u32[]{:S(2)}, u32[]{:S(2)}) collective-permute-start(bf16[80,768]{1,0:T(8,128)(2,1)S(1)} %collective-permute-done.3.refs_4_), channel_id=1, source_target_pairs={{0,3},{1,2},{2,1},{3,0},{4,7},{5,6},{6,5},{7,4},{8,11},{9,10},{10,... | collective-permute-start | bytes 368648 | tf_op jit(solution)/shard_map/ppermute | solution.py:486
  24.2 5.4 %copy-start.25 = (bf16[128,256]{1,0:T(8,128)(2,1)}, bf16[128,256]{1,0:T(8,128)(2,1)S(1)}, u32[]{:S(2)}) copy-start(bf16[128,256]{1,0:T(8,128)(2,1)S(1)} %collective-permute-done.8.refs_9_) | copy-start | bytes 196612
  24.2 9.6 %collective-permute-start.5 = (bf16[80,768]{1,0:T(8,128)(2,1)S(1)}, bf16[80,768]{1,0:T(8,128)(2,1)S(1)}, u32[]{:S(2)}, u32[]{:S(2)}) collective-permute-start(bf16[80,768]{1,0:T(8,128)(2,1)S(1)} %collective-permute-done.3.refs_4_), channel_id=1, source_target_pairs={{0,2},{1,3},{2,0},{3,1},{4,6},{5,7},{6,4},{7,5},{8,10},{9,11},{10,... | collective-permute-start | bytes 368648 | tf_op jit(solution)/shard_map/ppermute | solution.py:486
  25.3 4.3 %copy-start.15 = (bf16[128,768]{1,0:T(8,128)(2,1)}, bf16[128,768]{1,0:T(8,128)(2,1)S(1)}, u32[]{:S(2)}) copy-start(bf16[128,768]{1,0:T(8,128)(2,1)S(1)} %collective-permute-done.2.refs_3_) | copy-start | bytes 589828
  25.3 8.6 %collective-permute-start.4 = (bf16[80,768]{1,0:T(8,128)(2,1)S(1)}, bf16[80,768]{1,0:T(8,128)(2,1)S(1)}, u32[]{:S(2)}, u32[]{:S(2)}) collective-permute-start(bf16[80,768]{1,0:T(8,128)(2,1)S(1)} %collective-permute-done.3.refs_4_), channel_id=1, source_target_pairs={{0,1},{1,0},{2,3},{3,2},{4,5},{5,4},{6,7},{7,6},{8,9},{9,8},{10,11... | collective-permute-start | bytes 368648 | tf_op jit(solution)/shard_map/ppermute | solution.py:486
  26.6 4.1 %copy-start.5 = (s32[2]{0:T(128)}, s32[2]{0:T(128)S(1)}, u32[]{:S(2)}) copy-start(s32[2]{0:T(128)S(1)} %pad_add_fusion.1.place) | copy-start | bytes 28
  26.6 3.1 %copy-start.12 = (bf16[2,257,768]{2,0,1:T(2,128)(2,1)S(1)}, bf16[2,257,768]{2,0,1:T(2,128)(2,1)}, u32[]{:S(2)}) copy-start(bf16[2,257,768]{2,0,1:T(2,128)(2,1)} %param.17) | copy-start | bytes 2368516
  28.6 2.1 %copy-start.26 = (s32[16,4]{0,1:T(4,128)S(1)}, s32[16,4]{0,1:T(4,128)}, u32[]{:S(2)}) copy-start(s32[16,4]{0,1:T(4,128)} %param.21) | copy-start | bytes 772
  28.6 2.1 %copy-start.27 = (s32[16,4]{0,1:T(4,128)S(1)}, s32[16,4]{0,1:T(4,128)}, u32[]{:S(2)}) copy-start(s32[16,4]{0,1:T(4,128)} %param.20) | copy-start | bytes 772
  28.6 2.0 %copy-start.28 = (s32[16,4]{0,1:T(4,128)S(1)}, s32[16,4]{0,1:T(4,128)}, u32[]{:S(2)}) copy-start(s32[16,4]{0,1:T(4,128)} %param.19) | copy-start | bytes 772
  28.6 2.0 %copy-start.29 = (s32[16,4]{0,1:T(4,128)S(1)}, s32[16,4]{0,1:T(4,128)}, u32[]{:S(2)}) copy-start(s32[16,4]{0,1:T(4,128)} %param.18) | copy-start | bytes 772
  30.7 4.6 %copy-start.2 = (s32[16,16]{1,0:T(8,128)}, s32[16,16]{1,0:T(8,128)S(1)}, u32[]{:S(2)}) copy-start(s32[16,16]{1,0:T(8,128)S(1)} %pad_add_fusion.tables) | copy-start | bytes 3076
  32.9 0.9 copy-start
  33.8 0.7 copy-start.16
  33.8 0.7 copy-start.17
  33.8 0.8 copy-start.19
  33.9 0.8 copy-start.20
  34.6 0.6 copy-start.21
  35.3 21.6 %all-to-all-start = ((bf16[8,72,768]{2,1,0:T(8,128)(2,1)}), bf16[8,72,768]{2,1,0:T(8,128)(2,1)S(1)}, u32[]{:S(2)}, u32[]{:S(2)}) async-start(bf16[8,72,768]{2,1,0:T(8,128)(2,1)} %shard_map.175), calls=%async_computation | async-start | bytes 1769472 | tf_op jit(solution)/shard_map/all_to_all | solution.py:555
  56.9 4.5 %copy-start.8 = (bf16[8,72,768]{2,1,0:T(8,128)(2,1)}, bf16[8,72,768]{2,1,0:T(8,128)(2,1)S(1)}, u32[]{:S(2)}) copy-start(bf16[8,72,768]{2,1,0:T(8,128)(2,1)S(1)} %all-to-all-done.refs_8_) | copy-start | bytes 2654212
  56.9 33.7 %all-to-all-start.1 = ((bf16[8,72,768]{2,1,0:T(8,128)(2,1)}), bf16[8,72,768]{2,1,0:T(8,128)(2,1)S(1)}, u32[]{:S(2)}, u32[]{:S(2)}) async-start(bf16[8,72,768]{2,1,0:T(8,128)(2,1)} %get-tuple-element.43), calls=%async_computation.1 | async-start | bytes 1769472 | tf_op jit(solution)/shard_map/all_to_all | solution.py:597
  61.4 28.2 %copy-start.13 = (bf16[2,4,35,768]{3,2,1,0:T(8,128)(2,1)S(1)}, bf16[2,4,35,768]{3,2,1,0:T(8,128)(2,1)}, u32[]{:S(2)}) copy-start(bf16[2,4,35,768]{3,2,1,0:T(8,128)(2,1)} %get-tuple-element.56) | copy-start | bytes 1290244
  70.0 20.5 %copy-start.3 = (s32[16,16]{1,0:T(8,128)S(1)}, s32[16,16]{1,0:T(8,128)}, u32[]{:S(2)}) copy-start(s32[16,16]{1,0:T(8,128)} %copy-done.2) | copy-start | bytes 3076
  70.0 20.5 %copy-start.6 = (s32[2]{0:T(128)S(1)}, s32[2]{0:T(128)}, u32[]{:S(2)}) copy-start(s32[2]{0:T(128)} %copy-done.5) | copy-start | bytes 28
  70.0 15.8 %collective-permute-start.11 = (bf16[2,72,768]{2,1,0:T(8,128)(2,1)}, bf16[2,72,768]{2,1,0:T(8,128)(2,1)S(1)}, u32[]{:S(2)}, u32[]{:S(2)}) collective-permute-start(bf16[2,72,768]{2,1,0:T(8,128)(2,1)} %get-tuple-element.35), channel_id=1, source_target_pairs={{0,1},{1,0},{2,3},{3,2},{4,5},{5,4},{6,7},{7,6},{8,9},{9,8},{10,11... | collective-permute-start | bytes 663560 | tf_op jit(solution)/shard_map/ppermute | solution.py:486
  75.6 10.3 %collective-permute-start.12 = (bf16[2,72,768]{2,1,0:T(8,128)(2,1)}, bf16[2,72,768]{2,1,0:T(8,128)(2,1)S(1)}, u32[]{:S(2)}, u32[]{:S(2)}) collective-permute-start(bf16[2,72,768]{2,1,0:T(8,128)(2,1)} %get-tuple-element.36), channel_id=1, source_target_pairs={{0,2},{1,3},{2,0},{3,1},{4,6},{5,7},{6,4},{7,5},{8,10},{9,11},{10,... | collective-permute-start | bytes 663560 | tf_op jit(solution)/shard_map/ppermute | solution.py:486
  79.1 9.4 %collective-permute-start.13 = (bf16[2,72,768]{2,1,0:T(8,128)(2,1)}, bf16[2,72,768]{2,1,0:T(8,128)(2,1)S(1)}, u32[]{:S(2)}, u32[]{:S(2)}) collective-permute-start(bf16[2,72,768]{2,1,0:T(8,128)(2,1)} %get-tuple-element.37), channel_id=1, source_target_pairs={{0,3},{1,2},{2,1},{3,0},{4,7},{5,6},{6,5},{7,4},{8,11},{9,10},{10,... | collective-permute-start | bytes 663560 | tf_op jit(solution)/shard_map/ppermute | solution.py:486
  88.5 0.9 copy-start.1
  89.5 2.7 %copy-start.10 = (bf16[2,257,768]{2,1,0:T(8,128)(2,1)S(1)}, bf16[2,257,768]{2,1,0:T(8,128)(2,1)}, u32[]{:S(2)}) copy-start(bf16[2,257,768]{2,1,0:T(8,128)(2,1)} %get-tuple-element.59) | copy-start | bytes 2368516
  89.5 6.8 %collective-permute-start.14 = (bf16[72,768]{1,0:T(8,128)(2,1)S(1)}, bf16[72,768]{1,0:T(8,128)(2,1)S(1)}, u32[]{:S(2)}, u32[]{:S(2)}) collective-permute-start(bf16[72,768]{1,0:T(8,128)(2,1)S(1)} %get-tuple-element.39), channel_id=1, source_target_pairs={{0,4},{1,5},{2,6},{3,7},{4,0},{5,1},{6,2},{7,3},{8,12},{9,13},{10,... | collective-permute-start | bytes 331784 | tf_op jit(solution)/shard_map/ppermute | solution.py:486
  90.6 3.2 %copy-start.9 = (bf16[2,257,768]{2,1,0:T(8,128)(2,1)S(1)}, bf16[2,257,768]{2,1,0:T(8,128)(2,1)}, u32[]{:S(2)}) copy-start(bf16[2,257,768]{2,1,0:T(8,128)(2,1)} %get-tuple-element.60) | copy-start | bytes 2368516
